TPU v7x, 128 devices: a whole 4x4x4 slice. The times are simulated.
128 devices in a mesh: pts: 128 (over y, z, x, core).
Axes of the slice: x: 4, y: 4, z: 4, core: 2. Of those that a mesh axis runs over, the one named last changes fastest.
Arguments:
- loader_points: bfloat16 [524288, 256], P('pts'), may hold values from -6 to 6
- cotangent: bfloat16 [262144, 256], P('pts'), may hold values from -6 to 6
- block_counts: int32 [128], replicated, may hold values from 0 to 8, as said below
- dest_table: int32 [1024], P('pts'), may hold values from -1 to 511, as said below
- norm_gain: float32 [256], replicated, may hold values from 0.25 to 1.75
- w_feature: bfloat16 [256, 256], replicated, may hold values from -0.375 to 0.375
- w_middle: bfloat16 [256, 256], replicated, may hold values from -0.5625 to 0.5625
- w_slice: bfloat16 [32, 64], replicated, may hold values from -3.171875 to 3.171875
- w_temper: float32 [32], replicated, may hold values from -1 to 1
- attend_weight: float32 [3, 32, 32], replicated, may hold values from -6.363961 to 6.363961
- w_output: bfloat16 [256, 256], replicated, may hold values from -0.375 to 0.375
Outputs:
- layer_out: bfloat16 [262144, 256], P('pts')
- grad_points: bfloat16 [262144, 256], P('pts')
- grad_gain: float32 [256], replicated
- grad_feature: float32 [256, 256], replicated
- grad_middle: float32 [256, 256], replicated
- grad_slice: float32 [32, 64], replicated
- grad_temper: float32 [32], replicated
- grad_attend: float32 [3, 32, 32], replicated
- grad_output: float32 [256, 256], replicated
Inputs may be any that keep to these rules, and one draw needn't show every extreme that they name: `block_counts`: the counts sum to 512. Balanced device d owns blocks d * 4 to d * 4 + 3. Loader buffer d holds some last blocks of device d - 1, then its own blocks without some first and some last ones, then some first blocks of device d + 1; its first blocks are loaded by buffer d - 1 and its last ones by buffer d + 1. At most 2 blocks go from one device to one neighbour, and that most is reached. Some buffer is full and some buffer is empty. dest_table[d * 8 + s], for s < block_counts[d], is the balanced block index of slot s of buffer d; these rise with s. Empty slots hold -1.
All inputs are finite; a program needn't handle non-finite values.
Results may differ from a plain program's by a relative error of at most 0.013.
The roundings to bfloat16 on the way count: a program that leaves them out, or rounds other values in their place, can miss the bound.
Values may be sent and summed in bfloat16 or wider, within the bound.
No kernel may reach another device: no remote copies, remote signals or barrier semaphores. Data moves between devices by JAX's collectives and lax.ppermute only.
A program may use at most 192 MiB of HBM per device.

v0:
```python
import math

import jax
import jax.numpy as jnp
from jax import lax
from jax.sharding import PartitionSpec as P

BLOCK = 512
B_DEV = 4
HALF = 2
CAP = 8


def shifted(array, axis, by):
    length = lax.axis_size(axis)
    pairs = [(i, i + by) for i in range(length) if 0 <= i + by < length]
    return lax.ppermute(array, axis, pairs)


def mix_heads(form, left, right):
    return jnp.einsum(form, left, right, preferred_element_type=jnp.float32)


def transpose_dot(left, right):
    return lax.dot_general(
        left, right, (((0,), (0,)), ((), ())), preferred_element_type=jnp.float32
    )


def dot_against(left, right):
    return lax.dot_general(
        left, right, (((1,), (1,)), ((), ())), preferred_element_type=jnp.float32
    )


def slice_front(point_rows, row_mask, norm_gain, w_feature, w_middle, w_slice, w_temper):
    count_of_rows, feature_width = point_rows.shape
    head_width = w_slice.shape[0]
    count_of_heads = feature_width // head_width
    point_f = point_rows.astype(jnp.float32)
    center = point_f - jnp.mean(point_f, axis=-1, keepdims=True)
    inv_std = lax.rsqrt(jnp.mean(center * center, axis=-1, keepdims=True) + 1e-05)
    x_hat = center * inv_std
    normed = (x_hat * norm_gain).astype(jnp.bfloat16)
    features = jnp.dot(normed, w_feature, preferred_element_type=jnp.float32).astype(jnp.bfloat16)
    middle = jnp.dot(normed, w_middle, preferred_element_type=jnp.float32).astype(jnp.bfloat16)
    per_head = middle.reshape(count_of_rows * count_of_heads, head_width)
    temper = jnp.sum(per_head.astype(jnp.float32) * w_temper, axis=-1)
    temp_scale = 0.5 + jax.nn.softplus(temper)
    logits = jnp.dot(per_head, w_slice, preferred_element_type=jnp.float32) / temp_scale[:, None]
    slice_prob = jax.nn.softmax(logits, axis=-1) * jnp.repeat(row_mask, count_of_heads)[:, None]
    weights = slice_prob.astype(jnp.bfloat16).reshape(count_of_rows, -1)
    return (
        x_hat,
        inv_std,
        normed,
        features,
        per_head,
        temper,
        temp_scale,
        logits,
        slice_prob,
        weights,
    )


def slice_attention(numer, denom, attend_weight):
    head_width = numer.shape[-1]
    highest_precision = lax.Precision.HIGHEST
    slice_tokens = numer / (denom[..., None] + 1e-05)
    query_projection = jnp.einsum(
        "gpu,uo->gpo", slice_tokens, attend_weight[0], precision=highest_precision
    )
    key_projection = jnp.einsum(
        "gpu,uo->gpo", slice_tokens, attend_weight[1], precision=highest_precision
    )
    value_projection = jnp.einsum(
        "gpu,uo->gpo", slice_tokens, attend_weight[2], precision=highest_precision
    )
    score_matrix = jnp.einsum(
        "ykq,ysq->yks", query_projection, key_projection, precision=highest_precision
    ) / math.sqrt(head_width)
    attend_slices = jax.nn.softmax(score_matrix, axis=-1)
    return jnp.einsum("vsb,vbo->vso", attend_slices, value_projection, precision=highest_precision)


def own_count(block_counts, rank_here):
    here = jnp.arange(block_counts.shape[0]) == rank_here
    return jnp.sum(jnp.where(here, block_counts, 0))


def pick_slots(flag_row, take_count):
    ranking = jnp.cumsum(flag_row.astype(jnp.int32)) - 1
    hit = flag_row[None, :] & (ranking[None, :] == jnp.arange(take_count)[:, None])
    return jnp.sum(jnp.where(hit, jnp.arange(flag_row.shape[0])[None, :], 0), axis=1)


def outgoing(blocks, dest_table, rank_here, per_dev, half_cap):
    dest_dev = jnp.floor_divide(dest_table, per_dev)
    valid = dest_table >= 0
    to_next = jnp.take(blocks, pick_slots(valid & (dest_dev == rank_here + 1), half_cap), axis=0)
    to_prev = jnp.take(blocks, pick_slots(valid & (dest_dev == rank_here - 1), half_cap), axis=0)
    return (to_next, to_prev)


def assemble(blocks, got_prev, got_next, dest_table, rank_here, per_dev):
    capacity = blocks.shape[0]
    half_cap = got_prev.shape[0]
    target = jnp.arange(per_dev)
    matches = dest_table[None, :] == rank_here * per_dev + target[:, None]
    found = jnp.any(matches, axis=1)
    own_source = jnp.sum(jnp.where(matches, jnp.arange(capacity)[None, :], 0), axis=1)
    from_next = jnp.sum(~found & (target >= half_cap))
    tail_start = per_dev - from_next
    source = jnp.where(
        found,
        own_source,
        jnp.where(target < half_cap, capacity + target, capacity + half_cap + target - tail_start),
    )
    pool = jnp.concatenate([blocks, got_prev, got_next], axis=0)
    return jnp.take(pool, source, axis=0)


def loader_order(cot_blocks, prev_tail, next_head, dest_table, rank_here, per_dev):
    half_cap = prev_tail.shape[0]
    dest_dev = jnp.floor_divide(dest_table, per_dev)
    local_slot = dest_table - dest_dev * per_dev
    source = jnp.where(
        dest_dev == rank_here,
        local_slot,
        jnp.where(
            dest_dev == rank_here - 1, local_slot + half_cap, per_dev + half_cap + local_slot
        ),
    )
    source = jnp.where(dest_table >= 0, source, 0)
    pool = jnp.concatenate([cot_blocks, prev_tail, next_head], axis=0)
    return jnp.take(pool, source, axis=0)


def per_device(
    loader_points,
    cotangent,
    block_counts,
    dest_table,
    norm_gain,
    w_feature,
    w_middle,
    w_slice,
    w_temper,
    attend_weight,
    w_output,
):
    feature_width = loader_points.shape[1]
    head_width, slices = w_slice.shape
    count_of_heads = feature_width // head_width
    rank_here = lax.axis_index("pts")
    count_here = own_count(block_counts, rank_here)
    cot_blocks = cotangent.reshape(B_DEV, BLOCK, feature_width)
    prev_tail = shifted(cot_blocks[B_DEV - HALF :], "pts", 1)
    next_head = shifted(cot_blocks[:HALF], "pts", -1)
    cot_rows = loader_order(cot_blocks, prev_tail, next_head, dest_table, rank_here, B_DEV).reshape(
        CAP * BLOCK, feature_width
    )
    row_mask = (jnp.arange(CAP * BLOCK) // BLOCK < count_here).astype(jnp.float32)
    count_of_rows = loader_points.shape[0]
    x_hat, inv_std, normed, features, per_head, temper, temp_scale, logits, slice_prob, weights = (
        slice_front(loader_points, row_mask, norm_gain, w_feature, w_middle, w_slice, w_temper)
    )
    triple_weight = weights.reshape(count_of_rows, count_of_heads, slices)
    triple_features = features.reshape(count_of_rows, count_of_heads, head_width)
    numerator_partial = mix_heads("nkq,nka->kqa", triple_weight, triple_features)
    denom_part = jnp.sum(triple_weight, axis=0, dtype=jnp.float32)
    mixed_gradient = dot_against(cot_rows, w_output).astype(jnp.bfloat16)
    triple_output_gradient = mixed_gradient.reshape(count_of_rows, count_of_heads, head_width)
    partial_gradient = mix_heads("nkq,nka->kqa", triple_weight, triple_output_gradient)
    numer, denom = lax.psum((numerator_partial, denom_part), "pts")
    attended, back_mid = jax.vjp(slice_attention, numer, denom, attend_weight)
    attended_broadcast = attended.astype(jnp.bfloat16)
    mixed_heads = (
        mix_heads("uag,agx->uax", triple_weight, attended_broadcast)
        .astype(jnp.bfloat16)
        .reshape(count_of_rows, feature_width)
    )
    layer_out = (
        loader_points.astype(jnp.float32)
        + jnp.dot(mixed_heads, w_output, preferred_element_type=jnp.float32)
    ).astype(jnp.bfloat16)
    deslice_grad = lax.psum(partial_gradient, "pts")
    d_numer, denominator_gradient, grad_attend = back_mid(deslice_grad)
    numerator_broadcast = d_numer.astype(jnp.bfloat16)
    weights_gradient = (
        mix_heads("qcj,cxj->qcx", triple_output_gradient, attended_broadcast)
        + mix_heads("qcj,cxj->qcx", triple_features, numerator_broadcast)
        + denominator_gradient[None]
    )
    weights_gradient = weights_gradient.reshape(count_of_rows * count_of_heads, slices)
    d_logits = slice_prob * (
        weights_gradient - jnp.sum(slice_prob * weights_gradient, axis=-1, keepdims=True)
    )
    d_temper = -jnp.sum(d_logits * logits, axis=-1) / temp_scale * jax.nn.sigmoid(temper)
    d_raw = (d_logits / temp_scale[:, None]).astype(jnp.bfloat16)
    d_middle = (
        (dot_against(d_raw, w_slice) + d_temper[:, None] * w_temper)
        .astype(jnp.bfloat16)
        .reshape(count_of_rows, feature_width)
    )
    features_gradient = (
        mix_heads("uag,agx->uax", triple_weight, numerator_broadcast)
        .astype(jnp.bfloat16)
        .reshape(count_of_rows, feature_width)
    )
    d_normed = dot_against(features_gradient, w_feature) + dot_against(d_middle, w_middle)
    scaled = d_normed * norm_gain
    grad_rows = (
        cot_rows.astype(jnp.float32)
        + (
            scaled
            - jnp.mean(scaled, axis=-1, keepdims=True)
            - x_hat * jnp.mean(scaled * x_hat, axis=-1, keepdims=True)
        )
        * inv_std
    ).astype(jnp.bfloat16)
    grad_gain, grad_feature, grad_middle, grad_slice, grad_temper, grad_output = lax.psum(
        (
            jnp.sum(d_normed * x_hat, axis=0),
            transpose_dot(normed, features_gradient),
            transpose_dot(normed, d_middle),
            transpose_dot(per_head, d_raw),
            jnp.sum(d_temper[:, None] * per_head.astype(jnp.float32), axis=0),
            transpose_dot(mixed_heads, cot_rows),
        ),
        "pts",
    )
    stacked = jnp.stack(
        [
            layer_out.reshape(CAP, BLOCK, feature_width),
            grad_rows.reshape(CAP, BLOCK, feature_width),
        ],
        axis=1,
    )
    send_next, send_prev = outgoing(stacked, dest_table, rank_here, B_DEV, HALF)
    recv_prev = shifted(send_next, "pts", 1)
    recv_next = shifted(send_prev, "pts", -1)
    placed = assemble(stacked, recv_prev, recv_next, dest_table, rank_here, B_DEV)
    out_rows = placed[:, 0].reshape(B_DEV * BLOCK, feature_width)
    out_grads = placed[:, 1].reshape(B_DEV * BLOCK, feature_width)
    return (
        out_rows,
        out_grads,
        grad_gain,
        grad_feature,
        grad_middle,
        grad_slice,
        grad_temper,
        grad_attend,
        grad_output,
    )


def solution(mesh):
    return jax.shard_map(
        per_device,
        mesh=mesh,
        in_specs=(P("pts", None), P("pts", None), P(), P("pts"), P(), P(), P(), P(), P(), P(), P()),
        out_specs=(P("pts", None), P("pts", None), P(), P(), P(), P(), P(), P(), P()),
        check_vma=False,
    )
```

profile of v0, /device:TPU:1, one launch (start us, length us, event | category | flops | bytes accessed | tf_op | source)
XLA Modules:
  0.0 617.6 jit_solution(16396274201245815779)
XLA Ops:
  9.6 4.5 collective-permute-start
  34.1 10.0 %reshape.276 = bf16[32768,32]{1,0:T(8,128)(2,1)} reshape(bf16[4096,256]{1,0:T(8,128)(2,1)} %convolution_convert_fusion.4) | data formatting | bytes 4194304 | tf_op jit(solution)/shard_map/reshape | solution.py:47
  44.1 7.9 %copy.58 = bf16[32768,32]{0,1:T(8,128)(2,1)} copy(bf16[32768,32]{1,0:T(8,128)(2,1)} %reshape.276) | data formatting | bytes 4194304 | tf_op jit(solution)/shard_map/reshape | solution.py:47
  60.4 6.6 %fusion.58 = (f32[32768]{0:T(1024)S(1)}, f32[32768,64]{0,1:T(8,128)S(1)}) fusion(f32[32768]{0:T(1024)S(1)} %fusion.21, bf16[32768,32]{1,0:T(8,128)(2,1)} %reshape.276, bf16[32,64]{1,0:T(8,128)(2,1)S(1)} %copy-done.43), kind=kOutput, calls=%fused_computation.154 | convolution fusion | flops 138379264 | bytes 10752000 | tf_op jit(solution)/shard_map/dot_general | solution.py:50
  73.2 8.4 %copy.59 = bf16[32768,64]{1,0:T(8,128)(2,1)} copy(bf16[32768,64]{0,1:T(8,128)(2,1)} %fusion.55) | data formatting | bytes 8388608 | tf_op jit(solution)/shard_map/convert_element_type | solution.py:52
  81.5 7.1 %convert_reduce_fusion = f32[8,64]{1,0:T(8,128)} fusion(bf16[32768,64]{1,0:T(8,128)(2,1)} %copy.59), kind=kLoop, calls=%fused_computation.7 | loop fusion | flops 4193792 | bytes 4196352 | tf_op jit(solution)/shard_map/reduce_sum | solution.py:172
  88.7 10.0 %copy.60 = bf16[4096,8,64]{0,2,1:T(8,128)(2,1)} copy(bf16[4096,8,64]{2,1,0:T(8,128)(2,1)} %bitcast.141) | data formatting | bytes 8388608 | tf_op jit(solution)/shard_map/reshape;reshape | solution.py:169
  103.6 68.0 %psum.64 = f32[8,64]{1,0:T(8,128)} all-reduce(f32[8,64]{1,0:T(8,128)} %convert_reduce_fusion), channel_id=1, replica_groups=mesh['pts'=128] {'pts'}, use_global_device_ids=true, to_apply=%region_11.12 | all-reduce | flops 512 | bytes 4096 | tf_op jit(solution)/shard_map/psum | solution.py:176
  176.7 4.7 fusion.60
  198.1 135.1 %all-reduce.11.cloned.1.call-done = (f32[8,64,32]{1,2,0:T(8,128)}, f32[8,64,32]{1,2,0:T(8,128)}) async-done(((f32[8,64,32]{1,2,0:T(8,128)}, f32[8,64,32]{1,2,0:T(8,128)}), (f32[8,64,32]{1,2,0:T(8,128)}, f32[8,64,32]{1,2,0:T(8,128)})) %all-reduce.11.cloned.1.call-update) | async-done | bytes 131088 | tf_op jit(solution)/shard_map/psum | solution.py:188
  351.3 4.5 add_bitcast_fusion
  355.8 12.5 %copy.74 = f32[4096,8,64]{2,1,0:T(8,128)} copy(f32[4096,8,64]{0,2,1:T(8,128)} %add_bitcast_fusion) | data formatting | bytes 16777216 | tf_op jit(solution)/shard_map/add | solution.py:192
  368.3 12.7 %copy.76 = f32[32768,64]{0,1:T(8,128)} copy(f32[32768,64]{1,0:T(8,128)} %bitcast.142) | data formatting | bytes 16777216 | tf_op jit(solution)/shard_map/reshape | solution.py:196
  381.0 7.1 %multiply_reduce_fusion.1 = f32[32768]{0:T(1024)S(1)} fusion(f32[32768,64]{0,1:T(8,128)} %copy.76, f32[32768]{0:T(1024)S(1)} %copy-done.19, f32[32768]{0:T(1024)S(1)} %fusion.1, f32[32768,64]{0,1:T(8,128)} %copy-done.1, f32[32768]{0:T(1024)S(1)} %get-tuple-element.38), kind=kLoop, calls=%fused_computation.11 | loop fusion | flops 10452992 | bytes 17301504 | tf_op jit(solution)/shard_map/reduce_sum | solution.py:198
  389.2 6.3 %multiply_reduce_fusion = (f32[32768]{0:T(1024)S(1)}, bf16[32768,64]{0,1:T(8,128)(2,1)S(1)}) fusion(f32[32768,64]{0,1:T(8,128)} %copy-done.1, f32[32768,64]{0,1:T(8,128)S(1)} %copy-done.5, f32[32768]{0:T(1024)S(1)} %multiply_reduce_fusion.1, f32[32768]{0:T(1024)S(1)} %copy-done.19, f32[32768]{0:T(1024)S(1)} %fusion.1, f32[32768]{0:T(1024)S(1)} %get-tuple-element.38, ...), kind=kLoop, calls=%fused_computation.8 | loop fusion | flops 18841600 | bytes 21757952 | tf_op jit(solution)/shard_map/reduce_sum | solution.py:200
  400.7 7.4 %copy.77 = bf16[32768,32]{1,0:T(8,128)(2,1)} copy(bf16[32768,32]{0,1:T(8,128)(2,1)} %fusion) | data formatting | bytes 4194304 | tf_op jit(solution)/shard_map/convert_element_type | solution.py:204
  408.1 10.8 %reshape.283 = bf16[4096,256]{1,0:T(8,128)(2,1)} reshape(bf16[32768,32]{1,0:T(8,128)(2,1)} %copy.77) | data formatting | bytes 4194304 | tf_op jit(solution)/shard_map/reshape | solution.py:205
  418.8 3.8 fusion.65
  426.2 5.3 fusion.15
  431.5 4.5 fusion.14
  455.4 73.6 %all-reduce.3 = (f32[256]{0:T(256)}, f32[32,64]{1,0:T(8,128)}, f32[32]{0:T(128)}) all-reduce(f32[256]{0:T(256)} %get-tuple-element.10, f32[32,64]{1,0:T(8,128)S(1)} %copy-done.35, f32[32]{0:T(128)} %fusion.18), channel_id=1, replica_groups=mesh['pts'=128] {'pts'}, use_global_device_ids=true, to_apply=%region_26.28 | all-reduce | flops 2336 | bytes 18688 | tf_op jit(solution)/shard_map/psum | solution.py:223
  533.2 7.1 %pad_maximum_fusion = bf16[12,2,512,256]{3,2,1,0:T(8,128)(2,1)} fusion(bf16[2,2,512,256]{3,2,1,0:T(8,128)(2,1)S(1)} %collective-permute-done.3, bf16[2,2,512,256]{3,2,1,0:T(8,128)(2,1)} %collective-permute-done.2, bf16[8,1,512,256]{3,2,1,0:T(8,128)(2,1)} %bitcast.154, bf16[8,1,512,256]{3,2,1,0:T(8,128)(2,1)} %bitcast.151), kind=kLoop, calls=%fused_computation.16 | loop fusion | flops 9437184 | bytes 12582912 | tf_op jit(solution)/shard_map/concatenate | solution.py:120
  540.3 4.9 gather_fusion.1
  548.6 56.8 %all-reduce.9.cloned.1.call-done = (f32[256,256]{1,0:T(8,128)}, f32[256,256]{1,0:T(8,128)}, f32[256,256]{1,0:T(8,128)}) async-done(((f32[256,256]{1,0:T(8,128)}, f32[256,256]{1,0:T(8,128)}, f32[256,256]{1,0:T(8,128)}), (f32[256,256]{1,0:T(8,128)}, f32[256,256]{1,0:T(8,128)}, f32[256,256]{1,0:T(8,128)})) %all-reduce.9.cloned.1.call-update) | async-done | bytes 786448 | tf_op jit(solution)/shard_map/psum | solution.py:223
  (209 shorter events, 122.3 us)
Async XLA Ops:
  7.2 24.9 %copy-start = (bf16[256,256]{1,0:T(8,128)(2,1)S(1)}, bf16[256,256]{1,0:T(8,128)(2,1)}, u32[]{:S(2)}) copy-start(bf16[256,256]{1,0:T(8,128)(2,1)} %param.19) | copy-start | bytes 393220
  7.2 19.3 %copy-start.4 = (bf16[4096,256]{1,0:T(8,128)(2,1)S(1)}, bf16[4096,256]{1,0:T(8,128)(2,1)}, u32[]{:S(2)}) copy-start(bf16[4096,256]{1,0:T(8,128)(2,1)} %param.13) | copy-start | bytes 6291460
  7.2 21.3 %copy-start.41 = (f32[256]{0:T(256)S(1)}, f32[256]{0:T(256)}, u32[]{:S(2)}) copy-start(f32[256]{0:T(256)} %param.17) | copy-start | bytes 3076
  7.2 326.0 %all-reduce.11.cloned.1.call-start = ((), (), s32[]{:S(2)}) async-start(), calls=%async_computation.1 | async-start | bytes 524288 | tf_op jit(solution)/shard_map/psum | solution.py:188
  9.6 171.8 %collective-permute-start = (bf16[2,512,256]{2,1,0:T(8,128)(2,1)}, bf16[2,512,256]{2,1,0:T(8,128)(2,1)}, u32[]{:S(2)}, u32[]{:S(2)}) collective-permute-start(bf16[2,512,256]{2,1,0:T(8,128)(2,1)} %bitcast.13), channel_id=1, source_target_pairs={{0,1},{1,2},{2,3},{3,4},{4,5},{5,6},{6,7},{7,8},{8,9},{9,10},{10,1... | collective-permute-start | bytes 1572872 | tf_op jit(solution)/shard_map/ppermute | solution.py:17
  14.1 167.3 %collective-permute-start.1 = (bf16[2,512,256]{2,1,0:T(8,128)(2,1)}, bf16[2,512,256]{2,1,0:T(8,128)(2,1)}, u32[]{:S(2)}, u32[]{:S(2)}) collective-permute-start(bf16[2,512,256]{2,1,0:T(8,128)(2,1)} %bitcast.14), channel_id=1, source_target_pairs={{1,0},{2,1},{3,2},{4,3},{5,4},{6,5},{7,6},{8,7},{9,8},{10,9},{11,1... | collective-permute-start | bytes 1572872 | tf_op jit(solution)/shard_map/ppermute | solution.py:17
  18.7 80.5 %copy-start.45 = (pred[8]{0:T(512)(128)(4,1)}, pred[8]{0:T(512)(128)(4,1)S(1)}, u32[]{:S(2)}) copy-start(pred[8]{0:T(512)(128)(4,1)S(1)} %get-tuple-element.36) | copy-start | bytes 28
  44.1 10.4 %copy-start.51 = (s32[128]{0:T(128)S(1)}, s32[128]{0:T(128)}, u32[]{:S(2)}) copy-start(s32[128]{0:T(128)} %param.15) | copy-start | bytes 1540
  52.1 8.3 %copy-start.43 = (bf16[32,64]{1,0:T(8,128)(2,1)S(1)}, bf16[32,64]{1,0:T(8,128)(2,1)}, u32[]{:S(2)}) copy-start(bf16[32,64]{1,0:T(8,128)(2,1)} %param.20) | copy-start | bytes 12292
  54.5 12.5 %copy-start.25 = (f32[32768]{0:T(1024)}, f32[32768]{0:T(1024)S(1)}, u32[]{:S(2)}) copy-start(f32[32768]{0:T(1024)S(1)} %fusion.21) | copy-start | bytes 393220
  60.4 8.2 %copy-start.18 = (f32[32768]{0:T(1024)}, f32[32768]{0:T(1024)S(1)}, u32[]{:S(2)}) copy-start(f32[32768]{0:T(1024)S(1)} %mul.147) | copy-start | bytes 393220
  88.7 11.2 %copy-start.22 = (bf16[256,256]{1,0:T(8,128)(2,1)S(1)}, bf16[256,256]{1,0:T(8,128)(2,1)}, u32[]{:S(2)}) copy-start(bf16[256,256]{1,0:T(8,128)(2,1)} %param.18) | copy-start | bytes 393220
  103.6 77.9 %copy-start.17 = (bf16[2048,256]{1,0:T(8,128)(2,1)S(1)}, bf16[2048,256]{1,0:T(8,128)(2,1)}, u32[]{:S(2)}) copy-start(bf16[2048,256]{1,0:T(8,128)(2,1)} %param.14) | copy-start | bytes 3145732
  192.9 140.3 %copy-start.36 = (f32[3,32,32]{2,1,0:T(8,128)S(1)}, f32[3,32,32]{2,1,0:T(8,128)}, u32[]{:S(2)}) copy-start(f32[3,32,32]{2,1,0:T(8,128)} %param.22) | copy-start | bytes 36868
  192.9 140.3 %copy-start.39 = (f32[8,64]{1,0:T(8,128)S(1)}, f32[8,64]{1,0:T(8,128)}, u32[]{:S(2)}) copy-start(f32[8,64]{1,0:T(8,128)} %get-tuple-element.35) | copy-start | bytes 6148
  194.8 410.5 %all-reduce.9.cloned.1.call-start = ((), (), s32[]{:S(2)}) async-start(), calls=%async_computation | async-start | bytes 1572864 | tf_op jit(solution)/shard_map/psum | solution.py:223
  368.3 12.7 %copy-start.19 = (f32[32768]{0:T(1024)S(1)}, f32[32768]{0:T(1024)}, u32[]{:S(2)}) copy-start(f32[32768]{0:T(1024)} %copy-done.18) | copy-start | bytes 393220
  381.0 8.2 %copy-start.26 = (f32[32768]{0:T(1024)S(1)}, f32[32768]{0:T(1024)}, u32[]{:S(2)}) copy-start(f32[32768]{0:T(1024)} %copy-done.25) | copy-start | bytes 393220
  381.0 14.6 %slice-start = ((s8[8388608]{0:T(1024)(128)(4,1)}), s8[4194304]{0:T(1024)(128)(4,1)S(1)}, s32[]{:S(2)}) async-start(s8[8388608]{0:T(1024)(128)(4,1)} %bitcast.139), calls=%async_computation.2 | async-start | bytes 8388608
  439.6 14.7 %copy-start.13 = (bf16[32768,32]{0,1:T(8,128)(2,1)S(1)}, bf16[32768,32]{0,1:T(8,128)(2,1)}, u32[]{:S(2)}) copy-start(bf16[32768,32]{0,1:T(8,128)(2,1)} %copy.58) | copy-start | bytes 6291460
  442.7 12.7 %copy-start.35 = (f32[32,64]{1,0:T(8,128)S(1)}, f32[32,64]{1,0:T(8,128)}, u32[]{:S(2)}) copy-start(f32[32,64]{1,0:T(8,128)} %fusion.66) | copy-start | bytes 24580
  443.9 86.3 %copy-start.30 = (f32[8,64,32]{1,2,0:T(8,128)S(1)}, f32[8,64,32]{1,2,0:T(8,128)}, u32[]{:S(2)}) copy-start(f32[8,64,32]{1,2,0:T(8,128)} %copy-done.29) | copy-start | bytes 196612
  443.9 89.3 %collective-permute-start.2 = (bf16[2,2,512,256]{3,2,1,0:T(8,128)(2,1)}, bf16[2,2,512,256]{3,2,1,0:T(8,128)(2,1)}, u32[]{:S(2)}, u32[]{:S(2)}) collective-permute-start(bf16[2,2,512,256]{3,2,1,0:T(8,128)(2,1)} %broadcast_select_fusion.3), channel_id=1, source_target_pairs={{0,1},{1,2},{2,3},{3,4},{4,5},{5,6},{6,7},{7,8},{8,9},{9,10},{10,1... | collective-permute-start | bytes 3145736 | tf_op jit(solution)/shard_map/ppermute | solution.py:17
  452.2 81.0 %collective-permute-start.3 = (bf16[2,2,512,256]{3,2,1,0:T(8,128)(2,1)}, bf16[2,2,512,256]{3,2,1,0:T(8,128)(2,1)S(1)}, u32[]{:S(2)}, u32[]{:S(2)}) collective-permute-start(bf16[2,2,512,256]{3,2,1,0:T(8,128)(2,1)} %broadcast_select_fusion.2), channel_id=1, source_target_pairs={{1,0},{2,1},{3,2},{4,3},{5,4},{6,5},{7,6},{8,7},{9,8},{10,9},{11,1... | collective-permute-start | bytes 3145736 | tf_op jit(solution)/shard_map/ppermute | solution.py:17
  (36 other events, 145.7 us)
Sparse Core Ops, SparseCore 0:
  194.9 138.2 all-reduce.10
  454.5 150.8 all-reduce.8
where the time goes:
time: 630 us; the launch traced here: 618 us
  waiting for transfers between devices  192 us (30%)
  blocking collectives  142 us (23%)
  local copies, waits for them, and re-layouts  118 us (19%)
  other arithmetic  76.1 us (12%)
  matrix products  62.3 us (10%)
  between operations  15.9 us (3%)
  starting transfers between devices  12.2 us (2%)
    psum x1, waiting for transfers between devices, per_device(): deslice_grad = lax.psum(partial_gradient, 'pts')  135 us
    psum x1, blocking collectives, per_device(): lax.psum((jnp.sum(d_normed * x_hat, axis=0), transpose_dot(normed, featur...  73.6 us
    psum x1, blocking collectives, per_device(): numer, denom = lax.psum((numerator_partial, denom_part), 'pts')  68 us
    psum x1, waiting for transfers between devices, per_device(): lax.psum((jnp.sum(d_normed * x_hat, axis=0), transpose_dot(normed, featur...  56.8 us
    reshape x2, local copies, waits for them, and re-layouts, slice_front(): per_head = middle.reshape(count_of_rows * count_of_heads, head_width)  18 us
    dot_general x6, matrix products, mix_heads(): return jnp.einsum(form, left, right, preferred_element_type=jnp.float32)  15.1 us
    unnamed x113, local copies, waits for them, and re-layouts  14.9 us
    reshape x1, local copies, waits for them, and re-layouts, per_device(): weights_gradient.reshape(count_of_rows * count_of_heads, slices)  12.7 us
  transfers between devices with their start and end apart: 6, of which 2 were waited for; matrix products, arithmetic and copies ran while one was open for 20% of the time, Pallas kernels for 0%

commit v1 on v0

v1 whole, which is shorter than its diff:
```python
import math

import jax
import jax.numpy as jnp
from jax import lax
from jax.experimental import pallas as pl
from jax.experimental.pallas import tpu as pltpu
from jax.sharding import PartitionSpec as P

BLOCK = 512
B_DEV = 4
HALF = 2
CAP = 8
C = 256
HEADS = 8
HEAD = 32
SLICES = 64
HS = HEADS * SLICES
ROWS = B_DEV * BLOCK
PAY1 = 640
PAY2 = 896
BF = jnp.bfloat16
F32 = jnp.float32
HIGH = lax.Precision.HIGHEST
NN = (((1,), (0,)), ((), ()))
NT = (((1,), (1,)), ((), ()))
TN = (((0,), (0,)), ((), ()))


def dot(a, b, dims=NN):
    return lax.dot_general(a, b, dims, preferred_element_type=F32)


def dot_high(a, b, dims=NN):
    return lax.dot_general(a, b, dims, precision=HIGH, preferred_element_type=F32)


def head_mask(rows):
    row_head = lax.broadcasted_iota(jnp.int32, (rows, C), 0) // SLICES
    lane_head = lax.broadcasted_iota(jnp.int32, (rows, C), 1) // HEAD
    return row_head == lane_head


def fold_heads(full):
    masked = jnp.where(head_mask(HS), full, 0.0)
    return jnp.sum(masked.reshape(HEADS, SLICES, C), axis=0)


def spread_heads(small):
    tiled = jnp.concatenate([small] * HEADS, axis=0)
    return jnp.where(head_mask(HS), tiled, 0.0)


def normalize(points):
    point_f = points.astype(F32)
    center = point_f - jnp.mean(point_f, axis=-1, keepdims=True)
    inv_std = lax.rsqrt(jnp.mean(center * center, axis=-1, keepdims=True) + 1e-05)
    return center * inv_std, inv_std


def slice_softmax(mid, bd):
    out = dot(bd, mid, NT)
    width = mid.shape[0]
    temper = out[HS : HS + 8] + out[HS + 8 : HS + 16] + out[HS + 16 : HS + 24]
    scale = 0.5 + jnp.maximum(temper, 0.0) + jnp.log1p(jnp.exp(-jnp.abs(temper)))
    inv = 1.0 / scale
    logits = out[:HS].reshape(HEADS, SLICES, width) * inv[:, None, :]
    top = jnp.max(logits, axis=1, keepdims=True)
    e = jnp.exp(logits - top)
    prob = e * (1.0 / jnp.sum(e, axis=1, keepdims=True))
    return temper, inv, logits, prob


def front_kernel(
    sel, own, prev, nxt, dmix, gain, wfm, bd, ptsb, normed_out, feat_out, mid_out, pay, acc, den
):
    t = pl.program_id(0)
    kind = sel[3, t]

    @pl.when(kind == 0)
    def _():
        ptsb[...] = own[...]

    @pl.when(kind == 1)
    def _():
        ptsb[...] = prev[...]

    @pl.when(kind == 2)
    def _():
        ptsb[...] = nxt[...]

    x_hat, _ = normalize(ptsb[...])
    normed = (x_hat * gain[...]).astype(BF)
    normed_out[...] = normed
    fm = dot(normed, wfm[...]).astype(BF)
    feat, mid = fm[:, :C], fm[:, C:]
    feat_out[...] = feat
    mid_out[...] = mid
    _, _, _, prob = slice_softmax(mid, bd[...])
    weights = prob.reshape(HS, BLOCK).astype(BF)

    @pl.when(t == 0)
    def _():
        acc[...] = jnp.zeros_like(acc)
        den[...] = jnp.zeros_like(den)

    acc[:, :C] += dot(weights, feat)
    acc[:, C:] += dot(weights, dmix[...])
    wf = weights.astype(F32)
    den[...] += sum(wf[:, i * 128 : (i + 1) * 128] for i in range(BLOCK // 128))

    @pl.when(t == B_DEV - 1)
    def _():
        pay[:, :C] = fold_heads(acc[:, :C])
        pay[:, C : 2 * C] = fold_heads(acc[:, C:])
        total = jnp.sum(den[...], axis=1, keepdims=True)
        row_head = lax.broadcasted_iota(jnp.int32, (HS, 128), 0) // SLICES
        lane = lax.broadcasted_iota(jnp.int32, (HS, 128), 1)
        placed = jnp.where(row_head == lane, total, 0.0)
        pay[:, 2 * C :] = jnp.sum(placed.reshape(HEADS, SLICES, 128), axis=0)


def attention_step(pay, watt, an, ant, dd, gatt):
    numer = pay[:, :C]
    deslice = pay[:, C : 2 * C]
    head_of_lane = lax.broadcasted_iota(jnp.int32, (128, C), 1) // HEAD
    expand = (lax.broadcasted_iota(jnp.int32, (128, C), 0) == head_of_lane).astype(F32)
    inv_den = 1.0 / (dot_high(pay[:, 2 * C :], expand) + 1e-05)
    tokens = numer * inv_den
    mask = head_mask(HS)
    q = dot_high(tokens, watt[0])
    k = dot_high(tokens, watt[1])
    v = dot_high(tokens, watt[2])
    q_bd = spread_heads(q)
    root = 1.0 / math.sqrt(HEAD)
    scores = dot_high(q_bd, k, NT) * root
    top = jnp.max(scores, axis=-1, keepdims=True)
    e = jnp.exp(scores - top)
    att = e / jnp.sum(e, axis=-1, keepdims=True)
    attended = jnp.where(mask, dot_high(att, v), 0.0)
    do_bd = spread_heads(deslice)
    dv = dot_high(att, do_bd, TN)
    d_att = dot_high(do_bd, v, NT)
    ds = att * (d_att - jnp.sum(att * d_att, axis=-1, keepdims=True)) * root
    dq = fold_heads(dot_high(ds, k))
    dk = dot_high(ds, q_bd, TN)
    d_tokens = (
        dot_high(dq, watt[0], NT) + dot_high(dk, watt[1], NT) + dot_high(dv, watt[2], NT)
    )
    d_numer = d_tokens * inv_den
    d_den = -d_numer * tokens
    dd[...] = jnp.sum(spread_heads(d_den), axis=1, keepdims=True)
    d_numer_bd = spread_heads(d_numer)
    an[:, :C] = attended.astype(BF)
    an[:, C:] = d_numer_bd.astype(BF)
    ant[:C] = attended.T.astype(BF)
    ant[C:] = d_numer_bd.T.astype(BF)
    row_head = lax.broadcasted_iota(jnp.int32, (C, C), 0) // HEAD
    col_head = lax.broadcasted_iota(jnp.int32, (C, C), 1) // HEAD
    same = row_head == col_head
    lane_in = lax.broadcasted_iota(jnp.int32, (C, HEAD), 0) % HEAD
    fold = (lane_in == lax.broadcasted_iota(jnp.int32, (C, HEAD), 1)).astype(F32)
    for i, grad in enumerate((dq, dk, dv)):
        full = jnp.where(same, dot_high(tokens, grad, TN), 0.0)
        packed = dot_high(full, fold)
        gatt[i] = jnp.sum(packed.reshape(HEADS, HEAD, HEAD), axis=0)


def back_kernel(
    pay, watt, normed, feat, mid, dmix, cot, gain, wfmt, bd, bdt, wcol,
    res, gpay, gatt, an, ant, dd, gfm, gout, gsl,
):
    t = pl.program_id(0)

    @pl.when(t == 0)
    def _():
        attention_step(pay, watt, an, ant, dd, gatt)
        gfm[...] = jnp.zeros_like(gfm)
        gout[...] = jnp.zeros_like(gout)
        gsl[...] = jnp.zeros_like(gsl)

    mid_here = mid[...]
    temper, inv, logits, prob = slice_softmax(mid_here, bd[...])
    weights = prob.reshape(HS, BLOCK).astype(BF)
    dw = dot(an[:, :C], dmix[...], NT) + dot(an[:, C:], feat[...], NT) + dd[...]
    g = prob * dw.reshape(HEADS, SLICES, BLOCK)
    dl = g - prob * jnp.sum(g, axis=1, keepdims=True)
    d_temper = -jnp.sum(dl * logits, axis=1) * inv * jax.nn.sigmoid(temper)
    d_raw = (dl * inv[:, None, :]).reshape(HS, BLOCK).astype(BF)
    mixed_df = dot(ant[...], weights).astype(BF)
    spread = jnp.broadcast_to(d_temper[:, None, :], (HEADS, HEAD, BLOCK)).reshape(C, BLOCK)
    dm = (dot(bdt[...], d_raw) + spread * wcol[...]).astype(BF)
    res[: 2 * C] = mixed_df
    res[2 * C :] = dm
    normed_here = normed[...]
    gfm[:C] += dot(mixed_df[C:], normed_here)
    gfm[C:] += dot(dm, normed_here)
    gout[...] += dot(mixed_df[:C], cot[...])
    dt_hi = d_temper.astype(BF)
    dt_lo = (d_temper - dt_hi.astype(F32)).astype(BF)
    gsl[:HS] += dot(d_raw, mid_here)
    gsl[HS:] += dot(jnp.concatenate([dt_hi, dt_lo], axis=0), mid_here)

    @pl.when(t == B_DEV - 1)
    def _():
        grad_fm = gfm[...]
        gpay[: 2 * C] = grad_fm.astype(BF)
        gpay[2 * C : 3 * C] = gout[...].astype(BF)
        gpay[3 * C : 3 * C + SLICES] = fold_heads(gsl[:HS]).astype(BF)
        grad_gain = jnp.sum(grad_fm * wfmt[...].astype(F32), axis=0, keepdims=True) / gain[...]
        both = gsl[HS : HS + 8] + gsl[HS + 8 :]
        row = lax.broadcasted_iota(jnp.int32, (8, C), 0)
        lane_head = lax.broadcasted_iota(jnp.int32, (8, C), 1) // HEAD
        temper_row = jnp.sum(jnp.where(row == lane_head, both, 0.0), axis=0, keepdims=True)
        row = lax.broadcasted_iota(jnp.int32, (SLICES, C), 0)
        tail = jnp.where(row == 0, grad_gain, jnp.where(row == 1, temper_row, 0.0))
        gpay[3 * C + SLICES :] = tail.astype(BF)


def out_kernel(ptsb, cot, res, gain, wfmt, wout, layer, grad):
    points = ptsb[...]
    x_hat, inv_std = normalize(points)
    mixed_out = dot(res[:C], wout[...], TN)
    layer[...] = (points.astype(F32) + mixed_out).astype(BF)
    d_normed = dot(res[C:], wfmt[...], TN)
    scaled = d_normed * gain[...]
    mean_g = jnp.mean(scaled, axis=-1, keepdims=True)
    mean_gx = jnp.mean(scaled * x_hat, axis=-1, keepdims=True)
    grad[...] = (cot[...].astype(F32) + (scaled - mean_g - x_hat * mean_gx) * inv_std).astype(BF)


def unpack_kernel(got, gfeat, gmid, gout, gslice, gtemper, ggain):
    full = got[...].astype(F32).reshape(PAY2, C)
    gfeat[...] = full[:C].T
    gmid[...] = full[C : 2 * C].T
    gout[...] = full[2 * C : 3 * C]
    lane_in = lax.broadcasted_iota(jnp.int32, (C, HEAD), 0) % HEAD
    fold = (lane_in == lax.broadcasted_iota(jnp.int32, (C, HEAD), 1)).astype(F32)
    gslice[...] = dot_high(fold, full[3 * C : 3 * C + SLICES], (((0,), (1,)), ((), ())))
    tail = full[3 * C + SLICES : 3 * C + SLICES + 8]
    gtemper[...] = dot_high(tail, fold)[1:2]
    ggain[...] = tail[0:1]


def swap(array, mask):
    n = lax.axis_size("pts")
    return lax.ppermute(array, "pts", [(i, i ^ mask) for i in range(n)])


def quad_sum(x, low, high):
    a = swap(x, low)
    b = swap(x, high)
    c = swap(x, low ^ high)
    return (x + a) + (b + c)


def reduce_first(pay):
    core = lax.rem(lax.axis_index("pts"), 2)
    half = pay.shape[0] // 2
    send = lax.dynamic_slice_in_dim(pay, (1 - core) * half, half, 0)
    keep = lax.dynamic_slice_in_dim(pay, core * half, half, 0)
    x = keep + swap(send, 1)
    x = quad_sum(x, 2, 4)
    x = quad_sum(x, 8, 16)
    x = quad_sum(x, 32, 64)
    other = swap(x, 1)
    return jnp.where(
        core == 0, jnp.concatenate([x, other], 0), jnp.concatenate([other, x], 0)
    )


def groups_of_eight():
    return [[g * 8 + i for i in range(8)] for g in range(16)]


def reduce_second(gpay):
    pieces = gpay.reshape(8, PAY2 // 8, C)
    got = lax.all_to_all(pieces, "pts", 0, 0, tiled=True, axis_index_groups=groups_of_eight())
    x = jnp.sum(got.astype(F32), axis=0)
    for mask in (8, 24, 32, 96):
        x = x + swap(x, mask)
    tiled = jnp.broadcast_to(x.astype(BF)[None], (8, PAY2 // 8, C))
    return lax.all_to_all(tiled, "pts", 0, 0, tiled=True, axis_index_groups=groups_of_eight())


def shifted(array, by):
    n = lax.axis_size("pts")
    return lax.ppermute(array, "pts", [(i, i + by) for i in range(n) if 0 <= i + by < n])


def placement(dest_table, block_counts, rank):
    target = jnp.arange(B_DEV)
    matches = dest_table[None, :] == rank * B_DEV + target[:, None]
    found = jnp.any(matches, axis=1)
    own = jnp.sum(jnp.where(matches, jnp.arange(CAP)[None, :], 0), axis=1)
    from_prev = jnp.sum(~found & (target < HALF))
    from_next = jnp.sum(~found & (target >= HALF))
    left = jnp.sum(jnp.where(jnp.arange(block_counts.shape[0]) == rank - 1, block_counts, 0))
    start = jnp.maximum(left - HALF, 0)
    prev = jnp.clip(left - from_prev + target - start, 0, HALF - 1)
    nxt = jnp.clip(target - (B_DEV - from_next), 0, HALF - 1)
    kind = jnp.where(found, 0, jnp.where(target < HALF, 1, 2))
    return jnp.stack([own, prev, nxt, kind]).astype(jnp.int32)


def whole(shape):
    return pl.BlockSpec(shape, lambda t, *_: (0,) * len(shape))


def rows_spec(width):
    return pl.BlockSpec((BLOCK, width), lambda t, *_: (t, 0))


PARAMS = pltpu.CompilerParams(vmem_limit_bytes=48 * 1024 * 1024)


def per_device(
    loader_points, cotangent, block_counts, dest_table, norm_gain, w_feature, w_middle,
    w_slice, w_temper, attend_weight, w_output,
):
    rank = lax.axis_index("pts")
    count_here = jnp.sum(jnp.where(jnp.arange(block_counts.shape[0]) == rank, block_counts, 0))
    tail_at = jnp.maximum(count_here - HALF, 0) * BLOCK
    tail = lax.dynamic_slice_in_dim(loader_points, tail_at, HALF * BLOCK, 0)
    got_prev = shifted(tail, 1)
    got_next = shifted(loader_points[: HALF * BLOCK], -1)
    sel = placement(dest_table, block_counts, rank)
    gain = norm_gain.reshape(1, C)
    wfm = jnp.concatenate([w_feature, w_middle], axis=1)
    wfmt = wfm.T
    eye = jnp.eye(HEADS, dtype=F32)
    hi = lax.reduce_precision(w_temper, 8, 7)
    mid_part = lax.reduce_precision(w_temper - hi, 8, 7)
    low = w_temper - hi - mid_part
    slice_bd = jnp.kron(eye, w_slice.T.astype(F32))
    bd = jnp.concatenate(
        [slice_bd]
        + [jnp.kron(eye, part[None, :]) for part in (hi, mid_part, low)]
        + [jnp.zeros((8, C), F32)],
        axis=0,
    ).astype(BF)
    bdt = slice_bd.T.astype(BF)
    wcol = jnp.tile(w_temper, HEADS).reshape(C, 1)
    watt = jax.vmap(lambda w: jnp.kron(eye, w))(attend_weight)
    d_mixed = dot(cotangent, w_output, NT).astype(BF)

    wide = jax.ShapeDtypeStruct((ROWS, C), BF)
    ptsb, normed, feat, mid, pay = pl.pallas_call(
        front_kernel,
        grid_spec=pltpu.PrefetchScalarGridSpec(
            num_scalar_prefetch=1,
            grid=(B_DEV,),
            in_specs=[
                pl.BlockSpec((BLOCK, C), lambda t, s: (s[0, t], 0)),
                pl.BlockSpec((BLOCK, C), lambda t, s: (s[1, t], 0)),
                pl.BlockSpec((BLOCK, C), lambda t, s: (s[2, t], 0)),
                rows_spec(C),
                whole((1, C)),
                whole((C, 2 * C)),
                whole((HS + 32, C)),
            ],
            out_specs=[rows_spec(C)] * 4 + [whole((SLICES, PAY1))],
            scratch_shapes=[pltpu.VMEM((HS, 2 * C), F32), pltpu.VMEM((HS, 128), F32)],
        ),
        out_shape=[wide] * 4 + [jax.ShapeDtypeStruct((SLICES, PAY1), F32)],
        compiler_params=PARAMS,
        name="front",
    )(sel, loader_points, got_prev, got_next, d_mixed, gain, wfm, bd)

    pay = reduce_first(pay)

    res, gpay, grad_attend = pl.pallas_call(
        back_kernel,
        grid=(B_DEV,),
        in_specs=[whole((SLICES, PAY1)), whole((3, C, C))]
        + [rows_spec(C)] * 5
        + [
            whole((1, C)),
            whole((2 * C, C)),
            whole((HS + 32, C)),
            whole((C, HS)),
            whole((C, 1)),
        ],
        out_specs=[
            pl.BlockSpec((3 * C, BLOCK), lambda t: (0, t)),
            whole((PAY2, C)),
            whole((3, HEAD, HEAD)),
        ],
        out_shape=[
            jax.ShapeDtypeStruct((3 * C, ROWS), BF),
            jax.ShapeDtypeStruct((PAY2, C), BF),
            jax.ShapeDtypeStruct((3, HEAD, HEAD), F32),
        ],
        scratch_shapes=[
            pltpu.VMEM((HS, 2 * C), BF),
            pltpu.VMEM((2 * C, HS), BF),
            pltpu.VMEM((HS, 1), F32),
            pltpu.VMEM((2 * C, C), F32),
            pltpu.VMEM((C, C), F32),
            pltpu.VMEM((HS + 16, C), F32),
        ],
        compiler_params=PARAMS,
        name="back",
    )(pay, watt, normed, feat, mid, d_mixed, cotangent, gain, wfmt, bd, bdt, wcol)

    layer_out, grad_points = pl.pallas_call(
        out_kernel,
        grid=(B_DEV,),
        in_specs=[
            rows_spec(C),
            rows_spec(C),
            pl.BlockSpec((3 * C, BLOCK), lambda t: (0, t)),
            whole((1, C)),
            whole((2 * C, C)),
            whole((C, C)),
        ],
        out_specs=[rows_spec(C)] * 2,
        out_shape=[wide] * 2,
        compiler_params=PARAMS,
        cost_estimate=pl.CostEstimate(
            flops=2 * ROWS * C * 3 * C, bytes_accessed=7 * ROWS * C * 2, transcendentals=0
        ),
        name="outputs",
    )(ptsb, cotangent, res, gain, wfmt, w_output)

    got = reduce_second(gpay)
    grad_feature, grad_middle, grad_output, grad_slice, grad_temper, grad_gain = pl.pallas_call(
        unpack_kernel,
        out_shape=[
            jax.ShapeDtypeStruct((C, C), F32),
            jax.ShapeDtypeStruct((C, C), F32),
            jax.ShapeDtypeStruct((C, C), F32),
            jax.ShapeDtypeStruct((HEAD, SLICES), F32),
            jax.ShapeDtypeStruct((1, HEAD), F32),
            jax.ShapeDtypeStruct((1, C), F32),
        ],
        compiler_params=PARAMS,
        name="unpack",
    )(got)
    return (
        layer_out,
        grad_points,
        grad_gain.reshape(C),
        grad_feature,
        grad_middle,
        grad_slice,
        grad_temper.reshape(HEAD),
        grad_attend,
        grad_output,
    )


def solution(mesh):
    return jax.shard_map(
        per_device,
        mesh=mesh,
        in_specs=(P("pts", None), P("pts", None), P(), P("pts"), P(), P(), P(), P(), P(), P(), P()),
        out_specs=(P("pts", None), P("pts", None), P(), P(), P(), P(), P(), P(), P()),
        check_vma=False,
    )
```

time: 630 us -> 146 us (0.23); the launches traced: 618 us -> 145 us
  waiting for transfers between devices: 192 us -> 25.7 us
  blocking collectives: 142 us -> 11.5 us
  local copies, waits for them, and re-layouts: 118 us -> 25.8 us
  other arithmetic: 76.1 us -> 5.86 us
  matrix products: 62.3 us -> 1.45 us
  Pallas kernels: 0 us -> 30.2 us
  starting transfers between devices: 12.2 us -> 39.9 us
  between operations: 15.9 us -> 4.31 us
    psum x2 -> x0, waiting for transfers between devices: 192 us -> none  [the longest x1 135 us: per_device(): deslice_grad = lax.psum(partial_gradient, 'pts')]
    psum x2 -> x0, blocking collectives: 142 us -> none  [the longest x1 73.6 us: per_device(): lax.psum((jnp.sum(d_normed * x_hat, axis=0), transpose_dot(normed, featur...]
    dot_general x33 -> x1, matrix products: 62.3 us -> 1.45 us  [dot(): return lax.dot_general(a, b, dims, preferred_element_type=F32)]
    reshape x4 -> x0, local copies, waits for them, and re-layouts: 41.4 us -> none  [the longest x2 18 us: slice_front(): per_head = middle.reshape(count_of_rows * count_of_heads, head_width)]
    pallas_call x0 -> x4, Pallas kernels: none -> 30.2 us  [the longest x1 16.3 us: per_device(): pl.pallas_call(back_kernel, grid=(B_DEV,), in_specs=[whole((SLICES, PAY1)...]
    reduce_sum x14 -> x4, other arithmetic: 31.4 us -> 2.24 us  [the longest x1 1.35 us: per_device(): jnp.sum(jnp.where(jnp.arange(block_counts.shape[0]) == rank, block_counts...]
    ppermute x4 -> x17, waiting for transfers between devices: 0.01 us -> 22.5 us  [the longest x15 22.5 us: swap(): return lax.ppermute(array, 'pts', [(i, i ^ mask) for i in range(n)])]
    ppermute x4 -> x17, starting transfers between devices: 12.1 us -> 30.9 us  [the longest x15 24.5 us: swap(): return lax.ppermute(array, 'pts', [(i, i ^ mask) for i in range(n)])]
  transfers between devices with their start and end apart: 6 -> 18, of which waited for: 2 -> 11; matrix products, arithmetic and copies ran while one was open for 20% -> 11% of each run, Pallas kernels for 0% -> 3%
where the time goes in v1:
time: 146 us; the launch traced here: 145 us
  starting transfers between devices  39.9 us (27%)
  Pallas kernels  30.2 us (21%)
  local copies, waits for them, and re-layouts  25.8 us (18%)
  waiting for transfers between devices  25.7 us (18%)
  blocking collectives  11.5 us (8%)
  other arithmetic  5.86 us (4%)
  between operations  4.31 us (3%)
    ppermute x15, starting transfers between devices, swap(): return lax.ppermute(array, 'pts', [(i, i ^ mask) for i in range(n)])  24.5 us
    ppermute x15, waiting for transfers between devices, swap(): return lax.ppermute(array, 'pts', [(i, i ^ mask) for i in range(n)])  22.5 us
    pallas_call x1, Pallas kernels, per_device(): pl.pallas_call(back_kernel, grid=(B_DEV,), in_specs=[whole((SLICES, PAY1)...  16.3 us
    unnamed x42, local copies, waits for them, and re-layouts  12.4 us
    all_to_all x1, blocking collectives, reduce_second(): lax.all_to_all(pieces, 'pts', 0, 0, tiled=True, axis_index_groups=groups_...  11.5 us
    pallas_call x1, Pallas kernels, per_device(): pl.pallas_call(front_kernel, grid_spec=pltpu.PrefetchScalarGridSpec(num_s...  9.16 us
    all_to_all x1, starting transfers between devices, reduce_second(): lax.all_to_all(tiled, 'pts', 0, 0, tiled=True, axis_index_groups=groups_o...  8.92 us
    ppermute x2, starting transfers between devices, shifted(): lax.ppermute(array, 'pts', [(i, i + by) for i in range(n) if 0 <= i + by...  6.41 us
  transfers between devices with their start and end apart: 18, of which 11 were waited for; matrix products, arithmetic and copies ran while one was open for 11% of the time, Pallas kernels for 3%

profile of v1, /device:TPU:1, one launch (start us, length us, event | category | flops | bytes accessed | tf_op | source)
XLA Modules:
  0.0 144.7 jit_solution(7316889106887668816)
XLA Ops:
  2.7 2.3 %fusion.10 = (bf16[1024,256]{1,0:T(8,128)(2,1)}, bf16[1024,256]{1,0:T(8,128)(2,1)}) fusion(bf16[4096,256]{1,0:T(8,128)(2,1)} %own.1, s32[]{:T(128)S(6)} %select_n.55), kind=kLoop, calls=%fused_computation.42 | loop fusion | bytes 2097156 | tf_op jit(solution)/shard_map/slice | solution.py:326
  5.0 3.3 %collective-permute-start.1 = (bf16[1024,256]{1,0:T(8,128)(2,1)}, bf16[1024,256]{1,0:T(8,128)(2,1)S(1)}, u32[]{:S(2)}, u32[]{:S(2)}) collective-permute-start(bf16[1024,256]{1,0:T(8,128)(2,1)} %get-tuple-element.45), channel_id=1, source_target_pairs={{1,0},{2,1},{3,2},{4,3},{5,4},{6,5},{7,6},{8,7},{9,8},{10,9},{11,1... | collective-permute-start | bytes 1572872 | tf_op jit(solution)/shard_map/ppermute | solution.py:288
  8.3 3.1 %collective-permute-start = (bf16[1024,256]{1,0:T(8,128)(2,1)}, bf16[1024,256]{1,0:T(8,128)(2,1)S(1)}, u32[]{:S(2)}, u32[]{:S(2)}) collective-permute-start(bf16[1024,256]{1,0:T(8,128)(2,1)} %get-tuple-element.46), channel_id=1, source_target_pairs={{0,1},{1,2},{2,3},{3,4},{4,5},{5,6},{6,7},{7,8},{8,9},{9,10},{10,1... | collective-permute-start | bytes 1572872 | tf_op jit(solution)/shard_map/ppermute | solution.py:288
  25.5 9.2 %front.1 = (bf16[2048,256]{1,0:T(8,128)(2,1)S(1)}, bf16[2048,256]{1,0:T(8,128)(2,1)S(1)}, bf16[2048,256]{1,0:T(8,128)(2,1)S(1)}, bf16[2048,256]{1,0:T(8,128)(2,1)S(1)}, f32[64,640]{1,0:T(8,128)S(1)}) custom-call(s32[4,4]{1,0:T(4,128)S(1)} %pad_add_fusion.sel, bf16[4096,256]{1,0:T(8,128)(2,1)} %own.1, bf16[1024,256]{1,0:T(8,128)(2,1)S(1)} %copy-done.12, ...), custom_call_target="tpu_custom_call" | custom-call | tf_op jit(solution)/shard_map/front/pallas_call | solution.py:348
  38.9 4.6 %collective-permute-start.5 = (f32[32,640]{1,0:T(8,128)S(1)}, f32[32,640]{1,0:T(8,128)S(1)}, u32[]{:S(2)}, u32[]{:S(2)}) collective-permute-start(f32[32,640]{1,0:T(8,128)S(1)} %dynamic-slice_add_fusion), channel_id=1, source_target_pairs={{0,6},{1,7},{2,4},{3,5},{4,2},{5,3},{6,0},{7,1},{8,14},{9,15},{10,... | collective-permute-start | bytes 245768 | tf_op jit(solution)/shard_map/ppermute | solution.py:247
  44.2 2.7 %collective-permute-done.5 = f32[32,640]{1,0:T(8,128)S(1)} collective-permute-done((f32[32,640]{1,0:T(8,128)S(1)}, f32[32,640]{1,0:T(8,128)S(1)}, u32[]{:S(2)}, u32[]{:S(2)}) %collective-permute-start.5) | collective-permute-done | bytes 81952 | tf_op jit(solution)/shard_map/ppermute | solution.py:247
  48.5 5.9 %collective-permute-start.8 = (f32[32,640]{1,0:T(8,128)S(1)}, f32[32,640]{1,0:T(8,128)S(1)}, u32[]{:S(2)}, u32[]{:S(2)}) collective-permute-start(f32[32,640]{1,0:T(8,128)S(1)} %add_add_fusion.2), channel_id=1, source_target_pairs={{0,24},{1,25},{2,26},{3,27},{4,28},{5,29},{6,30},{7,31},{8,16},{9,... | collective-permute-start | bytes 245768 | tf_op jit(solution)/shard_map/ppermute | solution.py:247
  55.1 1.6 %collective-permute-done.8 = f32[32,640]{1,0:T(8,128)S(1)} collective-permute-done((f32[32,640]{1,0:T(8,128)S(1)}, f32[32,640]{1,0:T(8,128)S(1)}, u32[]{:S(2)}, u32[]{:S(2)}) %collective-permute-start.8) | collective-permute-done | bytes 81952 | tf_op jit(solution)/shard_map/ppermute | solution.py:247
  56.7 2.6 %collective-permute-done.7 = f32[32,640]{1,0:T(8,128)S(1)} collective-permute-done((f32[32,640]{1,0:T(8,128)S(1)}, f32[32,640]{1,0:T(8,128)S(1)}, u32[]{:S(2)}, u32[]{:S(2)}) %collective-permute-start.7) | collective-permute-done | bytes 81952 | tf_op jit(solution)/shard_map/ppermute | solution.py:247
  59.4 2.0 %collective-permute-start.11 = (f32[32,640]{1,0:T(8,128)S(1)}, f32[32,640]{1,0:T(8,128)S(1)}, u32[]{:S(2)}, u32[]{:S(2)}) collective-permute-start(f32[32,640]{1,0:T(8,128)S(1)} %add_add_fusion.1), channel_id=1, source_target_pairs={{0,96},{1,97},{2,98},{3,99},{4,100},{5,101},{6,102},{7,103},{8,104... | collective-permute-start | bytes 245768 | tf_op jit(solution)/shard_map/ppermute | solution.py:247
  63.2 2.8 %mul.161 = f32[3,8,32,8,32]{4,3,2,1,0:T(8,128)} broadcast(f32[3,32,32]{2,1,0:T(8,128)} %param.20), dimensions={0,2,4} | broadcast | bytes 798720 | tf_op jit(solution)/shard_map/vmap(jit(kron))/mul | solution.py:344
  66.0 3.1 %mul.162 = f32[3,256,256]{2,1,0:T(8,128)} reshape(f32[3,8,32,8,32]{4,3,2,1,0:T(8,128)} %mul.161) | data formatting | bytes 1572864 | tf_op jit(solution)/shard_map/vmap(jit(kron))/mul | solution.py:344
  70.0 4.8 %collective-permute-start.12 = (f32[32,640]{1,0:T(8,128)S(1)}, f32[32,640]{1,0:T(8,128)S(1)}, u32[]{:S(2)}, u32[]{:S(2)}) collective-permute-start(f32[32,640]{1,0:T(8,128)S(1)} %add_add_fusion), channel_id=1, source_target_pairs={{0,1},{1,0},{2,3},{3,2},{4,5},{5,4},{6,7},{7,6},{8,9},{9,8},{10,11... | collective-permute-start | bytes 245768 | tf_op jit(solution)/shard_map/ppermute | solution.py:247
  79.9 16.3 %back.1 = (bf16[768,2048]{1,0:T(8,128)(2,1)}, bf16[896,256]{1,0:T(8,128)(2,1)S(1)}, f32[3,32,32]{2,1,0:T(8,128)}) custom-call(f32[64,640]{1,0:T(8,128)S(1)} %maximum_select_fusion.pay, f32[3,256,256]{2,1,0:T(8,128)S(1)} %broadcast_multiply_fusion.watt, bf16[2048,256]{1,0:T(8,128)(2,1)S(1)} %copy-done.4, bf16[2048,256]{1,0:T(8,128)(2,1)S(1)} %copy-done.6, ...), custom_call_target="tpu_custom_call" | custom-call | tf_op jit(solution)/shard_map/back/pallas_call | solution.py:372
  96.1 11.5 %all_to_all.10 = bf16[8,112,256]{2,1,0:T(8,128)(2,1)S(1)} all-to-all(bf16[8,112,256]{2,1,0:T(8,128)(2,1)S(1)} %bitcast.33), channel_id=1, replica_groups={{0,1,2,3,4,5,6,7},{8,9,10,11,12,13,14,15},{16,17,18,19,20,21,22,23},{24..., dimensions={0} | all-to-all | bytes 917504 | tf_op jit(solution)/shard_map/all_to_all | solution.py:278
  107.8 3.6 %collective-permute-done.13 = f32[112,256]{1,0:T(8,128)S(1)} collective-permute-done((f32[112,256]{1,0:T(8,128)S(1)}, f32[112,256]{1,0:T(8,128)S(1)}, u32[]{:S(2)}, u32[]{:S(2)}) %collective-permute-start.13) | collective-permute-done | bytes 114720 | tf_op jit(solution)/shard_map/ppermute | solution.py:247
  112.7 3.7 %collective-permute-done.14 = f32[112,256]{1,0:T(8,128)S(1)} collective-permute-done((f32[112,256]{1,0:T(8,128)S(1)}, f32[112,256]{1,0:T(8,128)S(1)}, u32[]{:S(2)}, u32[]{:S(2)}) %collective-permute-start.14) | collective-permute-done | bytes 114720 | tf_op jit(solution)/shard_map/ppermute | solution.py:247
  117.8 2.3 %collective-permute-done.15 = f32[112,256]{1,0:T(8,128)S(1)} collective-permute-done((f32[112,256]{1,0:T(8,128)S(1)}, f32[112,256]{1,0:T(8,128)S(1)}, u32[]{:S(2)}, u32[]{:S(2)}) %collective-permute-start.15) | collective-permute-done | bytes 114720 | tf_op jit(solution)/shard_map/ppermute | solution.py:247
  120.1 1.8 %collective-permute-start.16 = (f32[112,256]{1,0:T(8,128)S(1)}, f32[112,256]{1,0:T(8,128)S(1)}, u32[]{:S(2)}, u32[]{:S(2)}) collective-permute-start(f32[112,256]{1,0:T(8,128)S(1)} %add.97), channel_id=1, source_target_pairs={{0,96},{1,97},{2,98},{3,99},{4,100},{5,101},{6,102},{7,103},{8,104... | collective-permute-start | bytes 344072 | tf_op jit(solution)/shard_map/ppermute | solution.py:247
  122.0 3.1 %collective-permute-done.16 = f32[112,256]{1,0:T(8,128)S(1)} collective-permute-done((f32[112,256]{1,0:T(8,128)S(1)}, f32[112,256]{1,0:T(8,128)S(1)}, u32[]{:S(2)}, u32[]{:S(2)}) %collective-permute-start.16) | collective-permute-done | bytes 114720 | tf_op jit(solution)/shard_map/ppermute | solution.py:247
  125.9 8.9 %all-to-all-start.1 = ((bf16[8,112,256]{2,1,0:T(8,128)(2,1)}), bf16[8,112,256]{2,1,0:T(8,128)(2,1)S(1)}, u32[]{:S(2)}, u32[]{:S(2)}) async-start(bf16[8,112,256]{2,1,0:T(8,128)(2,1)} %broadcast_in_dim.58), calls=%async_computation.1 | async-start | bytes 917504 | tf_op jit(solution)/shard_map/all_to_all | solution.py:283
  134.8 1.9 %copy-done.2 = bf16[768,2048]{1,0:T(8,128)(2,1)S(1)} copy-done((bf16[768,2048]{1,0:T(8,128)(2,1)S(1)}, bf16[768,2048]{1,0:T(8,128)(2,1)}, u32[]{:S(2)}) %copy-start.2) | copy-done | bytes 3145752
  136.7 3.7 %outputs.1 = (bf16[2048,256]{1,0:T(8,128)(2,1)}, bf16[2048,256]{1,0:T(8,128)(2,1)}) custom-call(bf16[2048,256]{1,0:T(8,128)(2,1)S(1)} %get-tuple-element.25.ptsb, bf16[2048,256]{1,0:T(8,128)(2,1)S(1)} %copy-done.1, bf16[768,2048]{1,0:T(8,128)(2,1)S(1)} %copy-done.2, f32[1,256]{1,0:T(1,128)S(1)} %bitcast.36, bf16[512,256]{1,0:T(8,128)(2,1)S(1)} %get-tuple-element.47.wfmt, ...), custom_call_target="tpu_custom_call" | custom-call | flops 805306368 | bytes 7340032 | tf_op jit(solution)/shard_map/outputs/pallas_call | solution.py:406
  140.4 3.2 %all-to-all-done.1.got = bf16[8,112,256]{2,1,0:T(8,128)(2,1)S(1)} async-done(((bf16[8,112,256]{2,1,0:T(8,128)(2,1)}), bf16[8,112,256]{2,1,0:T(8,128)(2,1)S(1)}, u32[]{:S(2)}, u32[]{:S(2)}) %all-to-all-start.1) | async-done | bytes 458784 | tf_op jit(solution)/shard_map/all_to_all | solution.py:283
  (106 shorter events, 32.3 us)
Async XLA Ops:
  0.6 11.4 %copy-start.19 = (s32[8]{0:T(128)S(1)}, s32[8]{0:T(128)}, u32[]{:S(2)}) copy-start(s32[8]{0:T(128)} %param.14) | copy-start | bytes 100
  0.7 14.2 %copy-start.18 = (f32[32]{0:T(128)S(1)}, f32[32]{0:T(128)}, u32[]{:S(2)}) copy-start(f32[32]{0:T(128)} %param.19) | copy-start | bytes 388
  0.7 14.2 %copy-start.17 = (bf16[32,64]{1,0:T(8,128)(2,1)S(1)}, bf16[32,64]{1,0:T(8,128)(2,1)}, u32[]{:S(2)}) copy-start(bf16[32,64]{1,0:T(8,128)(2,1)} %param.18) | copy-start | bytes 12292
  0.7 14.2 %copy-start.15 = (bf16[256,256]{1,0:T(8,128)(2,1)S(1)}, bf16[256,256]{1,0:T(8,128)(2,1)}, u32[]{:S(2)}) copy-start(bf16[256,256]{1,0:T(8,128)(2,1)} %param.16) | copy-start | bytes 393220
  0.7 14.3 %copy-start.16 = (bf16[256,256]{1,0:T(8,128)(2,1)S(1)}, bf16[256,256]{1,0:T(8,128)(2,1)}, u32[]{:S(2)}) copy-start(bf16[256,256]{1,0:T(8,128)(2,1)} %param.17) | copy-start | bytes 393220
  5.0 16.9 %collective-permute-start.1 = (bf16[1024,256]{1,0:T(8,128)(2,1)}, bf16[1024,256]{1,0:T(8,128)(2,1)S(1)}, u32[]{:S(2)}, u32[]{:S(2)}) collective-permute-start(bf16[1024,256]{1,0:T(8,128)(2,1)} %get-tuple-element.45), channel_id=1, source_target_pairs={{1,0},{2,1},{3,2},{4,3},{5,4},{6,5},{7,6},{8,7},{9,8},{10,9},{11,1... | collective-permute-start | bytes 1572872 | tf_op jit(solution)/shard_map/ppermute | solution.py:288
  8.3 14.4 %collective-permute-start = (bf16[1024,256]{1,0:T(8,128)(2,1)}, bf16[1024,256]{1,0:T(8,128)(2,1)S(1)}, u32[]{:S(2)}, u32[]{:S(2)}) collective-permute-start(bf16[1024,256]{1,0:T(8,128)(2,1)} %get-tuple-element.46), channel_id=1, source_target_pairs={{0,1},{1,2},{2,3},{3,4},{4,5},{5,6},{6,7},{7,8},{8,9},{9,10},{10,1... | collective-permute-start | bytes 1572872 | tf_op jit(solution)/shard_map/ppermute | solution.py:288
  37.6 1.3 collective-permute-start.2
  38.9 8.0 %collective-permute-start.5 = (f32[32,640]{1,0:T(8,128)S(1)}, f32[32,640]{1,0:T(8,128)S(1)}, u32[]{:S(2)}, u32[]{:S(2)}) collective-permute-start(f32[32,640]{1,0:T(8,128)S(1)} %dynamic-slice_add_fusion), channel_id=1, source_target_pairs={{0,6},{1,7},{2,4},{3,5},{4,2},{5,3},{6,0},{7,1},{8,14},{9,15},{10,... | collective-permute-start | bytes 245768 | tf_op jit(solution)/shard_map/ppermute | solution.py:247
  43.6 4.8 %collective-permute-start.4 = (f32[32,640]{1,0:T(8,128)S(1)}, f32[32,640]{1,0:T(8,128)S(1)}, u32[]{:S(2)}, u32[]{:S(2)}) collective-permute-start(f32[32,640]{1,0:T(8,128)S(1)} %dynamic-slice_add_fusion), channel_id=1, source_target_pairs={{0,4},{1,5},{2,6},{3,7},{4,0},{5,1},{6,2},{7,3},{8,12},{9,13},{10,... | collective-permute-start | bytes 245768 | tf_op jit(solution)/shard_map/ppermute | solution.py:247
  43.6 4.9 %collective-permute-start.3 = (f32[32,640]{1,0:T(8,128)S(1)}, f32[32,640]{1,0:T(8,128)S(1)}, u32[]{:S(2)}, u32[]{:S(2)}) collective-permute-start(f32[32,640]{1,0:T(8,128)S(1)} %dynamic-slice_add_fusion), channel_id=1, source_target_pairs={{0,2},{1,3},{2,0},{3,1},{4,6},{5,7},{6,4},{7,5},{8,10},{9,11},{10,... | collective-permute-start | bytes 245768 | tf_op jit(solution)/shard_map/ppermute | solution.py:247
  48.5 8.2 %collective-permute-start.8 = (f32[32,640]{1,0:T(8,128)S(1)}, f32[32,640]{1,0:T(8,128)S(1)}, u32[]{:S(2)}, u32[]{:S(2)}) collective-permute-start(f32[32,640]{1,0:T(8,128)S(1)} %add_add_fusion.2), channel_id=1, source_target_pairs={{0,24},{1,25},{2,26},{3,27},{4,28},{5,29},{6,30},{7,31},{8,16},{9,... | collective-permute-start | bytes 245768 | tf_op jit(solution)/shard_map/ppermute | solution.py:247
  54.4 4.9 %collective-permute-start.7 = (f32[32,640]{1,0:T(8,128)S(1)}, f32[32,640]{1,0:T(8,128)S(1)}, u32[]{:S(2)}, u32[]{:S(2)}) collective-permute-start(f32[32,640]{1,0:T(8,128)S(1)} %add_add_fusion.2), channel_id=1, source_target_pairs={{0,16},{1,17},{2,18},{3,19},{4,20},{5,21},{6,22},{7,23},{8,24},{9,... | collective-permute-start | bytes 245768 | tf_op jit(solution)/shard_map/ppermute | solution.py:247
  54.4 4.9 %collective-permute-start.6 = (f32[32,640]{1,0:T(8,128)S(1)}, f32[32,640]{1,0:T(8,128)S(1)}, u32[]{:S(2)}, u32[]{:S(2)}) collective-permute-start(f32[32,640]{1,0:T(8,128)S(1)} %add_add_fusion.2), channel_id=1, source_target_pairs={{0,8},{1,9},{2,10},{3,11},{4,12},{5,13},{6,14},{7,15},{8,0},{9,1},... | collective-permute-start | bytes 245768 | tf_op jit(solution)/shard_map/ppermute | solution.py:247
  59.4 9.8 %collective-permute-start.11 = (f32[32,640]{1,0:T(8,128)S(1)}, f32[32,640]{1,0:T(8,128)S(1)}, u32[]{:S(2)}, u32[]{:S(2)}) collective-permute-start(f32[32,640]{1,0:T(8,128)S(1)} %add_add_fusion.1), channel_id=1, source_target_pairs={{0,96},{1,97},{2,98},{3,99},{4,100},{5,101},{6,102},{7,103},{8,104... | collective-permute-start | bytes 245768 | tf_op jit(solution)/shard_map/ppermute | solution.py:247
  61.3 7.8 %collective-permute-start.10 = (f32[32,640]{1,0:T(8,128)S(1)}, f32[32,640]{1,0:T(8,128)S(1)}, u32[]{:S(2)}, u32[]{:S(2)}) collective-permute-start(f32[32,640]{1,0:T(8,128)S(1)} %add_add_fusion.1), channel_id=1, source_target_pairs={{0,64},{1,65},{2,66},{3,67},{4,68},{5,69},{6,70},{7,71},{8,72},{9,... | collective-permute-start | bytes 245768 | tf_op jit(solution)/shard_map/ppermute | solution.py:247
  62.5 6.6 %collective-permute-start.9 = (f32[32,640]{1,0:T(8,128)S(1)}, f32[32,640]{1,0:T(8,128)}, u32[]{:S(2)}, u32[]{:S(2)}) collective-permute-start(f32[32,640]{1,0:T(8,128)S(1)} %add_add_fusion.1), channel_id=1, source_target_pairs={{0,32},{1,33},{2,34},{3,35},{4,36},{5,37},{6,38},{7,39},{8,40},{9,... | collective-permute-start | bytes 245768 | tf_op jit(solution)/shard_map/ppermute | solution.py:247
  70.0 6.1 %collective-permute-start.12 = (f32[32,640]{1,0:T(8,128)S(1)}, f32[32,640]{1,0:T(8,128)S(1)}, u32[]{:S(2)}, u32[]{:S(2)}) collective-permute-start(f32[32,640]{1,0:T(8,128)S(1)} %add_add_fusion), channel_id=1, source_target_pairs={{0,1},{1,0},{2,3},{3,2},{4,5},{5,4},{6,7},{7,6},{8,9},{9,8},{10,11... | collective-permute-start | bytes 245768 | tf_op jit(solution)/shard_map/ppermute | solution.py:247
  96.1 38.7 %copy-start.1 = (bf16[2048,256]{1,0:T(8,128)(2,1)S(1)}, bf16[2048,256]{1,0:T(8,128)(2,1)}, u32[]{:S(2)}) copy-start(bf16[2048,256]{1,0:T(8,128)(2,1)} %cot.3) | copy-start | bytes 3145732
  107.7 3.7 %collective-permute-start.13 = (f32[112,256]{1,0:T(8,128)S(1)}, f32[112,256]{1,0:T(8,128)S(1)}, u32[]{:S(2)}, u32[]{:S(2)}) collective-permute-start(f32[112,256]{1,0:T(8,128)S(1)} %convert_reduce_fusion), channel_id=1, source_target_pairs={{0,8},{1,9},{2,10},{3,11},{4,12},{5,13},{6,14},{7,15},{8,0},{9,1},... | collective-permute-start | bytes 344072 | tf_op jit(solution)/shard_map/ppermute | solution.py:247
  111.4 4.9 %collective-permute-start.14 = (f32[112,256]{1,0:T(8,128)S(1)}, f32[112,256]{1,0:T(8,128)S(1)}, u32[]{:S(2)}, u32[]{:S(2)}) collective-permute-start(f32[112,256]{1,0:T(8,128)S(1)} %add.95), channel_id=1, source_target_pairs={{0,24},{1,25},{2,26},{3,27},{4,28},{5,29},{6,30},{7,31},{8,16},{9,... | collective-permute-start | bytes 344072 | tf_op jit(solution)/shard_map/ppermute | solution.py:247
  116.4 3.7 %collective-permute-start.15 = (f32[112,256]{1,0:T(8,128)S(1)}, f32[112,256]{1,0:T(8,128)S(1)}, u32[]{:S(2)}, u32[]{:S(2)}) collective-permute-start(f32[112,256]{1,0:T(8,128)S(1)} %add.96), channel_id=1, source_target_pairs={{0,32},{1,33},{2,34},{3,35},{4,36},{5,37},{6,38},{7,39},{8,40},{9,... | collective-permute-start | bytes 344072 | tf_op jit(solution)/shard_map/ppermute | solution.py:247
  120.1 4.9 %collective-permute-start.16 = (f32[112,256]{1,0:T(8,128)S(1)}, f32[112,256]{1,0:T(8,128)S(1)}, u32[]{:S(2)}, u32[]{:S(2)}) collective-permute-start(f32[112,256]{1,0:T(8,128)S(1)} %add.97), channel_id=1, source_target_pairs={{0,96},{1,97},{2,98},{3,99},{4,100},{5,101},{6,102},{7,103},{8,104... | collective-permute-start | bytes 344072 | tf_op jit(solution)/shard_map/ppermute | solution.py:247
  125.9 17.7 %all-to-all-start.1 = ((bf16[8,112,256]{2,1,0:T(8,128)(2,1)}), bf16[8,112,256]{2,1,0:T(8,128)(2,1)S(1)}, u32[]{:S(2)}, u32[]{:S(2)}) async-start(bf16[8,112,256]{2,1,0:T(8,128)(2,1)} %broadcast_in_dim.58), calls=%async_computation.1 | async-start | bytes 917504 | tf_op jit(solution)/shard_map/all_to_all | solution.py:283
  (14 other events, 28.1 us)

commit v2 on v1

--- a/solution.py
+++ b/solution.py
@@ -71,8 +71,99 @@
     return temper, inv, logits, prob
 
 
+def split_halves(core, full, send, keep):
+    half = full.shape[0] // 2
+
+    @pl.when(core == 0)
+    def _():
+        keep[...] = full[:half].astype(keep.dtype)
+        send[...] = full[half:].astype(send.dtype)
+
+    @pl.when(core != 0)
+    def _():
+        keep[...] = full[half:].astype(keep.dtype)
+        send[...] = full[:half].astype(send.dtype)
+
+
+def join_halves(core, mine, other, full):
+    half = full.shape[0] // 2
+
+    @pl.when(core == 0)
+    def _():
+        full[:half] = mine[...].astype(full.dtype)
+        full[half:] = other[...].astype(full.dtype)
+
+    @pl.when(core != 0)
+    def _():
+        full[:half] = other[...].astype(full.dtype)
+        full[half:] = mine[...].astype(full.dtype)
+
+
+def pick_kernel(rank, counts, loader, head, tail, sems):
+    start = jnp.maximum(counts[rank[0]] - HALF, 0) * BLOCK
+    start = pl.multiple_of(start, BLOCK)
+    first = pltpu.make_async_copy(loader.at[pl.ds(0, HALF * BLOCK)], head, sems.at[0])
+    last = pltpu.make_async_copy(loader.at[pl.ds(start, HALF * BLOCK)], tail, sems.at[1])
+    first.start()
+    last.start()
+    first.wait()
+    last.wait()
+
+
+def prep_kernel(
+    rank, counts, table, cot, wout, wf, wm, ws, wt, attw,
+    sel, dmix, wfmt, bd, bdt, wcol, watt,
+):
+    here = rank[0]
+    found, own = [], []
+    for t in range(B_DEV):
+        slot = jnp.int32(0)
+        hit = jnp.int32(0)
+        for s in range(CAP):
+            same = table[s] == here * B_DEV + t
+            slot = jnp.where(same, s, slot)
+            hit = jnp.where(same, 1, hit)
+        own.append(slot)
+        found.append(hit)
+    from_prev = 2 - found[0] - found[1]
+    from_next = 2 - found[2] - found[3]
+    left = counts[jnp.maximum(here - 1, 0)]
+    start = jnp.maximum(left - HALF, 0)
+    for t in range(B_DEV):
+        sel[0, t] = own[t]
+        sel[1, t] = jnp.clip(left - from_prev + t - start, 0, HALF - 1)
+        sel[2, t] = jnp.clip(t - (B_DEV - from_next), 0, HALF - 1)
+        sel[3, t] = jnp.where(found[t] == 1, 0, 1 if t < HALF else 2)
+
+    dmix[...] = dot(cot[...], wout[...], NT).astype(BF)
+    wfmt[:C] = wf[...].T
+    wfmt[C:] = wm[...].T
+    lane_in = lax.broadcasted_iota(jnp.int32, (HEAD, C), 1) % HEAD
+    spread = (lax.broadcasted_iota(jnp.int32, (HEAD, C), 0) == lane_in).astype(F32)
+    slice_rows = dot(ws[...], spread.astype(BF), TN)
+    slice_bd = spread_heads(slice_rows)
+    bd[:HS] = slice_bd.astype(BF)
+    bdt[...] = slice_bd.T.astype(BF)
+    temper = dot_high(wt[...], spread)
+    hi = temper.astype(BF).astype(F32)
+    middle = (temper - hi).astype(BF).astype(F32)
+    low = temper - hi - middle
+    row = lax.broadcasted_iota(jnp.int32, (8, C), 0)
+    own_head = row == lax.broadcasted_iota(jnp.int32, (8, C), 1) // HEAD
+    parts = [jnp.where(own_head, part, 0.0) for part in (hi, middle, low)]
+    bd[HS:] = jnp.concatenate(parts + [jnp.zeros((8, C), F32)], axis=0).astype(BF)
+    rows = lax.broadcasted_iota(jnp.int32, (C, C), 0)
+    cols = lax.broadcasted_iota(jnp.int32, (C, C), 1)
+    wcol[...] = jnp.sum(jnp.where(rows == cols, temper, 0.0), axis=1, keepdims=True)
+    same_head = rows // HEAD == cols // HEAD
+    for i in range(3):
+        wide = dot_high(attw[i], spread)
+        watt[i] = jnp.where(same_head, jnp.concatenate([wide] * HEADS, axis=0), 0.0)
+
+
 def front_kernel(
-    sel, own, prev, nxt, dmix, gain, wfm, bd, ptsb, normed_out, feat_out, mid_out, pay, acc, den
+    sel, core, own, prev, nxt, dmix, gain, wf, wm, bd,
+    ptsb, normed_out, feat_out, mid_out, send, keep, acc, den, pay
 ):
     t = pl.program_id(0)
     kind = sel[3, t]
@@ -92,8 +183,8 @@
     x_hat, _ = normalize(ptsb[...])
     normed = (x_hat * gain[...]).astype(BF)
     normed_out[...] = normed
-    fm = dot(normed, wfm[...]).astype(BF)
-    feat, mid = fm[:, :C], fm[:, C:]
+    feat = dot(normed, wf[...]).astype(BF)
+    mid = dot(normed, wm[...]).astype(BF)
     feat_out[...] = feat
     mid_out[...] = mid
     _, _, _, prob = slice_softmax(mid, bd[...])
@@ -118,9 +209,10 @@
         lane = lax.broadcasted_iota(jnp.int32, (HS, 128), 1)
         placed = jnp.where(row_head == lane, total, 0.0)
         pay[:, 2 * C :] = jnp.sum(placed.reshape(HEADS, SLICES, 128), axis=0)
-
-
-def attention_step(pay, watt, an, ant, dd, gatt):
+        split_halves(core[0], pay, send, keep)
+
+
+def attention_step(pay, watt, an, ant, dd, toks):
     numer = pay[:, :C]
     deslice = pay[:, C : 2 * C]
     head_of_lane = lax.broadcasted_iota(jnp.int32, (128, C), 1) // HEAD
@@ -155,26 +247,34 @@
     an[:, C:] = d_numer_bd.astype(BF)
     ant[:C] = attended.T.astype(BF)
     ant[C:] = d_numer_bd.T.astype(BF)
+    toks[0] = tokens
+    toks[1] = dq
+    toks[2] = dk
+    toks[3] = dv
+
+
+def attend_gradients(toks, gatt):
     row_head = lax.broadcasted_iota(jnp.int32, (C, C), 0) // HEAD
     col_head = lax.broadcasted_iota(jnp.int32, (C, C), 1) // HEAD
     same = row_head == col_head
     lane_in = lax.broadcasted_iota(jnp.int32, (C, HEAD), 0) % HEAD
     fold = (lane_in == lax.broadcasted_iota(jnp.int32, (C, HEAD), 1)).astype(F32)
-    for i, grad in enumerate((dq, dk, dv)):
-        full = jnp.where(same, dot_high(tokens, grad, TN), 0.0)
+    for i in range(3):
+        full = jnp.where(same, dot_high(toks[0], toks[i + 1], TN), 0.0)
         packed = dot_high(full, fold)
         gatt[i] = jnp.sum(packed.reshape(HEADS, HEAD, HEAD), axis=0)
 
 
 def back_kernel(
-    pay, watt, normed, feat, mid, dmix, cot, gain, wfmt, bd, bdt, wcol,
-    res, gpay, gatt, an, ant, dd, gfm, gout, gsl,
+    core, mine, other, watt, normed, feat, mid, dmix, cot, gain, wfmt, bd, bdt, wcol,
+    res, send, keep, toks, an, ant, dd, gfm, gout, gsl, pay, gpay,
 ):
     t = pl.program_id(0)
 
     @pl.when(t == 0)
     def _():
-        attention_step(pay, watt, an, ant, dd, gatt)
+        join_halves(core[0], mine, other, pay)
+        attention_step(pay, watt, an, ant, dd, toks)
         gfm[...] = jnp.zeros_like(gfm)
         gout[...] = jnp.zeros_like(gout)
         gsl[...] = jnp.zeros_like(gsl)
@@ -204,9 +304,9 @@
     @pl.when(t == B_DEV - 1)
     def _():
         grad_fm = gfm[...]
-        gpay[: 2 * C] = grad_fm.astype(BF)
-        gpay[2 * C : 3 * C] = gout[...].astype(BF)
-        gpay[3 * C : 3 * C + SLICES] = fold_heads(gsl[:HS]).astype(BF)
+        gpay[: 2 * C] = grad_fm
+        gpay[2 * C : 3 * C] = gout[...]
+        gpay[3 * C : 3 * C + SLICES] = fold_heads(gsl[:HS])
         grad_gain = jnp.sum(grad_fm * wfmt[...].astype(F32), axis=0, keepdims=True) / gain[...]
         both = gsl[HS : HS + 8] + gsl[HS + 8 :]
         row = lax.broadcasted_iota(jnp.int32, (8, C), 0)
@@ -214,10 +314,15 @@
         temper_row = jnp.sum(jnp.where(row == lane_head, both, 0.0), axis=0, keepdims=True)
         row = lax.broadcasted_iota(jnp.int32, (SLICES, C), 0)
         tail = jnp.where(row == 0, grad_gain, jnp.where(row == 1, temper_row, 0.0))
-        gpay[3 * C + SLICES :] = tail.astype(BF)
-
-
-def out_kernel(ptsb, cot, res, gain, wfmt, wout, layer, grad):
+        gpay[3 * C + SLICES :] = tail
+        split_halves(core[0], gpay, send, keep)
+
+
+def out_kernel(ptsb, cot, res, gain, wfmt, wout, toks, layer, grad, gatt):
+    @pl.when(pl.program_id(0) == 0)
+    def _():
+        attend_gradients(toks, gatt)
+
     points = ptsb[...]
     x_hat, inv_std = normalize(points)
     mixed_out = dot(res[:C], wout[...], TN)
@@ -229,8 +334,8 @@
     grad[...] = (cot[...].astype(F32) + (scaled - mean_g - x_hat * mean_gx) * inv_std).astype(BF)
 
 
-def unpack_kernel(got, gfeat, gmid, gout, gslice, gtemper, ggain):
-    full = got[...].astype(F32).reshape(PAY2, C)
+def unpack_kernel(core, mine, other, gfeat, gmid, gout, gslice, gtemper, ggain, full):
+    join_halves(core[0], mine, other, full)
     gfeat[...] = full[:C].T
     gmid[...] = full[C : 2 * C].T
     gout[...] = full[2 * C : 3 * C]
@@ -242,45 +347,25 @@
     ggain[...] = tail[0:1]
 
 
-def swap(array, mask):
+def swap(array, even, odd):
     n = lax.axis_size("pts")
-    return lax.ppermute(array, "pts", [(i, i ^ mask) for i in range(n)])
-
-
-def quad_sum(x, low, high):
-    a = swap(x, low)
-    b = swap(x, high)
-    c = swap(x, low ^ high)
-    return (x + a) + (b + c)
-
-
-def reduce_first(pay):
-    core = lax.rem(lax.axis_index("pts"), 2)
-    half = pay.shape[0] // 2
-    send = lax.dynamic_slice_in_dim(pay, (1 - core) * half, half, 0)
-    keep = lax.dynamic_slice_in_dim(pay, core * half, half, 0)
-    x = keep + swap(send, 1)
-    x = quad_sum(x, 2, 4)
-    x = quad_sum(x, 8, 16)
-    x = quad_sum(x, 32, 64)
-    other = swap(x, 1)
-    return jnp.where(
-        core == 0, jnp.concatenate([x, other], 0), jnp.concatenate([other, x], 0)
-    )
-
-
-def groups_of_eight():
-    return [[g * 8 + i for i in range(8)] for g in range(16)]
-
-
-def reduce_second(gpay):
-    pieces = gpay.reshape(8, PAY2 // 8, C)
-    got = lax.all_to_all(pieces, "pts", 0, 0, tiled=True, axis_index_groups=groups_of_eight())
-    x = jnp.sum(got.astype(F32), axis=0)
-    for mask in (8, 24, 32, 96):
-        x = x + swap(x, mask)
-    tiled = jnp.broadcast_to(x.astype(BF)[None], (8, PAY2 // 8, C))
-    return lax.all_to_all(tiled, "pts", 0, 0, tiled=True, axis_index_groups=groups_of_eight())
+    return lax.ppermute(array, "pts", [(i, i ^ (odd if i % 2 else even)) for i in range(n)])
+
+
+def quad_sum(x, even, odd, wire):
+    w = x.astype(wire)
+    a = swap(w, even, odd).astype(F32)
+    b = swap(w, 2 * even, 2 * odd).astype(F32)
+    c = swap(w, 3 * even, 3 * odd).astype(F32)
+    return (w.astype(F32) + a) + (b + c)
+
+
+def sum_over_chips(send, keep, wire):
+    x = keep + swap(send, 1, 1).astype(F32)
+    x = quad_sum(x, 2, 8, wire)
+    x = quad_sum(x, 8, 32, wire)
+    x = quad_sum(x, 32, 2, wire).astype(wire)
+    return x, swap(x, 1, 1)
 
 
 def shifted(array, by):
@@ -288,21 +373,6 @@
     return lax.ppermute(array, "pts", [(i, i + by) for i in range(n) if 0 <= i + by < n])
 
 
-def placement(dest_table, block_counts, rank):
-    target = jnp.arange(B_DEV)
-    matches = dest_table[None, :] == rank * B_DEV + target[:, None]
-    found = jnp.any(matches, axis=1)
-    own = jnp.sum(jnp.where(matches, jnp.arange(CAP)[None, :], 0), axis=1)
-    from_prev = jnp.sum(~found & (target < HALF))
-    from_next = jnp.sum(~found & (target >= HALF))
-    left = jnp.sum(jnp.where(jnp.arange(block_counts.shape[0]) == rank - 1, block_counts, 0))
-    start = jnp.maximum(left - HALF, 0)
-    prev = jnp.clip(left - from_prev + target - start, 0, HALF - 1)
-    nxt = jnp.clip(target - (B_DEV - from_next), 0, HALF - 1)
-    kind = jnp.where(found, 0, jnp.where(target < HALF, 1, 2))
-    return jnp.stack([own, prev, nxt, kind]).astype(jnp.int32)
-
-
 def whole(shape):
     return pl.BlockSpec(shape, lambda t, *_: (0,) * len(shape))
 
@@ -311,68 +381,91 @@
     return pl.BlockSpec((BLOCK, width), lambda t, *_: (t, 0))
 
 
-PARAMS = pltpu.CompilerParams(vmem_limit_bytes=48 * 1024 * 1024)
+PARAMS = pltpu.CompilerParams(vmem_limit_bytes=24 * 1024 * 1024)
+SCALARS = pl.BlockSpec(memory_space=pltpu.SMEM)
+HBM = pl.BlockSpec(memory_space=pl.ANY)
 
 
 def per_device(
     loader_points, cotangent, block_counts, dest_table, norm_gain, w_feature, w_middle,
     w_slice, w_temper, attend_weight, w_output,
 ):
-    rank = lax.axis_index("pts")
-    count_here = jnp.sum(jnp.where(jnp.arange(block_counts.shape[0]) == rank, block_counts, 0))
-    tail_at = jnp.maximum(count_here - HALF, 0) * BLOCK
-    tail = lax.dynamic_slice_in_dim(loader_points, tail_at, HALF * BLOCK, 0)
+    rank = lax.axis_index("pts").astype(jnp.int32).reshape(1)
+    core = lax.rem(rank, 2)
+    edge = jax.ShapeDtypeStruct((HALF * BLOCK, C), BF)
+    head, tail = pl.pallas_call(
+        pick_kernel,
+        in_specs=[SCALARS, SCALARS, HBM],
+        out_specs=[HBM, HBM],
+        out_shape=[edge, edge],
+        scratch_shapes=[pltpu.SemaphoreType.DMA((2,))],
+        name="pick",
+    )(rank, block_counts, loader_points)
     got_prev = shifted(tail, 1)
-    got_next = shifted(loader_points[: HALF * BLOCK], -1)
-    sel = placement(dest_table, block_counts, rank)
+    got_next = shifted(head, -1)
     gain = norm_gain.reshape(1, C)
-    wfm = jnp.concatenate([w_feature, w_middle], axis=1)
-    wfmt = wfm.T
-    eye = jnp.eye(HEADS, dtype=F32)
-    hi = lax.reduce_precision(w_temper, 8, 7)
-    mid_part = lax.reduce_precision(w_temper - hi, 8, 7)
-    low = w_temper - hi - mid_part
-    slice_bd = jnp.kron(eye, w_slice.T.astype(F32))
-    bd = jnp.concatenate(
-        [slice_bd]
-        + [jnp.kron(eye, part[None, :]) for part in (hi, mid_part, low)]
-        + [jnp.zeros((8, C), F32)],
-        axis=0,
-    ).astype(BF)
-    bdt = slice_bd.T.astype(BF)
-    wcol = jnp.tile(w_temper, HEADS).reshape(C, 1)
-    watt = jax.vmap(lambda w: jnp.kron(eye, w))(attend_weight)
-    d_mixed = dot(cotangent, w_output, NT).astype(BF)
+    sel, d_mixed, wfmt, bd, bdt, wcol, watt = pl.pallas_call(
+        prep_kernel,
+        in_specs=[SCALARS] * 3 + [pl.BlockSpec(memory_space=pltpu.VMEM)] * 7,
+        out_specs=[SCALARS] + [pl.BlockSpec(memory_space=pltpu.VMEM)] * 6,
+        out_shape=[
+            jax.ShapeDtypeStruct((4, B_DEV), jnp.int32),
+            jax.ShapeDtypeStruct((ROWS, C), BF),
+            jax.ShapeDtypeStruct((2 * C, C), BF),
+            jax.ShapeDtypeStruct((HS + 32, C), BF),
+            jax.ShapeDtypeStruct((C, HS), BF),
+            jax.ShapeDtypeStruct((C, 1), F32),
+            jax.ShapeDtypeStruct((3, C, C), F32),
+        ],
+        compiler_params=PARAMS,
+        cost_estimate=pl.CostEstimate(
+            flops=2 * ROWS * C * C, bytes_accessed=4 * 1024 * 1024, transcendentals=0
+        ),
+        name="prep",
+    )(
+        rank, block_counts, dest_table, cotangent, w_output, w_feature, w_middle, w_slice,
+        w_temper.reshape(1, HEAD), attend_weight,
+    )
 
     wide = jax.ShapeDtypeStruct((ROWS, C), BF)
-    ptsb, normed, feat, mid, pay = pl.pallas_call(
+    half1 = jax.ShapeDtypeStruct((SLICES // 2, PAY1), F32)
+    ptsb, normed, feat, mid, send, keep = pl.pallas_call(
         front_kernel,
         grid_spec=pltpu.PrefetchScalarGridSpec(
-            num_scalar_prefetch=1,
+            num_scalar_prefetch=2,
             grid=(B_DEV,),
             in_specs=[
-                pl.BlockSpec((BLOCK, C), lambda t, s: (s[0, t], 0)),
-                pl.BlockSpec((BLOCK, C), lambda t, s: (s[1, t], 0)),
-                pl.BlockSpec((BLOCK, C), lambda t, s: (s[2, t], 0)),
+                pl.BlockSpec((BLOCK, C), lambda t, s, c: (s[0, t], 0)),
+                pl.BlockSpec((BLOCK, C), lambda t, s, c: (s[1, t], 0)),
+                pl.BlockSpec((BLOCK, C), lambda t, s, c: (s[2, t], 0)),
                 rows_spec(C),
                 whole((1, C)),
-                whole((C, 2 * C)),
+                whole((C, C)),
+                whole((C, C)),
                 whole((HS + 32, C)),
             ],
-            out_specs=[rows_spec(C)] * 4 + [whole((SLICES, PAY1))],
-            scratch_shapes=[pltpu.VMEM((HS, 2 * C), F32), pltpu.VMEM((HS, 128), F32)],
+            out_specs=[rows_spec(C)] * 4 + [whole((SLICES // 2, PAY1))] * 2,
+            scratch_shapes=[
+                pltpu.VMEM((HS, 2 * C), F32),
+                pltpu.VMEM((HS, 128), F32),
+                pltpu.VMEM((SLICES, PAY1), F32),
+            ],
         ),
-        out_shape=[wide] * 4 + [jax.ShapeDtypeStruct((SLICES, PAY1), F32)],
+        out_shape=[wide] * 4 + [half1] * 2,
         compiler_params=PARAMS,
         name="front",
-    )(sel, loader_points, got_prev, got_next, d_mixed, gain, wfm, bd)
-
-    pay = reduce_first(pay)
-
-    res, gpay, grad_attend = pl.pallas_call(
+    )(
+        sel, core, loader_points, got_prev, got_next, d_mixed, gain, w_feature, w_middle, bd
+    )
+
+    mine, other = sum_over_chips(send, keep, F32)
+
+    res, send, keep, toks = pl.pallas_call(
         back_kernel,
         grid=(B_DEV,),
-        in_specs=[whole((SLICES, PAY1)), whole((3, C, C))]
+        in_specs=[SCALARS]
+        + [whole((SLICES // 2, PAY1))] * 2
+        + [whole((3, C, C))]
         + [rows_spec(C)] * 5
         + [
             whole((1, C)),
@@ -383,13 +476,15 @@
         ],
         out_specs=[
             pl.BlockSpec((3 * C, BLOCK), lambda t: (0, t)),
-            whole((PAY2, C)),
-            whole((3, HEAD, HEAD)),
+            whole((PAY2 // 2, C)),
+            whole((PAY2 // 2, C)),
+            whole((4, SLICES, C)),
         ],
         out_shape=[
             jax.ShapeDtypeStruct((3 * C, ROWS), BF),
-            jax.ShapeDtypeStruct((PAY2, C), BF),
-            jax.ShapeDtypeStruct((3, HEAD, HEAD), F32),
+            jax.ShapeDtypeStruct((PAY2 // 2, C), BF),
+            jax.ShapeDtypeStruct((PAY2 // 2, C), F32),
+            jax.ShapeDtypeStruct((4, SLICES, C), F32),
         ],
         scratch_shapes=[
             pltpu.VMEM((HS, 2 * C), BF),
@@ -398,12 +493,16 @@
             pltpu.VMEM((2 * C, C), F32),
             pltpu.VMEM((C, C), F32),
             pltpu.VMEM((HS + 16, C), F32),
+            pltpu.VMEM((SLICES, PAY1), F32),
+            pltpu.VMEM((PAY2, C), F32),
         ],
         compiler_params=PARAMS,
         name="back",
-    )(pay, watt, normed, feat, mid, d_mixed, cotangent, gain, wfmt, bd, bdt, wcol)
-
-    layer_out, grad_points = pl.pallas_call(
+    )(
+        core, mine, other, watt, normed, feat, mid, d_mixed, cotangent, gain, wfmt, bd, bdt, wcol
+    )
+
+    layer_out, grad_points, grad_attend = pl.pallas_call(
         out_kernel,
         grid=(B_DEV,),
         in_specs=[
@@ -413,19 +512,23 @@
             whole((1, C)),
             whole((2 * C, C)),
             whole((C, C)),
-        ],
-        out_specs=[rows_spec(C)] * 2,
-        out_shape=[wide] * 2,
+            whole((4, SLICES, C)),
+        ],
+        out_specs=[rows_spec(C)] * 2 + [whole((3, HEAD, HEAD))],
+        out_shape=[wide] * 2 + [jax.ShapeDtypeStruct((3, HEAD, HEAD), F32)],
         compiler_params=PARAMS,
         cost_estimate=pl.CostEstimate(
             flops=2 * ROWS * C * 3 * C, bytes_accessed=7 * ROWS * C * 2, transcendentals=0
         ),
         name="outputs",
-    )(ptsb, cotangent, res, gain, wfmt, w_output)
-
-    got = reduce_second(gpay)
+    )(ptsb, cotangent, res, gain, wfmt, w_output, toks)
+
+    mine, other = sum_over_chips(send, keep, BF)
+    vmem = pl.BlockSpec(memory_space=pltpu.VMEM)
     grad_feature, grad_middle, grad_output, grad_slice, grad_temper, grad_gain = pl.pallas_call(
         unpack_kernel,
+        in_specs=[SCALARS, vmem, vmem],
+        out_specs=[vmem] * 6,
         out_shape=[
             jax.ShapeDtypeStruct((C, C), F32),
             jax.ShapeDtypeStruct((C, C), F32),
@@ -434,9 +537,10 @@
             jax.ShapeDtypeStruct((1, HEAD), F32),
             jax.ShapeDtypeStruct((1, C), F32),
         ],
+        scratch_shapes=[pltpu.VMEM((PAY2, C), F32)],
         compiler_params=PARAMS,
         name="unpack",
-    )(got)
+    )(core, mine, other)
     return (
         layer_out,
         grad_points,

time: 146 us -> 147 us (level)
  Pallas kernels: 30.2 us -> 64 us
  local copies, waits for them, and re-layouts: 25.8 us -> 8.39 us
  blocking collectives: 11.5 us -> 0 us
  waiting for transfers between devices: 25.7 us -> 33.3 us
  other arithmetic: 5.86 us -> 0.47 us
  between operations: 4.31 us -> 0.84 us
    pallas_call x2 -> x4, Pallas kernels: 17.3 us -> 50.1 us  [the longest x1 33.7 us: per_device(): pl.pallas_call(pick_kernel, in_specs=[SCALARS, SCALARS, HBM], out_specs=[...]
    all_to_all x1 -> x0, blocking collectives: 11.5 us -> none  [reduce_second(): lax.all_to_all(pieces, 'pts', 0, 0, tiled=True, axis_index_groups=groups_...]
    ppermute x15 -> x22, waiting for transfers between devices: 22.5 us -> 33.3 us  [swap(): lax.ppermute(array, 'pts', [(i, i ^ (odd if i % 2 else even)) for i in ra...]
    all_to_all x1 -> x0, starting transfers between devices: 8.92 us -> none  [reduce_second(): lax.all_to_all(tiled, 'pts', 0, 0, tiled=True, axis_index_groups=groups_o...]
    ppermute x15 -> x22, starting transfers between devices: 24.5 us -> 32.7 us  [swap(): lax.ppermute(array, 'pts', [(i, i ^ (odd if i % 2 else even)) for i in ra...]
    mul x10 -> x0, local copies, waits for them, and re-layouts: 6.58 us -> none  [the longest x4 6.33 us: per_device(): watt = jax.vmap(lambda w: jnp.kron(eye, w))(attend_weight)]
    unnamed x42 -> x28, local copies, waits for them, and re-layouts: 12.4 us -> 8.39 us
    all_to_all x1 -> x0, waiting for transfers between devices: 3.19 us -> none  [reduce_second(): lax.all_to_all(tiled, 'pts', 0, 0, tiled=True, axis_index_groups=groups_o...]
  transfers between devices with their start and end apart: 18 -> 24, of which waited for: 11 -> 15; matrix products, arithmetic and copies ran while one was open for 11% -> 0% of each run, Pallas kernels for 3% -> 5%
where the time goes in v2:
time: 147 us; the launch traced here: 146 us
  Pallas kernels  64 us (44%)
  starting transfers between devices  39.2 us (27%)
  waiting for transfers between devices  33.3 us (23%)
  local copies, waits for them, and re-layouts  8.39 us (6%)
    pallas_call x1, Pallas kernels, per_device(): pl.pallas_call(pick_kernel, in_specs=[SCALARS, SCALARS, HBM], out_specs=[...  33.7 us
    ppermute x22, waiting for transfers between devices, swap(): lax.ppermute(array, 'pts', [(i, i ^ (odd if i % 2 else even)) for i in ra...  33.3 us
    ppermute x22, starting transfers between devices, swap(): lax.ppermute(array, 'pts', [(i, i ^ (odd if i % 2 else even)) for i in ra...  32.7 us
    pallas_call x1, Pallas kernels, per_device(): pl.pallas_call(back_kernel, grid=(B_DEV,), in_specs=[SCALARS] + [whole((S...  13.5 us
    unnamed x28, local copies, waits for them, and re-layouts  8.39 us
    pallas_call x1, Pallas kernels, per_device(): pl.pallas_call(front_kernel, grid_spec=pltpu.PrefetchScalarGridSpec(num_s...  8.18 us
    ppermute x2, starting transfers between devices, shifted(): lax.ppermute(array, 'pts', [(i, i + by) for i in range(n) if 0 <= i + by...  6.43 us
    pallas_call x1, Pallas kernels, per_device(): pl.pallas_call(out_kernel, grid=(B_DEV,), in_specs=[rows_spec(C), rows_sp...  5.73 us
  transfers between devices with their start and end apart: 24, of which 15 were waited for; matrix products, arithmetic and copies ran while one was open for 0% of the time, Pallas kernels for 5%

profile of v2, /device:TPU:1, one launch (start us, length us, event | category | flops | bytes accessed | tf_op | source)
XLA Modules:
  0.0 146.2 jit_solution(6826889857939224669)
XLA Ops:
  0.7 33.7 %pick.1 = (bf16[1024,256]{1,0:T(8,128)(2,1)}, bf16[1024,256]{1,0:T(8,128)(2,1)}) custom-call(s32[1]{0:T(128)} %bitcast.rank, s32[128]{0:T(128)} %counts.3, bf16[4096,256]{1,0:T(8,128)(2,1)} %own.1), custom_call_target="tpu_custom_call" | custom-call | tf_op jit(solution)/shard_map/pick/pallas_call | solution.py:396
  34.4 4.5 %collective-permute-start = (bf16[1024,256]{1,0:T(8,128)(2,1)}, bf16[1024,256]{1,0:T(8,128)(2,1)S(1)}, u32[]{:S(2)}, u32[]{:S(2)}) collective-permute-start(bf16[1024,256]{1,0:T(8,128)(2,1)} %get-tuple-element.38), channel_id=1, source_target_pairs={{0,1},{1,2},{2,3},{3,4},{4,5},{5,6},{6,7},{7,8},{8,9},{9,10},{10,1... | collective-permute-start | bytes 1572872 | tf_op jit(solution)/shard_map/ppermute | solution.py:373
  38.9 1.9 %collective-permute-start.1 = (bf16[1024,256]{1,0:T(8,128)(2,1)}, bf16[1024,256]{1,0:T(8,128)(2,1)S(1)}, u32[]{:S(2)}, u32[]{:S(2)}) collective-permute-start(bf16[1024,256]{1,0:T(8,128)(2,1)} %get-tuple-element.39), channel_id=1, source_target_pairs={{1,0},{2,1},{3,2},{4,3},{5,4},{6,5},{7,6},{8,7},{9,8},{10,9},{11,1... | collective-permute-start | bytes 1572872 | tf_op jit(solution)/shard_map/ppermute | solution.py:373
  48.2 1.8 %prep.1 = (s32[4,4]{1,0:T(4,128)S(1)}, bf16[2048,256]{1,0:T(8,128)(2,1)S(1)}, bf16[512,256]{1,0:T(8,128)(2,1)S(1)}, bf16[544,256]{1,0:T(8,128)(2,1)S(1)}, bf16[2...) custom-call(s32[1]{0:T(128)} %bitcast.rank, s32[128]{0:T(128)S(1)} %copy-done.11, ...), custom_call_target="tpu_custom_call" | custom-call | flops 268435456 | bytes 4194304 | tf_op jit(solution)/shard_map/prep/pallas_call | solution.py:407
  51.0 8.2 %front.1 = (bf16[2048,256]{1,0:T(8,128)(2,1)S(1)}, bf16[2048,256]{1,0:T(8,128)(2,1)S(1)}, bf16[2048,256]{1,0:T(8,128)(2,1)S(1)}, bf16[2048,256]{1,0:T(8,128)(2,1...) custom-call(s32[4,4]{1,0:T(4,128)S(1)} %get-tuple-element.37.sel, s32[1]{0:T(128)S(6)} %rem.18.core, ...), custom_call_target="tpu_custom_call" | custom-call | tf_op jit(solution)/shard_map/front/pallas_call | solution.py:432
  60.6 6.2 %collective-permute-start.5 = (f32[32,640]{1,0:T(8,128)S(1)}, f32[32,640]{1,0:T(8,128)S(1)}, u32[]{:S(2)}, u32[]{:S(2)}) collective-permute-start(f32[32,640]{1,0:T(8,128)S(1)} %add.60), channel_id=1, source_target_pairs={{0,6},{1,25},{2,4},{3,27},{4,2},{5,29},{6,0},{7,31},{8,14},{9,17},... | collective-permute-start | bytes 245768 | tf_op jit(solution)/shard_map/ppermute | solution.py:352
  67.5 1.6 %collective-permute-done.5 = f32[32,640]{1,0:T(8,128)S(1)} collective-permute-done((f32[32,640]{1,0:T(8,128)S(1)}, f32[32,640]{1,0:T(8,128)S(1)}, u32[]{:S(2)}, u32[]{:S(2)}) %collective-permute-start.5) | collective-permute-done | bytes 81952 | tf_op jit(solution)/shard_map/ppermute | solution.py:352
  69.1 2.5 %collective-permute-done.4 = f32[32,640]{1,0:T(8,128)S(1)} collective-permute-done((f32[32,640]{1,0:T(8,128)S(1)}, f32[32,640]{1,0:T(8,128)S(1)}, u32[]{:S(2)}, u32[]{:S(2)}) %collective-permute-start.4) | collective-permute-done | bytes 81952 | tf_op jit(solution)/shard_map/ppermute | solution.py:352
  71.6 2.8 %collective-permute-start.8 = (f32[32,640]{1,0:T(8,128)S(1)}, f32[32,640]{1,0:T(8,128)S(1)}, u32[]{:S(2)}, u32[]{:S(2)}) collective-permute-start(f32[32,640]{1,0:T(8,128)S(1)} %add_add_fusion.2), channel_id=1, source_target_pairs={{0,24},{1,97},{2,26},{3,99},{4,28},{5,101},{6,30},{7,103},{8,16},{... | collective-permute-start | bytes 245768 | tf_op jit(solution)/shard_map/ppermute | solution.py:352
  75.1 1.6 %collective-permute-done.8 = f32[32,640]{1,0:T(8,128)S(1)} collective-permute-done((f32[32,640]{1,0:T(8,128)S(1)}, f32[32,640]{1,0:T(8,128)S(1)}, u32[]{:S(2)}, u32[]{:S(2)}) %collective-permute-start.8) | collective-permute-done | bytes 81952 | tf_op jit(solution)/shard_map/ppermute | solution.py:352
  76.7 2.5 %collective-permute-done.7 = f32[32,640]{1,0:T(8,128)S(1)} collective-permute-done((f32[32,640]{1,0:T(8,128)S(1)}, f32[32,640]{1,0:T(8,128)S(1)}, u32[]{:S(2)}, u32[]{:S(2)}) %collective-permute-start.7) | collective-permute-done | bytes 81952 | tf_op jit(solution)/shard_map/ppermute | solution.py:352
  79.3 1.6 %collective-permute-start.11 = (f32[32,640]{1,0:T(8,128)S(1)}, f32[32,640]{1,0:T(8,128)S(1)}, u32[]{:S(2)}, u32[]{:S(2)}) collective-permute-start(f32[32,640]{1,0:T(8,128)S(1)} %add_add_fusion.1), channel_id=1, source_target_pairs={{0,96},{1,7},{2,98},{3,5},{4,100},{5,3},{6,102},{7,1},{8,104},{9,1... | collective-permute-start | bytes 245768 | tf_op jit(solution)/shard_map/ppermute | solution.py:352
  80.9 1.7 %collective-permute-start.9 = (f32[32,640]{1,0:T(8,128)S(1)}, f32[32,640]{1,0:T(8,128)S(1)}, u32[]{:S(2)}, u32[]{:S(2)}) collective-permute-start(f32[32,640]{1,0:T(8,128)S(1)} %add_add_fusion.1), channel_id=1, source_target_pairs={{0,32},{1,3},{2,34},{3,1},{4,36},{5,7},{6,38},{7,5},{8,40},{9,11},... | collective-permute-start | bytes 245768 | tf_op jit(solution)/shard_map/ppermute | solution.py:352
  83.8 1.9 %collective-permute-done.10 = f32[32,640]{1,0:T(8,128)S(1)} collective-permute-done((f32[32,640]{1,0:T(8,128)S(1)}, f32[32,640]{1,0:T(8,128)S(1)}, u32[]{:S(2)}, u32[]{:S(2)}) %collective-permute-start.10) | collective-permute-done | bytes 81952 | tf_op jit(solution)/shard_map/ppermute | solution.py:352
  85.7 4.5 %collective-permute-start.12 = (f32[32,640]{1,0:T(8,128)S(1)}, f32[32,640]{1,0:T(8,128)S(1)}, u32[]{:S(2)}, u32[]{:S(2)}) collective-permute-start(f32[32,640]{1,0:T(8,128)S(1)} %add_add_fusion.mine), channel_id=1, source_target_pairs={{0,1},{1,0},{2,3},{3,2},{4,5},{5,4},{6,7},{7,6},{8,9},{9,8},{10,11... | collective-permute-start | bytes 245768 | tf_op jit(solution)/shard_map/ppermute | solution.py:352
  91.2 13.5 %back.1 = (bf16[768,2048]{1,0:T(8,128)(2,1)S(1)}, bf16[448,256]{1,0:T(8,128)(2,1)S(1)}, f32[448,256]{1,0:T(8,128)S(1)}, f32[4,64,256]{2,1,0:T(8,128)S(1)}) custom-call(s32[1]{0:T(128)S(6)} %rem.18.core, f32[32,640]{1,0:T(8,128)S(1)} %add_add_fusion.mine, f32[32,640]{1,0:T(8,128)S(1)} %collective-permute-done.12.other, ...), custom_call_target="tpu_custom_call" | custom-call | tf_op jit(solution)/shard_map/back/pallas_call | solution.py:463
  108.6 1.3 collective-permute-start.14
  109.8 5.6 %collective-permute-done.16 = bf16[448,256]{1,0:T(8,128)(2,1)S(1)} collective-permute-done((bf16[448,256]{1,0:T(8,128)(2,1)S(1)}, bf16[448,256]{1,0:T(8,128)(2,1)S(1)}, u32[]{:S(2)}, u32[]{:S(2)}) %collective-permute-start.16) | collective-permute-done | bytes 229408 | tf_op jit(solution)/shard_map/ppermute | solution.py:352
  116.2 1.7 %collective-permute-start.19 = (bf16[448,256]{1,0:T(8,128)(2,1)S(1)}, bf16[448,256]{1,0:T(8,128)(2,1)S(1)}, u32[]{:S(2)}, u32[]{:S(2)}) collective-permute-start(bf16[448,256]{1,0:T(8,128)(2,1)S(1)} %add_convert_fusion.2), channel_id=1, source_target_pairs={{0,24},{1,97},{2,26},{3,99},{4,28},{5,101},{6,30},{7,103},{8,16},{... | collective-permute-start | bytes 688136 | tf_op jit(solution)/shard_map/ppermute | solution.py:352
  119.5 5.6 %collective-permute-done.19 = bf16[448,256]{1,0:T(8,128)(2,1)S(1)} collective-permute-done((bf16[448,256]{1,0:T(8,128)(2,1)S(1)}, bf16[448,256]{1,0:T(8,128)(2,1)S(1)}, u32[]{:S(2)}, u32[]{:S(2)}) %collective-permute-start.19) | collective-permute-done | bytes 229408 | tf_op jit(solution)/shard_map/ppermute | solution.py:352
  125.8 1.4 collective-permute-start.22
  129.2 5.6 %collective-permute-done.22 = bf16[448,256]{1,0:T(8,128)(2,1)S(1)} collective-permute-done((bf16[448,256]{1,0:T(8,128)(2,1)S(1)}, bf16[448,256]{1,0:T(8,128)(2,1)S(1)}, u32[]{:S(2)}, u32[]{:S(2)}) %collective-permute-start.22) | collective-permute-done | bytes 229408 | tf_op jit(solution)/shard_map/ppermute | solution.py:352
  135.5 3.8 %collective-permute-start.23 = (bf16[448,256]{1,0:T(8,128)(2,1)S(1)}, bf16[448,256]{1,0:T(8,128)(2,1)S(1)}, u32[]{:S(2)}, u32[]{:S(2)}) collective-permute-start(bf16[448,256]{1,0:T(8,128)(2,1)S(1)} %add_convert_fusion.mine), channel_id=1, source_target_pairs={{0,1},{1,0},{2,3},{3,2},{4,5},{5,4},{6,7},{7,6},{8,9},{9,8},{10,11... | collective-permute-start | bytes 688136 | tf_op jit(solution)/shard_map/ppermute | solution.py:352
  139.3 5.7 %outputs.1 = (bf16[2048,256]{1,0:T(8,128)(2,1)}, bf16[2048,256]{1,0:T(8,128)(2,1)}, f32[3,32,32]{2,1,0:T(8,128)}) custom-call(bf16[2048,256]{1,0:T(8,128)(2,1)S(1)} %get-tuple-element.42.ptsb, bf16[2048,256]{1,0:T(8,128)(2,1)S(1)} %copy-done.1, bf16[768,2048]{1,0:T(8,128)(2,1)S(1)} %get-tuple-element.52.res, f32[1,256]{1,0:T(1,128)S(1)} %bitcast.7, ...), custom_call_target="tpu_custom_call" | custom-call | flops 805306368 | bytes 7340032 | tf_op jit(solution)/shard_map/outputs/pallas_call | solution.py:505
  (66 shorter events, 24.1 us)
Async XLA Ops:
  34.4 15.6 %collective-permute-start = (bf16[1024,256]{1,0:T(8,128)(2,1)}, bf16[1024,256]{1,0:T(8,128)(2,1)S(1)}, u32[]{:S(2)}, u32[]{:S(2)}) collective-permute-start(bf16[1024,256]{1,0:T(8,128)(2,1)} %get-tuple-element.38), channel_id=1, source_target_pairs={{0,1},{1,2},{2,3},{3,4},{4,5},{5,6},{6,7},{7,8},{8,9},{9,10},{10,1... | collective-permute-start | bytes 1572872 | tf_op jit(solution)/shard_map/ppermute | solution.py:373
  38.9 11.1 %collective-permute-start.1 = (bf16[1024,256]{1,0:T(8,128)(2,1)}, bf16[1024,256]{1,0:T(8,128)(2,1)S(1)}, u32[]{:S(2)}, u32[]{:S(2)}) collective-permute-start(bf16[1024,256]{1,0:T(8,128)(2,1)} %get-tuple-element.39), channel_id=1, source_target_pairs={{1,0},{2,1},{3,2},{4,3},{5,4},{6,5},{7,6},{8,7},{9,8},{10,9},{11,1... | collective-permute-start | bytes 1572872 | tf_op jit(solution)/shard_map/ppermute | solution.py:373
  59.2 1.4 collective-permute-start.2
  60.6 8.5 %collective-permute-start.5 = (f32[32,640]{1,0:T(8,128)S(1)}, f32[32,640]{1,0:T(8,128)S(1)}, u32[]{:S(2)}, u32[]{:S(2)}) collective-permute-start(f32[32,640]{1,0:T(8,128)S(1)} %add.60), channel_id=1, source_target_pairs={{0,6},{1,25},{2,4},{3,27},{4,2},{5,29},{6,0},{7,31},{8,14},{9,17},... | collective-permute-start | bytes 245768 | tf_op jit(solution)/shard_map/ppermute | solution.py:352
  66.8 4.8 %collective-permute-start.4 = (f32[32,640]{1,0:T(8,128)S(1)}, f32[32,640]{1,0:T(8,128)S(1)}, u32[]{:S(2)}, u32[]{:S(2)}) collective-permute-start(f32[32,640]{1,0:T(8,128)S(1)} %add.60), channel_id=1, source_target_pairs={{0,4},{1,17},{2,6},{3,19},{4,0},{5,21},{6,2},{7,23},{8,12},{9,25},... | collective-permute-start | bytes 245768 | tf_op jit(solution)/shard_map/ppermute | solution.py:352
  66.8 4.8 %collective-permute-start.3 = (f32[32,640]{1,0:T(8,128)S(1)}, f32[32,640]{1,0:T(8,128)S(1)}, u32[]{:S(2)}, u32[]{:S(2)}) collective-permute-start(f32[32,640]{1,0:T(8,128)S(1)} %add.60), channel_id=1, source_target_pairs={{0,2},{1,9},{2,0},{3,11},{4,6},{5,13},{6,4},{7,15},{8,10},{9,1},{1... | collective-permute-start | bytes 245768 | tf_op jit(solution)/shard_map/ppermute | solution.py:352
  71.6 5.1 %collective-permute-start.8 = (f32[32,640]{1,0:T(8,128)S(1)}, f32[32,640]{1,0:T(8,128)S(1)}, u32[]{:S(2)}, u32[]{:S(2)}) collective-permute-start(f32[32,640]{1,0:T(8,128)S(1)} %add_add_fusion.2), channel_id=1, source_target_pairs={{0,24},{1,97},{2,26},{3,99},{4,28},{5,101},{6,30},{7,103},{8,16},{... | collective-permute-start | bytes 245768 | tf_op jit(solution)/shard_map/ppermute | solution.py:352
  74.4 4.8 %collective-permute-start.7 = (f32[32,640]{1,0:T(8,128)S(1)}, f32[32,640]{1,0:T(8,128)S(1)}, u32[]{:S(2)}, u32[]{:S(2)}) collective-permute-start(f32[32,640]{1,0:T(8,128)S(1)} %add_add_fusion.2), channel_id=1, source_target_pairs={{0,16},{1,65},{2,18},{3,67},{4,20},{5,69},{6,22},{7,71},{8,24},{9,... | collective-permute-start | bytes 245768 | tf_op jit(solution)/shard_map/ppermute | solution.py:352
  74.8 4.5 %collective-permute-start.6 = (f32[32,640]{1,0:T(8,128)S(1)}, f32[32,640]{1,0:T(8,128)S(1)}, u32[]{:S(2)}, u32[]{:S(2)}) collective-permute-start(f32[32,640]{1,0:T(8,128)S(1)} %add_add_fusion.2), channel_id=1, source_target_pairs={{0,8},{1,33},{2,10},{3,35},{4,12},{5,37},{6,14},{7,39},{8,0},{9,41... | collective-permute-start | bytes 245768 | tf_op jit(solution)/shard_map/ppermute | solution.py:352
  79.3 4.6 %collective-permute-start.11 = (f32[32,640]{1,0:T(8,128)S(1)}, f32[32,640]{1,0:T(8,128)S(1)}, u32[]{:S(2)}, u32[]{:S(2)}) collective-permute-start(f32[32,640]{1,0:T(8,128)S(1)} %add_add_fusion.1), channel_id=1, source_target_pairs={{0,96},{1,7},{2,98},{3,5},{4,100},{5,3},{6,102},{7,1},{8,104},{9,1... | collective-permute-start | bytes 245768 | tf_op jit(solution)/shard_map/ppermute | solution.py:352
  80.9 4.8 %collective-permute-start.10 = (f32[32,640]{1,0:T(8,128)S(1)}, f32[32,640]{1,0:T(8,128)S(1)}, u32[]{:S(2)}, u32[]{:S(2)}) collective-permute-start(f32[32,640]{1,0:T(8,128)S(1)} %add_add_fusion.1), channel_id=1, source_target_pairs={{0,64},{1,5},{2,66},{3,7},{4,68},{5,1},{6,70},{7,3},{8,72},{9,13},... | collective-permute-start | bytes 245768 | tf_op jit(solution)/shard_map/ppermute | solution.py:352
  80.9 4.8 %collective-permute-start.9 = (f32[32,640]{1,0:T(8,128)S(1)}, f32[32,640]{1,0:T(8,128)S(1)}, u32[]{:S(2)}, u32[]{:S(2)}) collective-permute-start(f32[32,640]{1,0:T(8,128)S(1)} %add_add_fusion.1), channel_id=1, source_target_pairs={{0,32},{1,3},{2,34},{3,1},{4,36},{5,7},{6,38},{7,5},{8,40},{9,11},... | collective-permute-start | bytes 245768 | tf_op jit(solution)/shard_map/ppermute | solution.py:352
  85.7 5.4 %collective-permute-start.12 = (f32[32,640]{1,0:T(8,128)S(1)}, f32[32,640]{1,0:T(8,128)S(1)}, u32[]{:S(2)}, u32[]{:S(2)}) collective-permute-start(f32[32,640]{1,0:T(8,128)S(1)} %add_add_fusion.mine), channel_id=1, source_target_pairs={{0,1},{1,0},{2,3},{3,2},{4,5},{5,4},{6,7},{7,6},{8,9},{9,8},{10,11... | collective-permute-start | bytes 245768 | tf_op jit(solution)/shard_map/ppermute | solution.py:352
  104.7 1.7 %collective-permute-start.13 = (bf16[448,256]{1,0:T(8,128)(2,1)S(1)}, bf16[448,256]{1,0:T(8,128)(2,1)S(1)}, u32[]{:S(2)}, u32[]{:S(2)}) collective-permute-start(bf16[448,256]{1,0:T(8,128)(2,1)S(1)} %get-tuple-element.57), channel_id=1, source_target_pairs={{0,1},{1,0},{2,3},{3,2},{4,5},{5,4},{6,7},{7,6},{8,9},{9,8},{10,11... | collective-permute-start | bytes 688136 | tf_op jit(solution)/shard_map/ppermute | solution.py:352
  106.5 8.9 %collective-permute-start.16 = (bf16[448,256]{1,0:T(8,128)(2,1)S(1)}, bf16[448,256]{1,0:T(8,128)(2,1)S(1)}, u32[]{:S(2)}, u32[]{:S(2)}) collective-permute-start(bf16[448,256]{1,0:T(8,128)(2,1)S(1)} %add_convert_fusion.3), channel_id=1, source_target_pairs={{0,6},{1,25},{2,4},{3,27},{4,2},{5,29},{6,0},{7,31},{8,14},{9,17},... | collective-permute-start | bytes 688136 | tf_op jit(solution)/shard_map/ppermute | solution.py:352
  107.7 7.7 %collective-permute-start.15 = (bf16[448,256]{1,0:T(8,128)(2,1)S(1)}, bf16[448,256]{1,0:T(8,128)(2,1)S(1)}, u32[]{:S(2)}, u32[]{:S(2)}) collective-permute-start(bf16[448,256]{1,0:T(8,128)(2,1)S(1)} %add_convert_fusion.3), channel_id=1, source_target_pairs={{0,4},{1,17},{2,6},{3,19},{4,0},{5,21},{6,2},{7,23},{8,12},{9,25},... | collective-permute-start | bytes 688136 | tf_op jit(solution)/shard_map/ppermute | solution.py:352
  108.6 7.5 %collective-permute-start.14 = (bf16[448,256]{1,0:T(8,128)(2,1)S(1)}, bf16[448,256]{1,0:T(8,128)(2,1)S(1)}, u32[]{:S(2)}, u32[]{:S(2)}) collective-permute-start(bf16[448,256]{1,0:T(8,128)(2,1)S(1)} %add_convert_fusion.3), channel_id=1, source_target_pairs={{0,2},{1,9},{2,0},{3,11},{4,6},{5,13},{6,4},{7,15},{8,10},{9,1},{1... | collective-permute-start | bytes 688136 | tf_op jit(solution)/shard_map/ppermute | solution.py:352
  116.2 8.9 %collective-permute-start.19 = (bf16[448,256]{1,0:T(8,128)(2,1)S(1)}, bf16[448,256]{1,0:T(8,128)(2,1)S(1)}, u32[]{:S(2)}, u32[]{:S(2)}) collective-permute-start(bf16[448,256]{1,0:T(8,128)(2,1)S(1)} %add_convert_fusion.2), channel_id=1, source_target_pairs={{0,24},{1,97},{2,26},{3,99},{4,28},{5,101},{6,30},{7,103},{8,16},{... | collective-permute-start | bytes 688136 | tf_op jit(solution)/shard_map/ppermute | solution.py:352
  117.9 7.2 %collective-permute-start.18 = (bf16[448,256]{1,0:T(8,128)(2,1)S(1)}, bf16[448,256]{1,0:T(8,128)(2,1)S(1)}, u32[]{:S(2)}, u32[]{:S(2)}) collective-permute-start(bf16[448,256]{1,0:T(8,128)(2,1)S(1)} %add_convert_fusion.2), channel_id=1, source_target_pairs={{0,16},{1,65},{2,18},{3,67},{4,20},{5,69},{6,22},{7,71},{8,24},{9,... | collective-permute-start | bytes 688136 | tf_op jit(solution)/shard_map/ppermute | solution.py:352
  118.6 7.1 %collective-permute-start.17 = (bf16[448,256]{1,0:T(8,128)(2,1)S(1)}, bf16[448,256]{1,0:T(8,128)(2,1)S(1)}, u32[]{:S(2)}, u32[]{:S(2)}) collective-permute-start(bf16[448,256]{1,0:T(8,128)(2,1)S(1)} %add_convert_fusion.2), channel_id=1, source_target_pairs={{0,8},{1,33},{2,10},{3,35},{4,12},{5,37},{6,14},{7,39},{8,0},{9,41... | collective-permute-start | bytes 688136 | tf_op jit(solution)/shard_map/ppermute | solution.py:352
  125.8 8.9 %collective-permute-start.22 = (bf16[448,256]{1,0:T(8,128)(2,1)S(1)}, bf16[448,256]{1,0:T(8,128)(2,1)S(1)}, u32[]{:S(2)}, u32[]{:S(2)}) collective-permute-start(bf16[448,256]{1,0:T(8,128)(2,1)S(1)} %add_convert_fusion.1), channel_id=1, source_target_pairs={{0,96},{1,7},{2,98},{3,5},{4,100},{5,3},{6,102},{7,1},{8,104},{9,1... | collective-permute-start | bytes 688136 | tf_op jit(solution)/shard_map/ppermute | solution.py:352
  127.2 7.5 %collective-permute-start.21 = (bf16[448,256]{1,0:T(8,128)(2,1)S(1)}, bf16[448,256]{1,0:T(8,128)(2,1)S(1)}, u32[]{:S(2)}, u32[]{:S(2)}) collective-permute-start(bf16[448,256]{1,0:T(8,128)(2,1)S(1)} %add_convert_fusion.1), channel_id=1, source_target_pairs={{0,64},{1,5},{2,66},{3,7},{4,68},{5,1},{6,70},{7,3},{8,72},{9,13},... | collective-permute-start | bytes 688136 | tf_op jit(solution)/shard_map/ppermute | solution.py:352
  128.4 7.0 %collective-permute-start.20 = (bf16[448,256]{1,0:T(8,128)(2,1)S(1)}, bf16[448,256]{1,0:T(8,128)(2,1)S(1)}, u32[]{:S(2)}, u32[]{:S(2)}) collective-permute-start(bf16[448,256]{1,0:T(8,128)(2,1)S(1)} %add_convert_fusion.1), channel_id=1, source_target_pairs={{0,32},{1,3},{2,34},{3,1},{4,36},{5,7},{6,38},{7,5},{8,40},{9,11},... | collective-permute-start | bytes 688136 | tf_op jit(solution)/shard_map/ppermute | solution.py:352
  135.5 9.6 %collective-permute-start.23 = (bf16[448,256]{1,0:T(8,128)(2,1)S(1)}, bf16[448,256]{1,0:T(8,128)(2,1)S(1)}, u32[]{:S(2)}, u32[]{:S(2)}) collective-permute-start(bf16[448,256]{1,0:T(8,128)(2,1)S(1)} %add_convert_fusion.mine), channel_id=1, source_target_pairs={{0,1},{1,0},{2,3},{3,2},{4,5},{5,4},{6,7},{7,6},{8,9},{9,8},{10,11... | collective-permute-start | bytes 688136 | tf_op jit(solution)/shard_map/ppermute | solution.py:352
  (14 other events, 182.9 us)

commit v3 on v2

--- a/solution.py
+++ b/solution.py
@@ -99,15 +99,9 @@
         full[half:] = mine[...].astype(full.dtype)
 
 
-def pick_kernel(rank, counts, loader, head, tail, sems):
-    start = jnp.maximum(counts[rank[0]] - HALF, 0) * BLOCK
-    start = pl.multiple_of(start, BLOCK)
-    first = pltpu.make_async_copy(loader.at[pl.ds(0, HALF * BLOCK)], head, sems.at[0])
-    last = pltpu.make_async_copy(loader.at[pl.ds(start, HALF * BLOCK)], tail, sems.at[1])
-    first.start()
-    last.start()
-    first.wait()
-    last.wait()
+def pick_kernel(rank, counts, first, last, head, tail):
+    head[...] = first[...]
+    tail[...] = last[...]
 
 
 def prep_kernel(
@@ -318,11 +312,7 @@
         split_halves(core[0], gpay, send, keep)
 
 
-def out_kernel(ptsb, cot, res, gain, wfmt, wout, toks, layer, grad, gatt):
-    @pl.when(pl.program_id(0) == 0)
-    def _():
-        attend_gradients(toks, gatt)
-
+def out_kernel(ptsb, cot, res, gain, wfmt, wout, layer, grad):
     points = ptsb[...]
     x_hat, inv_std = normalize(points)
     mixed_out = dot(res[:C], wout[...], TN)
@@ -360,12 +350,17 @@
     return (w.astype(F32) + a) + (b + c)
 
 
-def sum_over_chips(send, keep, wire):
+def sum_over_chips(send, keep, wire, beside=()):
     x = keep + swap(send, 1, 1).astype(F32)
-    x = quad_sum(x, 2, 8, wire)
-    x = quad_sum(x, 8, 32, wire)
-    x = quad_sum(x, 32, 2, wire).astype(wire)
-    return x, swap(x, 1, 1)
+    done = []
+    for i, (even, odd) in enumerate(((2, 8), (8, 32), (32, 2))):
+        x = quad_sum(x, even, odd, wire)
+        for at, arrays in beside:
+            if at == i:
+                x, arrays = lax.optimization_barrier((x, arrays))
+                done.append(arrays)
+    x = x.astype(wire)
+    return x, swap(x, 1, 1), done
 
 
 def shifted(array, by):
@@ -393,21 +388,46 @@
     rank = lax.axis_index("pts").astype(jnp.int32).reshape(1)
     core = lax.rem(rank, 2)
     edge = jax.ShapeDtypeStruct((HALF * BLOCK, C), BF)
+
+    def last_slots(t, rank, counts):
+        return (jnp.maximum(counts[rank[0]] - HALF, 0) + t, 0)
+
     head, tail = pl.pallas_call(
         pick_kernel,
-        in_specs=[SCALARS, SCALARS, HBM],
-        out_specs=[HBM, HBM],
+        grid_spec=pltpu.PrefetchScalarGridSpec(
+            num_scalar_prefetch=2,
+            grid=(HALF,),
+            in_specs=[rows_spec(C), pl.BlockSpec((BLOCK, C), last_slots)],
+            out_specs=[rows_spec(C)] * 2,
+        ),
         out_shape=[edge, edge],
-        scratch_shapes=[pltpu.SemaphoreType.DMA((2,))],
         name="pick",
-    )(rank, block_counts, loader_points)
+    )(rank, block_counts, loader_points, loader_points)
     got_prev = shifted(tail, 1)
     got_next = shifted(head, -1)
     gain = norm_gain.reshape(1, C)
     sel, d_mixed, wfmt, bd, bdt, wcol, watt = pl.pallas_call(
         prep_kernel,
-        in_specs=[SCALARS] * 3 + [pl.BlockSpec(memory_space=pltpu.VMEM)] * 7,
-        out_specs=[SCALARS] + [pl.BlockSpec(memory_space=pltpu.VMEM)] * 6,
+        grid=(1,),
+        in_specs=[SCALARS] * 3
+        + [
+            whole((ROWS, C)),
+            whole((C, C)),
+            whole((C, C)),
+            whole((C, C)),
+            whole((HEAD, SLICES)),
+            whole((1, HEAD)),
+            whole((3, HEAD, HEAD)),
+        ],
+        out_specs=[
+            SCALARS,
+            whole((ROWS, C)),
+            whole((2 * C, C)),
+            whole((HS + 32, C)),
+            whole((C, HS)),
+            whole((C, 1)),
+            whole((3, C, C)),
+        ],
         out_shape=[
             jax.ShapeDtypeStruct((4, B_DEV), jnp.int32),
             jax.ShapeDtypeStruct((ROWS, C), BF),
@@ -458,7 +478,7 @@
         sel, core, loader_points, got_prev, got_next, d_mixed, gain, w_feature, w_middle, bd
     )
 
-    mine, other = sum_over_chips(send, keep, F32)
+    mine, other, _ = sum_over_chips(send, keep, F32)
 
     res, send, keep, toks = pl.pallas_call(
         back_kernel,
@@ -502,7 +522,7 @@
         core, mine, other, watt, normed, feat, mid, d_mixed, cotangent, gain, wfmt, bd, bdt, wcol
     )
 
-    layer_out, grad_points, grad_attend = pl.pallas_call(
+    layer_out, grad_points = pl.pallas_call(
         out_kernel,
         grid=(B_DEV,),
         in_specs=[
@@ -512,18 +532,26 @@
             whole((1, C)),
             whole((2 * C, C)),
             whole((C, C)),
-            whole((4, SLICES, C)),
-        ],
-        out_specs=[rows_spec(C)] * 2 + [whole((3, HEAD, HEAD))],
-        out_shape=[wide] * 2 + [jax.ShapeDtypeStruct((3, HEAD, HEAD), F32)],
+        ],
+        out_specs=[rows_spec(C)] * 2,
+        out_shape=[wide] * 2,
         compiler_params=PARAMS,
         cost_estimate=pl.CostEstimate(
             flops=2 * ROWS * C * 3 * C, bytes_accessed=7 * ROWS * C * 2, transcendentals=0
         ),
         name="outputs",
-    )(ptsb, cotangent, res, gain, wfmt, w_output, toks)
-
-    mine, other = sum_over_chips(send, keep, BF)
+    )(ptsb, cotangent, res, gain, wfmt, w_output)
+
+    grad_attend = pl.pallas_call(
+        attend_gradients,
+        out_shape=jax.ShapeDtypeStruct((3, HEAD, HEAD), F32),
+        compiler_params=PARAMS,
+        name="attend_grads",
+    )(toks)
+
+    beside = ((0, (layer_out, grad_points)), (1, grad_attend))
+    mine, other, done = sum_over_chips(send, keep, BF, beside)
+    (layer_out, grad_points), grad_attend = done
     vmem = pl.BlockSpec(memory_space=pltpu.VMEM)
     grad_feature, grad_middle, grad_output, grad_slice, grad_temper, grad_gain = pl.pallas_call(
         unpack_kernel,

time: 147 us -> 109 us (0.74)
  Pallas kernels: 64 us -> 33.8 us
  local copies, waits for them, and re-layouts: 8.39 us -> 2.14 us
    pallas_call x2 -> x3, Pallas kernels: 35.4 us -> 7.37 us  [the longest x1 3.05 us: per_device(): pl.pallas_call(pick_kernel, grid_spec=pltpu.PrefetchScalarGridSpec(num_sc...]
    unnamed x28 -> x22, local copies, waits for them, and re-layouts: 8.39 us -> 2.14 us
    ppermute x2, waiting for transfers between devices: 0.01 us -> 4.84 us  [shifted(): lax.ppermute(array, 'pts', [(i, i + by) for i in range(n) if 0 <= i + by...]
    ppermute x22, waiting for transfers between devices: 33.3 us -> 28.5 us  [swap(): lax.ppermute(array, 'pts', [(i, i ^ (odd if i % 2 else even)) for i in ra...]
    pallas_call x1, Pallas kernels: 5.73 us -> 3.69 us  [per_device(): pl.pallas_call(out_kernel, grid=(B_DEV,), in_specs=[rows_spec(C), rows_sp...]
  transfers between devices with their start and end apart: 24 -> 24, of which waited for: 15 -> 20; matrix products, arithmetic and copies ran while one was open for 0% -> 0% of each run, Pallas kernels for 5% -> 7%
where the time goes in v3:
time: 109 us
  starting transfers between devices  38.1 us (35%)
  Pallas kernels  33.8 us (31%)
  waiting for transfers between devices  33.4 us (31%)
  local copies, waits for them, and re-layouts  2.14 us (2%)
    ppermute x22, starting transfers between devices, swap(): lax.ppermute(array, 'pts', [(i, i ^ (odd if i % 2 else even)) for i in ra...  31.7 us
    ppermute x22, waiting for transfers between devices, swap(): lax.ppermute(array, 'pts', [(i, i ^ (odd if i % 2 else even)) for i in ra...  28.5 us
    pallas_call x1, Pallas kernels, per_device(): pl.pallas_call(back_kernel, grid=(B_DEV,), in_specs=[SCALARS] + [whole((S...  13.5 us
    pallas_call x1, Pallas kernels, per_device(): pl.pallas_call(front_kernel, grid_spec=pltpu.PrefetchScalarGridSpec(num_s...  8.17 us
    ppermute x2, starting transfers between devices, shifted(): lax.ppermute(array, 'pts', [(i, i + by) for i in range(n) if 0 <= i + by...  6.42 us
    ppermute x2, waiting for transfers between devices, shifted(): lax.ppermute(array, 'pts', [(i, i + by) for i in range(n) if 0 <= i + by...  4.84 us
    pallas_call x1, Pallas kernels, per_device(): pl.pallas_call(out_kernel, grid=(B_DEV,), in_specs=[rows_spec(C), rows_sp...  3.69 us
    pallas_call x1, Pallas kernels, per_device(): pl.pallas_call(pick_kernel, grid_spec=pltpu.PrefetchScalarGridSpec(num_sc...  3.05 us
  transfers between devices with their start and end apart: 24, of which 20 were waited for; matrix products, arithmetic and copies ran while one was open for 0% of the time, Pallas kernels for 7%

profile of v3, /device:TPU:1, one launch (start us, length us, event | category | flops | bytes accessed | tf_op | source)
XLA Modules:
  0.0 108.8 jit_solution(2560015217414639428)
XLA Ops:
  0.7 3.1 %pick.1 = (bf16[1024,256]{1,0:T(8,128)(2,1)}, bf16[1024,256]{1,0:T(8,128)(2,1)}) custom-call(s32[1]{0:T(128)} %bitcast.rank, s32[128]{0:T(128)} %counts.3, bf16[4096,256]{1,0:T(8,128)(2,1)} %own.1, bf16[4096,256]{1,0:T(8,128)(2,1)} %own.1), custom_call_target="tpu_custom_call" | custom-call | tf_op jit(solution)/shard_map/pick/pallas_call | solution.py:395
  3.8 4.5 %collective-permute-start = (bf16[1024,256]{1,0:T(8,128)(2,1)}, bf16[1024,256]{1,0:T(8,128)(2,1)S(1)}, u32[]{:S(2)}, u32[]{:S(2)}) collective-permute-start(bf16[1024,256]{1,0:T(8,128)(2,1)} %get-tuple-element.42), channel_id=1, source_target_pairs={{0,1},{1,2},{2,3},{3,4},{4,5},{5,6},{6,7},{7,8},{8,9},{9,10},{10,1... | collective-permute-start | bytes 1572872 | tf_op jit(solution)/shard_map/ppermute | solution.py:368
  8.3 1.9 %collective-permute-start.1 = (bf16[1024,256]{1,0:T(8,128)(2,1)}, bf16[1024,256]{1,0:T(8,128)(2,1)S(1)}, u32[]{:S(2)}, u32[]{:S(2)}) collective-permute-start(bf16[1024,256]{1,0:T(8,128)(2,1)} %get-tuple-element.43), channel_id=1, source_target_pairs={{1,0},{2,1},{3,2},{4,3},{5,4},{6,5},{7,6},{8,7},{9,8},{10,9},{11,1... | collective-permute-start | bytes 1572872 | tf_op jit(solution)/shard_map/ppermute | solution.py:368
  12.4 1.8 %prep.1 = (s32[4,4]{1,0:T(4,128)S(1)}, bf16[2048,256]{1,0:T(8,128)(2,1)S(1)}, bf16[512,256]{1,0:T(8,128)(2,1)S(1)}, bf16[544,256]{1,0:T(8,128)(2,1)S(1)}, bf16[2...) custom-call(s32[1]{0:T(128)} %bitcast.rank, s32[128]{0:T(128)S(1)} %copy-done.8, ...), custom_call_target="tpu_custom_call" | custom-call | flops 268435456 | bytes 4194304 | tf_op jit(solution)/shard_map/prep/pallas_call | solution.py:409
  14.7 4.3 %collective-permute-done.1.nxt = bf16[1024,256]{1,0:T(8,128)(2,1)S(1)} collective-permute-done((bf16[1024,256]{1,0:T(8,128)(2,1)}, bf16[1024,256]{1,0:T(8,128)(2,1)S(1)}, u32[]{:S(2)}, u32[]{:S(2)}) %collective-permute-start.1) | collective-permute-done | bytes 524320 | tf_op jit(solution)/shard_map/ppermute | solution.py:368
  19.0 8.2 %front.1 = (bf16[2048,256]{1,0:T(8,128)(2,1)S(1)}, bf16[2048,256]{1,0:T(8,128)(2,1)S(1)}, bf16[2048,256]{1,0:T(8,128)(2,1)S(1)}, bf16[2048,256]{1,0:T(8,128)(2,1...) custom-call(s32[4,4]{1,0:T(4,128)S(1)} %get-tuple-element.41.sel, s32[1]{0:T(128)S(6)} %rem.18.core, ...), custom_call_target="tpu_custom_call" | custom-call | tf_op jit(solution)/shard_map/front/pallas_call | solution.py:452
  28.6 4.4 %collective-permute-start.5 = (f32[32,640]{1,0:T(8,128)S(1)}, f32[32,640]{1,0:T(8,128)S(1)}, u32[]{:S(2)}, u32[]{:S(2)}) collective-permute-start(f32[32,640]{1,0:T(8,128)S(1)} %add.60), channel_id=1, source_target_pairs={{0,6},{1,25},{2,4},{3,27},{4,2},{5,29},{6,0},{7,31},{8,14},{9,17},... | collective-permute-start | bytes 245768 | tf_op jit(solution)/shard_map/ppermute | solution.py:342
  33.7 1.6 %collective-permute-done.5 = f32[32,640]{1,0:T(8,128)S(1)} collective-permute-done((f32[32,640]{1,0:T(8,128)S(1)}, f32[32,640]{1,0:T(8,128)S(1)}, u32[]{:S(2)}, u32[]{:S(2)}) %collective-permute-start.5) | collective-permute-done | bytes 81952 | tf_op jit(solution)/shard_map/ppermute | solution.py:342
  35.3 2.5 %collective-permute-done.4 = f32[32,640]{1,0:T(8,128)S(1)} collective-permute-done((f32[32,640]{1,0:T(8,128)S(1)}, f32[32,640]{1,0:T(8,128)S(1)}, u32[]{:S(2)}, u32[]{:S(2)}) %collective-permute-start.4) | collective-permute-done | bytes 81952 | tf_op jit(solution)/shard_map/ppermute | solution.py:342
  37.8 2.8 %collective-permute-start.8 = (f32[32,640]{1,0:T(8,128)S(1)}, f32[32,640]{1,0:T(8,128)S(1)}, u32[]{:S(2)}, u32[]{:S(2)}) collective-permute-start(f32[32,640]{1,0:T(8,128)S(1)} %add_add_fusion.4), channel_id=1, source_target_pairs={{0,24},{1,97},{2,26},{3,99},{4,28},{5,101},{6,30},{7,103},{8,16},{... | collective-permute-start | bytes 245768 | tf_op jit(solution)/shard_map/ppermute | solution.py:342
  42.9 2.5 %collective-permute-done.7 = f32[32,640]{1,0:T(8,128)S(1)} collective-permute-done((f32[32,640]{1,0:T(8,128)S(1)}, f32[32,640]{1,0:T(8,128)S(1)}, u32[]{:S(2)}, u32[]{:S(2)}) %collective-permute-start.7) | collective-permute-done | bytes 81952 | tf_op jit(solution)/shard_map/ppermute | solution.py:342
  45.5 4.0 %collective-permute-start.11 = (f32[32,640]{1,0:T(8,128)S(1)}, f32[32,640]{1,0:T(8,128)S(1)}, u32[]{:S(2)}, u32[]{:S(2)}) collective-permute-start(f32[32,640]{1,0:T(8,128)S(1)} %add_add_fusion.3), channel_id=1, source_target_pairs={{0,96},{1,7},{2,98},{3,5},{4,100},{5,3},{6,102},{7,1},{8,104},{9,1... | collective-permute-start | bytes 245768 | tf_op jit(solution)/shard_map/ppermute | solution.py:342
  50.1 1.6 %collective-permute-done.11 = f32[32,640]{1,0:T(8,128)S(1)} collective-permute-done((f32[32,640]{1,0:T(8,128)S(1)}, f32[32,640]{1,0:T(8,128)S(1)}, u32[]{:S(2)}, u32[]{:S(2)}) %collective-permute-start.11) | collective-permute-done | bytes 81952 | tf_op jit(solution)/shard_map/ppermute | solution.py:342
  51.7 2.5 %collective-permute-done.10 = f32[32,640]{1,0:T(8,128)S(1)} collective-permute-done((f32[32,640]{1,0:T(8,128)S(1)}, f32[32,640]{1,0:T(8,128)S(1)}, u32[]{:S(2)}, u32[]{:S(2)}) %collective-permute-start.10) | collective-permute-done | bytes 81952 | tf_op jit(solution)/shard_map/ppermute | solution.py:342
  54.2 4.7 %collective-permute-start.12 = (f32[32,640]{1,0:T(8,128)S(1)}, f32[32,640]{1,0:T(8,128)S(1)}, u32[]{:S(2)}, u32[]{:S(2)}) collective-permute-start(f32[32,640]{1,0:T(8,128)S(1)} %add_add_fusion.2.mine), channel_id=1, source_target_pairs={{0,1},{1,0},{2,3},{3,2},{4,5},{5,4},{6,7},{7,6},{8,9},{9,8},{10,11... | collective-permute-start | bytes 245768 | tf_op jit(solution)/shard_map/ppermute | solution.py:342
  59.8 13.5 %back.1 = (bf16[768,2048]{1,0:T(8,128)(2,1)S(1)}, bf16[448,256]{1,0:T(8,128)(2,1)S(1)}, f32[448,256]{1,0:T(8,128)S(1)}, f32[4,64,256]{2,1,0:T(8,128)S(1)}) custom-call(s32[1]{0:T(128)S(6)} %rem.18.core, f32[32,640]{1,0:T(8,128)S(1)} %add_add_fusion.2.mine, f32[32,640]{1,0:T(8,128)S(1)} %collective-permute-done.12.other, ...), custom_call_target="tpu_custom_call" | custom-call | tf_op jit(solution)/shard_map/back/pallas_call | solution.py:483
  78.3 3.7 %outputs.1 = (bf16[2048,256]{1,0:T(8,128)(2,1)}, bf16[2048,256]{1,0:T(8,128)(2,1)}) custom-call(bf16[2048,256]{1,0:T(8,128)(2,1)S(1)} %get-tuple-element.57.ptsb, bf16[2048,256]{1,0:T(8,128)(2,1)S(1)} %copy-done.1, bf16[768,2048]{1,0:T(8,128)(2,1)S(1)} %get-tuple-element.58.res, f32[1,256]{1,0:T(1,128)S(1)} %bitcast.7, ...), custom_call_target="tpu_custom_call" | custom-call | flops 805306368 | bytes 7340032 | tf_op jit(solution)/shard_map/outputs/pallas_call | solution.py:525
  82.0 1.9 %collective-permute-done.16 = bf16[448,256]{1,0:T(8,128)(2,1)S(1)} collective-permute-done((bf16[448,256]{1,0:T(8,128)(2,1)S(1)}, bf16[448,256]{1,0:T(8,128)(2,1)S(1)}, u32[]{:S(2)}, u32[]{:S(2)}) %collective-permute-start.16) | collective-permute-done | bytes 229408 | tf_op jit(solution)/shard_map/ppermute | solution.py:342
  84.6 2.0 %collective-permute-start.18 = (bf16[448,256]{1,0:T(8,128)(2,1)S(1)}, bf16[448,256]{1,0:T(8,128)(2,1)S(1)}, u32[]{:S(2)}, u32[]{:S(2)}) collective-permute-start(bf16[448,256]{1,0:T(8,128)(2,1)S(1)} %add_add_fusion.1), channel_id=1, source_target_pairs={{0,16},{1,65},{2,18},{3,67},{4,20},{5,69},{6,22},{7,71},{8,24},{9,... | collective-permute-start | bytes 688136 | tf_op jit(solution)/shard_map/ppermute | solution.py:342
  87.9 2.6 %attend_grads.1 = f32[3,32,32]{2,1,0:T(8,128)} custom-call(f32[4,64,256]{2,1,0:T(8,128)S(1)} %get-tuple-element.64.toks), custom_call_target="tpu_custom_call" | custom-call | tf_op jit(solution)/shard_map/attend_grads/pallas_call | solution.py:545
  91.4 1.7 %collective-permute-done.17 = bf16[448,256]{1,0:T(8,128)(2,1)S(1)} collective-permute-done((bf16[448,256]{1,0:T(8,128)(2,1)S(1)}, bf16[448,256]{1,0:T(8,128)(2,1)S(1)}, u32[]{:S(2)}, u32[]{:S(2)}) %collective-permute-start.17) | collective-permute-done | bytes 229408 | tf_op jit(solution)/shard_map/ppermute | solution.py:342
  93.9 1.8 %collective-permute-start.21 = (bf16[448,256]{1,0:T(8,128)(2,1)S(1)}, bf16[448,256]{1,0:T(8,128)(2,1)S(1)}, u32[]{:S(2)}, u32[]{:S(2)}) collective-permute-start(bf16[448,256]{1,0:T(8,128)(2,1)S(1)} %add_add_fusion), channel_id=1, source_target_pairs={{0,64},{1,5},{2,66},{3,7},{4,68},{5,1},{6,70},{7,3},{8,72},{9,13},... | collective-permute-start | bytes 688136 | tf_op jit(solution)/shard_map/ppermute | solution.py:342
  97.3 3.2 %collective-permute-done.21 = bf16[448,256]{1,0:T(8,128)(2,1)S(1)} collective-permute-done((bf16[448,256]{1,0:T(8,128)(2,1)S(1)}, bf16[448,256]{1,0:T(8,128)(2,1)S(1)}, u32[]{:S(2)}, u32[]{:S(2)}) %collective-permute-start.21) | collective-permute-done | bytes 229408 | tf_op jit(solution)/shard_map/ppermute | solution.py:342
  103.3 3.3 %collective-permute-start.23 = (bf16[448,256]{1,0:T(8,128)(2,1)S(1)}, bf16[448,256]{1,0:T(8,128)(2,1)S(1)}, u32[]{:S(2)}, u32[]{:S(2)}) collective-permute-start(bf16[448,256]{1,0:T(8,128)(2,1)S(1)} %add_convert_fusion.mine), channel_id=1, source_target_pairs={{0,1},{1,0},{2,3},{3,2},{4,5},{5,4},{6,7},{7,6},{8,9},{9,8},{10,11... | collective-permute-start | bytes 688136 | tf_op jit(solution)/shard_map/ppermute | solution.py:342
  (61 shorter events, 24.0 us)
Async XLA Ops:
  3.8 10.9 %collective-permute-start = (bf16[1024,256]{1,0:T(8,128)(2,1)}, bf16[1024,256]{1,0:T(8,128)(2,1)S(1)}, u32[]{:S(2)}, u32[]{:S(2)}) collective-permute-start(bf16[1024,256]{1,0:T(8,128)(2,1)} %get-tuple-element.42), channel_id=1, source_target_pairs={{0,1},{1,2},{2,3},{3,4},{4,5},{5,6},{6,7},{7,8},{8,9},{9,10},{10,1... | collective-permute-start | bytes 1572872 | tf_op jit(solution)/shard_map/ppermute | solution.py:368
  8.3 10.7 %collective-permute-start.1 = (bf16[1024,256]{1,0:T(8,128)(2,1)}, bf16[1024,256]{1,0:T(8,128)(2,1)S(1)}, u32[]{:S(2)}, u32[]{:S(2)}) collective-permute-start(bf16[1024,256]{1,0:T(8,128)(2,1)} %get-tuple-element.43), channel_id=1, source_target_pairs={{1,0},{2,1},{3,2},{4,3},{5,4},{6,5},{7,6},{8,7},{9,8},{10,9},{11,1... | collective-permute-start | bytes 1572872 | tf_op jit(solution)/shard_map/ppermute | solution.py:368
  27.2 1.4 %collective-permute-start.2 = (f32[32,640]{1,0:T(8,128)S(1)}, f32[32,640]{1,0:T(8,128)S(1)}, u32[]{:S(2)}, u32[]{:S(2)}) collective-permute-start(f32[32,640]{1,0:T(8,128)S(1)} %get-tuple-element.47), channel_id=1, source_target_pairs={{0,1},{1,0},{2,3},{3,2},{4,5},{5,4},{6,7},{7,6},{8,9},{9,8},{10,11... | collective-permute-start | bytes 245768 | tf_op jit(solution)/shard_map/ppermute | solution.py:342
  28.6 6.7 %collective-permute-start.5 = (f32[32,640]{1,0:T(8,128)S(1)}, f32[32,640]{1,0:T(8,128)S(1)}, u32[]{:S(2)}, u32[]{:S(2)}) collective-permute-start(f32[32,640]{1,0:T(8,128)S(1)} %add.60), channel_id=1, source_target_pairs={{0,6},{1,25},{2,4},{3,27},{4,2},{5,29},{6,0},{7,31},{8,14},{9,17},... | collective-permute-start | bytes 245768 | tf_op jit(solution)/shard_map/ppermute | solution.py:342
  33.0 4.8 %collective-permute-start.4 = (f32[32,640]{1,0:T(8,128)S(1)}, f32[32,640]{1,0:T(8,128)S(1)}, u32[]{:S(2)}, u32[]{:S(2)}) collective-permute-start(f32[32,640]{1,0:T(8,128)S(1)} %add.60), channel_id=1, source_target_pairs={{0,4},{1,17},{2,6},{3,19},{4,0},{5,21},{6,2},{7,23},{8,12},{9,25},... | collective-permute-start | bytes 245768 | tf_op jit(solution)/shard_map/ppermute | solution.py:342
  33.0 4.8 %collective-permute-start.3 = (f32[32,640]{1,0:T(8,128)S(1)}, f32[32,640]{1,0:T(8,128)S(1)}, u32[]{:S(2)}, u32[]{:S(2)}) collective-permute-start(f32[32,640]{1,0:T(8,128)S(1)} %add.60), channel_id=1, source_target_pairs={{0,2},{1,9},{2,0},{3,11},{4,6},{5,13},{6,4},{7,15},{8,10},{9,1},{1... | collective-permute-start | bytes 245768 | tf_op jit(solution)/shard_map/ppermute | solution.py:342
  37.8 5.1 %collective-permute-start.8 = (f32[32,640]{1,0:T(8,128)S(1)}, f32[32,640]{1,0:T(8,128)S(1)}, u32[]{:S(2)}, u32[]{:S(2)}) collective-permute-start(f32[32,640]{1,0:T(8,128)S(1)} %add_add_fusion.4), channel_id=1, source_target_pairs={{0,24},{1,97},{2,26},{3,99},{4,28},{5,101},{6,30},{7,103},{8,16},{... | collective-permute-start | bytes 245768 | tf_op jit(solution)/shard_map/ppermute | solution.py:342
  40.6 4.8 %collective-permute-start.7 = (f32[32,640]{1,0:T(8,128)S(1)}, f32[32,640]{1,0:T(8,128)S(1)}, u32[]{:S(2)}, u32[]{:S(2)}) collective-permute-start(f32[32,640]{1,0:T(8,128)S(1)} %add_add_fusion.4), channel_id=1, source_target_pairs={{0,16},{1,65},{2,18},{3,67},{4,20},{5,69},{6,22},{7,71},{8,24},{9,... | collective-permute-start | bytes 245768 | tf_op jit(solution)/shard_map/ppermute | solution.py:342
  41.0 4.5 %collective-permute-start.6 = (f32[32,640]{1,0:T(8,128)S(1)}, f32[32,640]{1,0:T(8,128)S(1)}, u32[]{:S(2)}, u32[]{:S(2)}) collective-permute-start(f32[32,640]{1,0:T(8,128)S(1)} %add_add_fusion.4), channel_id=1, source_target_pairs={{0,8},{1,33},{2,10},{3,35},{4,12},{5,37},{6,14},{7,39},{8,0},{9,41... | collective-permute-start | bytes 245768 | tf_op jit(solution)/shard_map/ppermute | solution.py:342
  45.5 6.2 %collective-permute-start.11 = (f32[32,640]{1,0:T(8,128)S(1)}, f32[32,640]{1,0:T(8,128)S(1)}, u32[]{:S(2)}, u32[]{:S(2)}) collective-permute-start(f32[32,640]{1,0:T(8,128)S(1)} %add_add_fusion.3), channel_id=1, source_target_pairs={{0,96},{1,7},{2,98},{3,5},{4,100},{5,3},{6,102},{7,1},{8,104},{9,1... | collective-permute-start | bytes 245768 | tf_op jit(solution)/shard_map/ppermute | solution.py:342
  49.4 4.8 %collective-permute-start.10 = (f32[32,640]{1,0:T(8,128)S(1)}, f32[32,640]{1,0:T(8,128)S(1)}, u32[]{:S(2)}, u32[]{:S(2)}) collective-permute-start(f32[32,640]{1,0:T(8,128)S(1)} %add_add_fusion.3), channel_id=1, source_target_pairs={{0,64},{1,5},{2,66},{3,7},{4,68},{5,1},{6,70},{7,3},{8,72},{9,13},... | collective-permute-start | bytes 245768 | tf_op jit(solution)/shard_map/ppermute | solution.py:342
  49.4 4.8 %collective-permute-start.9 = (f32[32,640]{1,0:T(8,128)S(1)}, f32[32,640]{1,0:T(8,128)S(1)}, u32[]{:S(2)}, u32[]{:S(2)}) collective-permute-start(f32[32,640]{1,0:T(8,128)S(1)} %add_add_fusion.3), channel_id=1, source_target_pairs={{0,32},{1,3},{2,34},{3,1},{4,36},{5,7},{6,38},{7,5},{8,40},{9,11},... | collective-permute-start | bytes 245768 | tf_op jit(solution)/shard_map/ppermute | solution.py:342
  54.2 5.6 %collective-permute-start.12 = (f32[32,640]{1,0:T(8,128)S(1)}, f32[32,640]{1,0:T(8,128)S(1)}, u32[]{:S(2)}, u32[]{:S(2)}) collective-permute-start(f32[32,640]{1,0:T(8,128)S(1)} %add_add_fusion.2.mine), channel_id=1, source_target_pairs={{0,1},{1,0},{2,3},{3,2},{4,5},{5,4},{6,7},{7,6},{8,9},{9,8},{10,11... | collective-permute-start | bytes 245768 | tf_op jit(solution)/shard_map/ppermute | solution.py:342
  73.3 1.6 %collective-permute-start.13 = (bf16[448,256]{1,0:T(8,128)(2,1)S(1)}, bf16[448,256]{1,0:T(8,128)(2,1)S(1)}, u32[]{:S(2)}, u32[]{:S(2)}) collective-permute-start(bf16[448,256]{1,0:T(8,128)(2,1)S(1)} %get-tuple-element.56), channel_id=1, source_target_pairs={{0,1},{1,0},{2,3},{3,2},{4,5},{5,4},{6,7},{7,6},{8,9},{9,8},{10,11... | collective-permute-start | bytes 688136 | tf_op jit(solution)/shard_map/ppermute | solution.py:342
  74.9 8.9 %collective-permute-start.16 = (bf16[448,256]{1,0:T(8,128)(2,1)S(1)}, bf16[448,256]{1,0:T(8,128)(2,1)S(1)}, u32[]{:S(2)}, u32[]{:S(2)}) collective-permute-start(bf16[448,256]{1,0:T(8,128)(2,1)S(1)} %add_convert_fusion.1), channel_id=1, source_target_pairs={{0,6},{1,25},{2,4},{3,27},{4,2},{5,29},{6,0},{7,31},{8,14},{9,17},... | collective-permute-start | bytes 688136 | tf_op jit(solution)/shard_map/ppermute | solution.py:342
  76.2 7.7 %collective-permute-start.15 = (bf16[448,256]{1,0:T(8,128)(2,1)S(1)}, bf16[448,256]{1,0:T(8,128)(2,1)S(1)}, u32[]{:S(2)}, u32[]{:S(2)}) collective-permute-start(bf16[448,256]{1,0:T(8,128)(2,1)S(1)} %add_convert_fusion.1), channel_id=1, source_target_pairs={{0,4},{1,17},{2,6},{3,19},{4,0},{5,21},{6,2},{7,23},{8,12},{9,25},... | collective-permute-start | bytes 688136 | tf_op jit(solution)/shard_map/ppermute | solution.py:342
  76.9 7.6 %collective-permute-start.14 = (bf16[448,256]{1,0:T(8,128)(2,1)S(1)}, bf16[448,256]{1,0:T(8,128)(2,1)S(1)}, u32[]{:S(2)}, u32[]{:S(2)}) collective-permute-start(bf16[448,256]{1,0:T(8,128)(2,1)S(1)} %add_convert_fusion.1), channel_id=1, source_target_pairs={{0,2},{1,9},{2,0},{3,11},{4,6},{5,13},{6,4},{7,15},{8,10},{9,1},{1... | collective-permute-start | bytes 688136 | tf_op jit(solution)/shard_map/ppermute | solution.py:342
  84.6 6.8 %collective-permute-start.18 = (bf16[448,256]{1,0:T(8,128)(2,1)S(1)}, bf16[448,256]{1,0:T(8,128)(2,1)S(1)}, u32[]{:S(2)}, u32[]{:S(2)}) collective-permute-start(bf16[448,256]{1,0:T(8,128)(2,1)S(1)} %add_add_fusion.1), channel_id=1, source_target_pairs={{0,16},{1,65},{2,18},{3,67},{4,20},{5,69},{6,22},{7,71},{8,24},{9,... | collective-permute-start | bytes 688136 | tf_op jit(solution)/shard_map/ppermute | solution.py:342
  86.6 6.4 %collective-permute-start.17 = (bf16[448,256]{1,0:T(8,128)(2,1)S(1)}, bf16[448,256]{1,0:T(8,128)(2,1)S(1)}, u32[]{:S(2)}, u32[]{:S(2)}) collective-permute-start(bf16[448,256]{1,0:T(8,128)(2,1)S(1)} %add_add_fusion.1), channel_id=1, source_target_pairs={{0,8},{1,33},{2,10},{3,35},{4,12},{5,37},{6,14},{7,39},{8,0},{9,41... | collective-permute-start | bytes 688136 | tf_op jit(solution)/shard_map/ppermute | solution.py:342
  86.9 6.9 %collective-permute-start.19 = (bf16[448,256]{1,0:T(8,128)(2,1)S(1)}, bf16[448,256]{1,0:T(8,128)(2,1)S(1)}, u32[]{:S(2)}, u32[]{:S(2)}) collective-permute-start(bf16[448,256]{1,0:T(8,128)(2,1)S(1)} %add_add_fusion.1), channel_id=1, source_target_pairs={{0,24},{1,97},{2,26},{3,99},{4,28},{5,101},{6,30},{7,103},{8,16},{... | collective-permute-start | bytes 688136 | tf_op jit(solution)/shard_map/ppermute | solution.py:342
  93.9 6.6 %collective-permute-start.21 = (bf16[448,256]{1,0:T(8,128)(2,1)S(1)}, bf16[448,256]{1,0:T(8,128)(2,1)S(1)}, u32[]{:S(2)}, u32[]{:S(2)}) collective-permute-start(bf16[448,256]{1,0:T(8,128)(2,1)S(1)} %add_add_fusion), channel_id=1, source_target_pairs={{0,64},{1,5},{2,66},{3,7},{4,68},{5,1},{6,70},{7,3},{8,72},{9,13},... | collective-permute-start | bytes 688136 | tf_op jit(solution)/shard_map/ppermute | solution.py:342
  95.8 6.1 %collective-permute-start.20 = (bf16[448,256]{1,0:T(8,128)(2,1)S(1)}, bf16[448,256]{1,0:T(8,128)(2,1)S(1)}, u32[]{:S(2)}, u32[]{:S(2)}) collective-permute-start(bf16[448,256]{1,0:T(8,128)(2,1)S(1)} %add_add_fusion), channel_id=1, source_target_pairs={{0,32},{1,3},{2,34},{3,1},{4,36},{5,7},{6,38},{7,5},{8,40},{9,11},... | collective-permute-start | bytes 688136 | tf_op jit(solution)/shard_map/ppermute | solution.py:342
  95.8 7.4 %collective-permute-start.22 = (bf16[448,256]{1,0:T(8,128)(2,1)S(1)}, bf16[448,256]{1,0:T(8,128)(2,1)S(1)}, u32[]{:S(2)}, u32[]{:S(2)}) collective-permute-start(bf16[448,256]{1,0:T(8,128)(2,1)S(1)} %add_add_fusion), channel_id=1, source_target_pairs={{0,96},{1,7},{2,98},{3,5},{4,100},{5,3},{6,102},{7,1},{8,104},{9,1... | collective-permute-start | bytes 688136 | tf_op jit(solution)/shard_map/ppermute | solution.py:342
  103.3 4.4 %collective-permute-start.23 = (bf16[448,256]{1,0:T(8,128)(2,1)S(1)}, bf16[448,256]{1,0:T(8,128)(2,1)S(1)}, u32[]{:S(2)}, u32[]{:S(2)}) collective-permute-start(bf16[448,256]{1,0:T(8,128)(2,1)S(1)} %add_convert_fusion.mine), channel_id=1, source_target_pairs={{0,1},{1,0},{2,3},{3,2},{4,5},{5,4},{6,7},{7,6},{8,9},{9,8},{10,11... | collective-permute-start | bytes 688136 | tf_op jit(solution)/shard_map/ppermute | solution.py:342
  (11 other events, 96.1 us)

commit v4 on v3

--- a/solution.py
+++ b/solution.py
@@ -21,7 +21,9 @@
 PAY2 = 896
 BF = jnp.bfloat16
 F32 = jnp.float32
-HIGH = lax.Precision.HIGHEST
+HIGH = lax.Precision.HIGH
+G = C // 2
+GS = HS // 2
 NN = (((1,), (0,)), ((), ()))
 NT = (((1,), (1,)), ((), ()))
 TN = (((0,), (0,)), ((), ()))
@@ -58,17 +60,17 @@
     return center * inv_std, inv_std
 
 
-def slice_softmax(mid, bd):
-    out = dot(bd, mid, NT)
-    width = mid.shape[0]
+def slice_softmax(mid_t, bd):
+    out = dot(bd, mid_t)
+    width = mid_t.shape[1]
     temper = out[HS : HS + 8] + out[HS + 8 : HS + 16] + out[HS + 16 : HS + 24]
     scale = 0.5 + jnp.maximum(temper, 0.0) + jnp.log1p(jnp.exp(-jnp.abs(temper)))
     inv = 1.0 / scale
-    logits = out[:HS].reshape(HEADS, SLICES, width) * inv[:, None, :]
-    top = jnp.max(logits, axis=1, keepdims=True)
-    e = jnp.exp(logits - top)
+    powers = out[:HS].reshape(HEADS, SLICES, width) * (inv * math.log2(math.e))[:, None, :]
+    top = jnp.max(powers, axis=1, keepdims=True)
+    e = jnp.exp2(powers - top)
     prob = e * (1.0 / jnp.sum(e, axis=1, keepdims=True))
-    return temper, inv, logits, prob
+    return temper, inv, prob
 
 
 def split_halves(core, full, send, keep):
@@ -99,9 +101,9 @@
         full[half:] = mine[...].astype(full.dtype)
 
 
-def pick_kernel(rank, counts, first, last, head, tail):
-    head[...] = first[...]
-    tail[...] = last[...]
+def pick_kernel(rank, counts, inner, outer, inner_out, outer_out):
+    inner_out[...] = inner[...]
+    outer_out[...] = outer[...]
 
 
 def prep_kernel(
@@ -125,9 +127,9 @@
     start = jnp.maximum(left - HALF, 0)
     for t in range(B_DEV):
         sel[0, t] = own[t]
-        sel[1, t] = jnp.clip(left - from_prev + t - start, 0, HALF - 1)
-        sel[2, t] = jnp.clip(t - (B_DEV - from_next), 0, HALF - 1)
-        sel[3, t] = jnp.where(found[t] == 1, 0, 1 if t < HALF else 2)
+        place = left - from_prev + t - start if t < HALF else t - (B_DEV - from_next)
+        sel[1, t] = jnp.clip(place, 0, HALF - 1)
+        sel[2, t] = found[t]
 
     dmix[...] = dot(cot[...], wout[...], NT).astype(BF)
     wfmt[:C] = wf[...].T
@@ -155,33 +157,61 @@
         watt[i] = jnp.where(same_head, jnp.concatenate([wide] * HEADS, axis=0), 0.0)
 
 
-def front_kernel(
-    sel, core, own, prev, nxt, dmix, gain, wf, wm, bd,
-    ptsb, normed_out, feat_out, mid_out, send, keep, acc, den, pay
+def first_tile(t, core):
+    return t + HALF * (1 - core[0])
+
+
+def second_tile(t, core):
+    return t + HALF * core[0]
+
+
+def front_first(sel, core, own, other, dmix, gain, wf, wmt, bd, *outs):
+    *arrays, pay, acc, den = outs
+    tile = first_tile(pl.program_id(0), core)
+    front_tile(sel[2, tile], own, other, dmix, gain, wf, wmt, bd, *arrays, acc, den)
+
+    @pl.when(pl.program_id(0) == HALF - 1)
+    def _():
+        fold_sums(acc, den, pay)
+
+
+def front_second(sel, core, own, other, dmix, gain, wf, wmt, bd, pay_first, *rest):
+    *arrays, send, keep, acc, den, pay = rest[6:]
+    tile = second_tile(pl.program_id(0), core)
+    front_tile(sel[2, tile], own, other, dmix, gain, wf, wmt, bd, *arrays, acc, den)
+
+    @pl.when(pl.program_id(0) == HALF - 1)
+    def _():
+        fold_sums(acc, den, pay)
+        pay[...] += pay_first[...]
+        split_halves(core[0], pay, send, keep)
+
+
+def front_tile(
+    found, own, other, dmix, gain, wf, wmt, bd,
+    ptsb, normed_out, feat_out, mid_out, prob_out, aux, acc, den,
 ):
     t = pl.program_id(0)
-    kind = sel[3, t]
-
-    @pl.when(kind == 0)
+
+    @pl.when(found == 1)
     def _():
         ptsb[...] = own[...]
 
-    @pl.when(kind == 1)
-    def _():
-        ptsb[...] = prev[...]
-
-    @pl.when(kind == 2)
-    def _():
-        ptsb[...] = nxt[...]
+    @pl.when(found != 1)
+    def _():
+        ptsb[...] = other[...]
 
     x_hat, _ = normalize(ptsb[...])
     normed = (x_hat * gain[...]).astype(BF)
     normed_out[...] = normed
     feat = dot(normed, wf[...]).astype(BF)
-    mid = dot(normed, wm[...]).astype(BF)
+    mid_t = dot(wmt[...], normed, NT).astype(BF)
     feat_out[...] = feat
-    mid_out[...] = mid
-    _, _, _, prob = slice_softmax(mid, bd[...])
+    mid_out[...] = mid_t
+    temper, inv, prob = slice_softmax(mid_t, bd[...])
+    prob_out[...] = prob.reshape(HS, BLOCK)
+    aux[:HEADS] = inv
+    aux[HEADS:] = inv * jax.nn.sigmoid(temper)
     weights = prob.reshape(HS, BLOCK).astype(BF)
 
     @pl.when(t == 0)
@@ -189,21 +219,25 @@
         acc[...] = jnp.zeros_like(acc)
         den[...] = jnp.zeros_like(den)
 
-    acc[:, :C] += dot(weights, feat)
-    acc[:, C:] += dot(weights, dmix[...])
-    wf = weights.astype(F32)
-    den[...] += sum(wf[:, i * 128 : (i + 1) * 128] for i in range(BLOCK // 128))
-
-    @pl.when(t == B_DEV - 1)
-    def _():
-        pay[:, :C] = fold_heads(acc[:, :C])
-        pay[:, C : 2 * C] = fold_heads(acc[:, C:])
-        total = jnp.sum(den[...], axis=1, keepdims=True)
-        row_head = lax.broadcasted_iota(jnp.int32, (HS, 128), 0) // SLICES
-        lane = lax.broadcasted_iota(jnp.int32, (HS, 128), 1)
-        placed = jnp.where(row_head == lane, total, 0.0)
-        pay[:, 2 * C :] = jnp.sum(placed.reshape(HEADS, SLICES, 128), axis=0)
-        split_halves(core[0], pay, send, keep)
+    grad = dmix[...]
+    for i in range(2):
+        both = jnp.concatenate([feat[:, i * G : (i + 1) * G], grad[:, i * G : (i + 1) * G]], axis=1)
+        acc[i * GS : (i + 1) * GS] += dot(weights[i * GS : (i + 1) * GS], both)
+    den[...] += dot(weights, jnp.ones((BLOCK, 128), BF))
+
+
+def fold_sums(acc, den, pay):
+    row_head = lax.broadcasted_iota(jnp.int32, (GS, C), 0) // SLICES
+    lane_head = lax.broadcasted_iota(jnp.int32, (GS, C), 1) % G // HEAD
+    for i in range(2):
+        own_part = jnp.where(row_head == lane_head, acc[i * GS : (i + 1) * GS], 0.0)
+        folded = jnp.sum(own_part.reshape(HEADS // 2, SLICES, C), axis=0)
+        pay[:, i * G : (i + 1) * G] = folded[:, :G]
+        pay[:, C + i * G : C + (i + 1) * G] = folded[:, G:]
+    row_head = lax.broadcasted_iota(jnp.int32, (HS, 128), 0) // SLICES
+    lane = lax.broadcasted_iota(jnp.int32, (HS, 128), 1)
+    placed = jnp.where(row_head == lane, den[...], 0.0)
+    pay[:, 2 * C :] = jnp.sum(placed.reshape(HEADS, SLICES, 128), axis=0)
 
 
 def attention_step(pay, watt, an, ant, dd, toks):
@@ -237,10 +271,12 @@
     d_den = -d_numer * tokens
     dd[...] = jnp.sum(spread_heads(d_den), axis=1, keepdims=True)
     d_numer_bd = spread_heads(d_numer)
-    an[:, :C] = attended.astype(BF)
-    an[:, C:] = d_numer_bd.astype(BF)
-    ant[:C] = attended.T.astype(BF)
-    ant[C:] = d_numer_bd.T.astype(BF)
+    for i in range(2):
+        rows = slice(i * GS, (i + 1) * GS)
+        lanes = slice(i * G, (i + 1) * G)
+        both = jnp.concatenate([attended[rows, lanes], d_numer_bd[rows, lanes]], axis=1)
+        an[i] = both.astype(BF)
+        ant[i] = both.T.astype(BF)
     toks[0] = tokens
     toks[1] = dq
     toks[2] = dk
@@ -260,7 +296,7 @@
 
 
 def back_kernel(
-    core, mine, other, watt, normed, feat, mid, dmix, cot, gain, wfmt, bd, bdt, wcol,
+    core, mine, other, watt, normed, feat, mid, prob_in, aux, dmix, cot, gain, wfmt, bdt, wcol,
     res, send, keep, toks, an, ant, dd, gfm, gout, gsl, pay, gpay,
 ):
     t = pl.program_id(0)
@@ -273,17 +309,26 @@
         gout[...] = jnp.zeros_like(gout)
         gsl[...] = jnp.zeros_like(gsl)
 
-    mid_here = mid[...]
-    temper, inv, logits, prob = slice_softmax(mid_here, bd[...])
-    weights = prob.reshape(HS, BLOCK).astype(BF)
-    dw = dot(an[:, :C], dmix[...], NT) + dot(an[:, C:], feat[...], NT) + dd[...]
-    g = prob * dw.reshape(HEADS, SLICES, BLOCK)
-    dl = g - prob * jnp.sum(g, axis=1, keepdims=True)
-    d_temper = -jnp.sum(dl * logits, axis=1) * inv * jax.nn.sigmoid(temper)
+    mid_t = mid[...]
+    weights = prob_in[...].astype(BF)
+    prob = prob_in[...].reshape(HEADS, SLICES, BLOCK)
+    inv = aux[:HEADS]
+    groups = []
+    for i in range(2):
+        lanes = slice(i * G, (i + 1) * G)
+        groups.append(dot(an[i], jnp.concatenate([dmix[:, lanes], feat[:, lanes]], axis=1), NT))
+    dw = jnp.concatenate(groups, axis=0) + dd[...]
+    dw = dw.reshape(HEADS, SLICES, BLOCK)
+    dl = prob * (dw - jnp.sum(prob * dw, axis=1, keepdims=True))
     d_raw = (dl * inv[:, None, :]).reshape(HS, BLOCK).astype(BF)
-    mixed_df = dot(ant[...], weights).astype(BF)
+    direct = dot(bdt[...], d_raw)
+    inner = (mid_t.astype(F32) * direct).reshape(HEADS, HEAD, BLOCK)
+    d_temper = -jnp.sum(inner, axis=1) * aux[HEADS:]
+    low = dot(ant[0], weights[:GS]).astype(BF)
+    high = dot(ant[1], weights[GS:]).astype(BF)
+    mixed_df = jnp.concatenate([low[:G], high[:G], low[G:], high[G:]], axis=0)
     spread = jnp.broadcast_to(d_temper[:, None, :], (HEADS, HEAD, BLOCK)).reshape(C, BLOCK)
-    dm = (dot(bdt[...], d_raw) + spread * wcol[...]).astype(BF)
+    dm = (direct + spread * wcol[...]).astype(BF)
     res[: 2 * C] = mixed_df
     res[2 * C :] = dm
     normed_here = normed[...]
@@ -292,8 +337,8 @@
     gout[...] += dot(mixed_df[:C], cot[...])
     dt_hi = d_temper.astype(BF)
     dt_lo = (d_temper - dt_hi.astype(F32)).astype(BF)
-    gsl[:HS] += dot(d_raw, mid_here)
-    gsl[HS:] += dot(jnp.concatenate([dt_hi, dt_lo], axis=0), mid_here)
+    gsl[:HS] += dot(d_raw, mid_t, NT)
+    gsl[HS:] += dot(jnp.concatenate([dt_hi, dt_lo], axis=0), mid_t, NT)
 
     @pl.when(t == B_DEV - 1)
     def _():
@@ -363,9 +408,11 @@
     return x, swap(x, 1, 1), done
 
 
-def shifted(array, by):
+def neighbour_blocks(inner, outer):
     n = lax.axis_size("pts")
-    return lax.ppermute(array, "pts", [(i, i + by) for i in range(n) if 0 <= i + by < n])
+    edges = [(i, i + 1) for i in range(1, n - 1, 2)]
+    got_outer = lax.ppermute(outer, "pts", edges + [(j, i) for i, j in edges])
+    return swap(inner, 1, 1), got_outer
 
 
 def whole(shape):
@@ -389,22 +436,27 @@
     core = lax.rem(rank, 2)
     edge = jax.ShapeDtypeStruct((HALF * BLOCK, C), BF)
 
-    def last_slots(t, rank, counts):
-        return (jnp.maximum(counts[rank[0]] - HALF, 0) + t, 0)
-
-    head, tail = pl.pallas_call(
+    def tail_slot(t, rank, counts):
+        return jnp.maximum(counts[rank[0]] - HALF, 0) + t
+
+    def inner_slot(t, rank, counts):
+        return (jnp.where(rank[0] % 2 == 0, tail_slot(t, rank, counts), t), 0)
+
+    def outer_slot(t, rank, counts):
+        return (jnp.where(rank[0] % 2 == 0, t, tail_slot(t, rank, counts)), 0)
+
+    inner, outer = pl.pallas_call(
         pick_kernel,
         grid_spec=pltpu.PrefetchScalarGridSpec(
             num_scalar_prefetch=2,
             grid=(HALF,),
-            in_specs=[rows_spec(C), pl.BlockSpec((BLOCK, C), last_slots)],
+            in_specs=[pl.BlockSpec((BLOCK, C), inner_slot), pl.BlockSpec((BLOCK, C), outer_slot)],
             out_specs=[rows_spec(C)] * 2,
         ),
         out_shape=[edge, edge],
         name="pick",
     )(rank, block_counts, loader_points, loader_points)
-    got_prev = shifted(tail, 1)
-    got_next = shifted(head, -1)
+    got_inner, got_outer = neighbour_blocks(inner, outer)
     gain = norm_gain.reshape(1, C)
     sel, d_mixed, wfmt, bd, bdt, wcol, watt = pl.pallas_call(
         prep_kernel,
@@ -429,7 +481,7 @@
             whole((3, C, C)),
         ],
         out_shape=[
-            jax.ShapeDtypeStruct((4, B_DEV), jnp.int32),
+            jax.ShapeDtypeStruct((3, B_DEV), jnp.int32),
             jax.ShapeDtypeStruct((ROWS, C), BF),
             jax.ShapeDtypeStruct((2 * C, C), BF),
             jax.ShapeDtypeStruct((HS + 32, C), BF),
@@ -449,34 +501,61 @@
 
     wide = jax.ShapeDtypeStruct((ROWS, C), BF)
     half1 = jax.ShapeDtypeStruct((SLICES // 2, PAY1), F32)
-    ptsb, normed, feat, mid, send, keep = pl.pallas_call(
-        front_kernel,
+    cols_of = lambda rows: pl.BlockSpec((rows, BLOCK), lambda t, *_: (0, t))
+    arrays = [wide] * 3 + [
+        jax.ShapeDtypeStruct((C, ROWS), BF),
+        jax.ShapeDtypeStruct((HS, ROWS), F32),
+        jax.ShapeDtypeStruct((2 * HEADS, ROWS), F32),
+    ]
+
+    def front_specs(tile):
+        rows = pl.BlockSpec((BLOCK, C), lambda t, s, c: (tile(t, c), 0))
+        cols = lambda n: pl.BlockSpec((n, BLOCK), lambda t, s, c: (0, tile(t, c)))
+        ins = [
+            pl.BlockSpec((BLOCK, C), lambda t, s, c: (s[0, tile(t, c)], 0)),
+            pl.BlockSpec((BLOCK, C), lambda t, s, c: (s[1, tile(t, c)], 0)),
+            rows,
+            whole((1, C)),
+            whole((C, C)),
+            pl.BlockSpec((C, C), lambda t, s, c: (1, 0)),
+            whole((HS + 32, C)),
+        ]
+        return ins, [rows] * 3 + [cols(C), cols(HS), cols(2 * HEADS)]
+
+    sums = [pltpu.VMEM((HS, C), F32), pltpu.VMEM((HS, 128), F32)]
+    ins, outs = front_specs(first_tile)
+    *first, pay = pl.pallas_call(
+        front_first,
         grid_spec=pltpu.PrefetchScalarGridSpec(
             num_scalar_prefetch=2,
-            grid=(B_DEV,),
-            in_specs=[
-                pl.BlockSpec((BLOCK, C), lambda t, s, c: (s[0, t], 0)),
-                pl.BlockSpec((BLOCK, C), lambda t, s, c: (s[1, t], 0)),
-                pl.BlockSpec((BLOCK, C), lambda t, s, c: (s[2, t], 0)),
-                rows_spec(C),
-                whole((1, C)),
-                whole((C, C)),
-                whole((C, C)),
-                whole((HS + 32, C)),
-            ],
-            out_specs=[rows_spec(C)] * 4 + [whole((SLICES // 2, PAY1))] * 2,
-            scratch_shapes=[
-                pltpu.VMEM((HS, 2 * C), F32),
-                pltpu.VMEM((HS, 128), F32),
-                pltpu.VMEM((SLICES, PAY1), F32),
-            ],
+            grid=(HALF,),
+            in_specs=ins,
+            out_specs=outs + [whole((SLICES, PAY1))],
+            scratch_shapes=sums,
         ),
-        out_shape=[wide] * 4 + [half1] * 2,
+        out_shape=arrays + [jax.ShapeDtypeStruct((SLICES, PAY1), F32)],
         compiler_params=PARAMS,
-        name="front",
-    )(
-        sel, core, loader_points, got_prev, got_next, d_mixed, gain, w_feature, w_middle, bd
-    )
+        cost_estimate=pl.CostEstimate(
+            flops=2 * ROWS * C * 3 * C, bytes_accessed=6 * 1024 * 1024, transcendentals=0
+        ),
+        name="front_first",
+    )(sel, core, loader_points, got_inner, d_mixed, gain, w_feature, wfmt, bd)
+    ins, outs = front_specs(second_tile)
+    *first, send, keep = pl.pallas_call(
+        front_second,
+        grid_spec=pltpu.PrefetchScalarGridSpec(
+            num_scalar_prefetch=2,
+            grid=(HALF,),
+            in_specs=ins + [whole((SLICES, PAY1))] + [HBM] * 6,
+            out_specs=outs + [whole((SLICES // 2, PAY1))] * 2,
+            scratch_shapes=sums + [pltpu.VMEM((SLICES, PAY1), F32)],
+        ),
+        out_shape=arrays + [half1] * 2,
+        input_output_aliases={10 + i: i for i in range(6)},
+        compiler_params=PARAMS,
+        name="front_second",
+    )(sel, core, loader_points, got_outer, d_mixed, gain, w_feature, wfmt, bd, pay, *first)
+    ptsb, normed, feat, mid, prob, aux = first
 
     mine, other, _ = sum_over_chips(send, keep, F32)
 
@@ -486,11 +565,12 @@
         in_specs=[SCALARS]
         + [whole((SLICES // 2, PAY1))] * 2
         + [whole((3, C, C))]
-        + [rows_spec(C)] * 5
+        + [rows_spec(C)] * 2
+        + [cols_of(C), cols_of(HS), cols_of(2 * HEADS)]
+        + [rows_spec(C)] * 2
         + [
             whole((1, C)),
             whole((2 * C, C)),
-            whole((HS + 32, C)),
             whole((C, HS)),
             whole((C, 1)),
         ],
@@ -507,8 +587,8 @@
             jax.ShapeDtypeStruct((4, SLICES, C), F32),
         ],
         scratch_shapes=[
-            pltpu.VMEM((HS, 2 * C), BF),
-            pltpu.VMEM((2 * C, HS), BF),
+            pltpu.VMEM((2, GS, C), BF),
+            pltpu.VMEM((2, C, GS), BF),
             pltpu.VMEM((HS, 1), F32),
             pltpu.VMEM((2 * C, C), F32),
             pltpu.VMEM((C, C), F32),
@@ -519,7 +599,8 @@
         compiler_params=PARAMS,
         name="back",
     )(
-        core, mine, other, watt, normed, feat, mid, d_mixed, cotangent, gain, wfmt, bd, bdt, wcol
+        core, mine, other, watt, normed, feat, mid, prob, aux, d_mixed, cotangent, gain, wfmt,
+        bdt, wcol,
     )
 
     layer_out, grad_points = pl.pallas_call(

time: 109 us -> 99.9 us (0.917)
  waiting for transfers between devices: 33.4 us -> 28.8 us
  Pallas kernels: 33.8 us -> 30 us
    ppermute x2 -> x1, waiting for transfers between devices: 4.84 us -> 0.01 us  [neighbour_blocks(): got_outer = lax.ppermute(outer, 'pts', edges + [(j, i) for i, j in edges])]
    pallas_call x1, Pallas kernels: 13.5 us -> 9.22 us  [per_device(): pl.pallas_call(back_kernel, grid=(B_DEV,), in_specs=[SCALARS] + [whole((S...]
    ppermute x2 -> x1, starting transfers between devices: 6.42 us -> 3.08 us  [neighbour_blocks(): got_outer = lax.ppermute(outer, 'pts', edges + [(j, i) for i, j in edges])]
    ppermute x22 -> x23, starting transfers between devices: 31.7 us -> 34.3 us  [swap(): lax.ppermute(array, 'pts', [(i, i ^ (odd if i % 2 else even)) for i in ra...]
    pallas_call x1 -> x2, Pallas kernels: 8.17 us -> 9.32 us  [the longest x1 4.68 us: per_device(): pl.pallas_call(front_second, grid_spec=pltpu.PrefetchScalarGridSpec(num_s...]
    ppermute x22 -> x23, waiting for transfers between devices: 28.5 us -> 28.8 us  [swap(): lax.ppermute(array, 'pts', [(i, i ^ (odd if i % 2 else even)) for i in ra...]
  transfers between devices with their start and end apart: 24 -> 24, of which waited for: 20 -> 18; matrix products, arithmetic and copies ran while one was open for 0% -> 0% of each run, Pallas kernels for 7% -> 12%
where the time goes in v4:
time: 99.9 us; the launch traced here: 99.7 us
  starting transfers between devices  37.4 us (37%)
  Pallas kernels  30 us (30%)
  waiting for transfers between devices  28.8 us (29%)
  local copies, waits for them, and re-layouts  2.14 us (2%)
    ppermute x23, starting transfers between devices, swap(): lax.ppermute(array, 'pts', [(i, i ^ (odd if i % 2 else even)) for i in ra...  34.3 us
    ppermute x23, waiting for transfers between devices, swap(): lax.ppermute(array, 'pts', [(i, i ^ (odd if i % 2 else even)) for i in ra...  28.8 us
    pallas_call x1, Pallas kernels, per_device(): pl.pallas_call(back_kernel, grid=(B_DEV,), in_specs=[SCALARS] + [whole((S...  9.22 us
    pallas_call x1, Pallas kernels, per_device(): pl.pallas_call(front_second, grid_spec=pltpu.PrefetchScalarGridSpec(num_s...  4.68 us
    pallas_call x1, Pallas kernels, per_device(): pl.pallas_call(front_first, grid_spec=pltpu.PrefetchScalarGridSpec(num_sc...  4.64 us
    pallas_call x1, Pallas kernels, per_device(): pl.pallas_call(out_kernel, grid=(B_DEV,), in_specs=[rows_spec(C), rows_sp...  3.69 us
    ppermute x1, starting transfers between devices, neighbour_blocks(): got_outer = lax.ppermute(outer, 'pts', edges + [(j, i) for i, j in edges])  3.08 us
    pallas_call x1, Pallas kernels, per_device(): pl.pallas_call(pick_kernel, grid_spec=pltpu.PrefetchScalarGridSpec(num_sc...  3.08 us
  transfers between devices with their start and end apart: 24, of which 18 were waited for; matrix products, arithmetic and copies ran while one was open for 0% of the time, Pallas kernels for 12%

profile of v4, /device:TPU:1, one launch (start us, length us, event | category | flops | bytes accessed | tf_op | source)
XLA Modules:
  0.0 99.7 jit_solution(13790108528673702294)
XLA Ops:
  0.7 3.1 %pick.1 = (bf16[1024,256]{1,0:T(8,128)(2,1)}, bf16[1024,256]{1,0:T(8,128)(2,1)}) custom-call(s32[1]{0:T(128)} %bitcast.rank, s32[128]{0:T(128)} %counts.3, bf16[4096,256]{1,0:T(8,128)(2,1)} %own.3, bf16[4096,256]{1,0:T(8,128)(2,1)} %own.3), custom_call_target="tpu_custom_call" | custom-call | tf_op jit(solution)/shard_map/pick/pallas_call | solution.py:448
  5.2 3.1 %collective-permute-start = (bf16[1024,256]{1,0:T(8,128)(2,1)}, bf16[1024,256]{1,0:T(8,128)(2,1)S(1)}, u32[]{:S(2)}, u32[]{:S(2)}) collective-permute-start(bf16[1024,256]{1,0:T(8,128)(2,1)} %get-tuple-element.51), channel_id=1, source_target_pairs={{1,2},{3,4},{5,6},{7,8},{9,10},{11,12},{13,14},{15,16},{17,18},{19... | collective-permute-start | bytes 1572872 | tf_op jit(solution)/shard_map/ppermute | solution.py:414
  10.5 1.8 %prep.1 = (s32[3,4]{1,0:T(4,128)S(1)}, bf16[2048,256]{1,0:T(8,128)(2,1)S(1)}, bf16[512,256]{1,0:T(8,128)(2,1)S(1)}, bf16[544,256]{1,0:T(8,128)(2,1)S(1)}, bf16[2...) custom-call(s32[1]{0:T(128)} %bitcast.rank, s32[128]{0:T(128)S(1)} %copy-done.8, ...), custom_call_target="tpu_custom_call" | custom-call | flops 268435456 | bytes 4194304 | tf_op jit(solution)/shard_map/prep/pallas_call | solution.py:461
  12.3 4.6 %front_first.1 = (bf16[2048,256]{1,0:T(8,128)(2,1)S(1)}, bf16[2048,256]{1,0:T(8,128)(2,1)S(1)}, bf16[2048,256]{1,0:T(8,128)(2,1)S(1)}, bf16[256,2048]{1,0:T(8,12...) custom-call(s32[3,4]{1,0:T(4,128)S(1)} %get-tuple-element.50.sel, ...), custom_call_target="tpu_custom_call" | custom-call | flops 805306368 | bytes 6291456 | tf_op jit(solution)/shard_map/front_first/pallas_call | solution.py:527
  17.0 4.7 %front_second.1 = (bf16[2048,256]{1,0:T(8,128)(2,1)S(1)}, bf16[2048,256]{1,0:T(8,128)(2,1)S(1)}, bf16[2048,256]{1,0:T(8,128)(2,1)S(1)}, bf16[256,2048]{1,0:T(8,1...) custom-call(s32[3,4]{1,0:T(4,128)S(1)} %get-tuple-element.50.sel, ...), custom_call_target="tpu_custom_call", output_to_operand_aliasing={{0}: (10, {}), {1}: (11, {}), {2}: (12, {}), {3}: (13, {}),... | custom-call | tf_op jit(solution)/shard_map/front_second/pallas_call | solution.py:544
  23.1 5.1 %collective-permute-start.5 = (f32[32,640]{1,0:T(8,128)S(1)}, f32[32,640]{1,0:T(8,128)S(1)}, u32[]{:S(2)}, u32[]{:S(2)}) collective-permute-start(f32[32,640]{1,0:T(8,128)S(1)} %add.60), channel_id=1, source_target_pairs={{0,6},{1,25},{2,4},{3,27},{4,2},{5,29},{6,0},{7,31},{8,14},{9,17},... | collective-permute-start | bytes 245768 | tf_op jit(solution)/shard_map/ppermute | solution.py:387
  28.8 1.6 %collective-permute-done.5 = f32[32,640]{1,0:T(8,128)S(1)} collective-permute-done((f32[32,640]{1,0:T(8,128)S(1)}, f32[32,640]{1,0:T(8,128)S(1)}, u32[]{:S(2)}, u32[]{:S(2)}) %collective-permute-start.5) | collective-permute-done | bytes 81952 | tf_op jit(solution)/shard_map/ppermute | solution.py:387
  30.4 2.5 %collective-permute-done.4 = f32[32,640]{1,0:T(8,128)S(1)} collective-permute-done((f32[32,640]{1,0:T(8,128)S(1)}, f32[32,640]{1,0:T(8,128)S(1)}, u32[]{:S(2)}, u32[]{:S(2)}) %collective-permute-start.4) | collective-permute-done | bytes 81952 | tf_op jit(solution)/shard_map/ppermute | solution.py:387
  33.0 4.3 %collective-permute-start.8 = (f32[32,640]{1,0:T(8,128)S(1)}, f32[32,640]{1,0:T(8,128)S(1)}, u32[]{:S(2)}, u32[]{:S(2)}) collective-permute-start(f32[32,640]{1,0:T(8,128)S(1)} %add_add_fusion.4), channel_id=1, source_target_pairs={{0,24},{1,97},{2,26},{3,99},{4,28},{5,101},{6,30},{7,103},{8,16},{... | collective-permute-start | bytes 245768 | tf_op jit(solution)/shard_map/ppermute | solution.py:387
  38.0 1.6 %collective-permute-done.8 = f32[32,640]{1,0:T(8,128)S(1)} collective-permute-done((f32[32,640]{1,0:T(8,128)S(1)}, f32[32,640]{1,0:T(8,128)S(1)}, u32[]{:S(2)}, u32[]{:S(2)}) %collective-permute-start.8) | collective-permute-done | bytes 81952 | tf_op jit(solution)/shard_map/ppermute | solution.py:387
  39.6 2.5 %collective-permute-done.7 = f32[32,640]{1,0:T(8,128)S(1)} collective-permute-done((f32[32,640]{1,0:T(8,128)S(1)}, f32[32,640]{1,0:T(8,128)S(1)}, u32[]{:S(2)}, u32[]{:S(2)}) %collective-permute-start.7) | collective-permute-done | bytes 81952 | tf_op jit(solution)/shard_map/ppermute | solution.py:387
  42.1 2.1 %collective-permute-start.11 = (f32[32,640]{1,0:T(8,128)S(1)}, f32[32,640]{1,0:T(8,128)S(1)}, u32[]{:S(2)}, u32[]{:S(2)}) collective-permute-start(f32[32,640]{1,0:T(8,128)S(1)} %add_add_fusion.3), channel_id=1, source_target_pairs={{0,96},{1,7},{2,98},{3,5},{4,100},{5,3},{6,102},{7,1},{8,104},{9,1... | collective-permute-start | bytes 245768 | tf_op jit(solution)/shard_map/ppermute | solution.py:387
  46.7 2.4 %collective-permute-done.10 = f32[32,640]{1,0:T(8,128)S(1)} collective-permute-done((f32[32,640]{1,0:T(8,128)S(1)}, f32[32,640]{1,0:T(8,128)S(1)}, u32[]{:S(2)}, u32[]{:S(2)}) %collective-permute-start.10) | collective-permute-done | bytes 81952 | tf_op jit(solution)/shard_map/ppermute | solution.py:387
  49.1 4.7 %collective-permute-start.12 = (f32[32,640]{1,0:T(8,128)S(1)}, f32[32,640]{1,0:T(8,128)S(1)}, u32[]{:S(2)}, u32[]{:S(2)}) collective-permute-start(f32[32,640]{1,0:T(8,128)S(1)} %add_add_fusion.2.mine), channel_id=1, source_target_pairs={{0,1},{1,0},{2,3},{3,2},{4,5},{5,4},{6,7},{7,6},{8,9},{9,8},{10,11... | collective-permute-start | bytes 245768 | tf_op jit(solution)/shard_map/ppermute | solution.py:387
  54.7 9.2 %back.1 = (bf16[768,2048]{1,0:T(8,128)(2,1)S(1)}, bf16[448,256]{1,0:T(8,128)(2,1)S(1)}, f32[448,256]{1,0:T(8,128)S(1)}, f32[4,64,256]{2,1,0:T(8,128)S(1)}) custom-call(s32[1]{0:T(128)S(6)} %rem.18.core, f32[32,640]{1,0:T(8,128)S(1)} %add_add_fusion.2.mine, f32[32,640]{1,0:T(8,128)S(1)} %collective-permute-done.12.other, ...), custom_call_target="tpu_custom_call" | custom-call | tf_op jit(solution)/shard_map/back/pallas_call | solution.py:562
  68.9 3.7 %outputs.1 = (bf16[2048,256]{1,0:T(8,128)(2,1)}, bf16[2048,256]{1,0:T(8,128)(2,1)}) custom-call(bf16[2048,256]{1,0:T(8,128)(2,1)S(1)} %get-tuple-element.75.ptsb, bf16[2048,256]{1,0:T(8,128)(2,1)S(1)} %copy-done.1, bf16[768,2048]{1,0:T(8,128)(2,1)S(1)} %get-tuple-element.76.res, f32[1,256]{1,0:T(1,128)S(1)} %bitcast.8, ...), custom_call_target="tpu_custom_call" | custom-call | flops 805306368 | bytes 7340032 | tf_op jit(solution)/shard_map/outputs/pallas_call | solution.py:606
  72.6 1.9 %collective-permute-done.16 = bf16[448,256]{1,0:T(8,128)(2,1)S(1)} collective-permute-done((bf16[448,256]{1,0:T(8,128)(2,1)S(1)}, bf16[448,256]{1,0:T(8,128)(2,1)S(1)}, u32[]{:S(2)}, u32[]{:S(2)}) %collective-permute-start.16) | collective-permute-done | bytes 229408 | tf_op jit(solution)/shard_map/ppermute | solution.py:387
  75.2 2.3 %collective-permute-start.18 = (bf16[448,256]{1,0:T(8,128)(2,1)S(1)}, bf16[448,256]{1,0:T(8,128)(2,1)S(1)}, u32[]{:S(2)}, u32[]{:S(2)}) collective-permute-start(bf16[448,256]{1,0:T(8,128)(2,1)S(1)} %add_add_fusion.1), channel_id=1, source_target_pairs={{0,16},{1,65},{2,18},{3,67},{4,20},{5,69},{6,22},{7,71},{8,24},{9,... | collective-permute-start | bytes 688136 | tf_op jit(solution)/shard_map/ppermute | solution.py:387
  78.6 1.7 %attend_grads.1 = f32[3,32,32]{2,1,0:T(8,128)} custom-call(f32[4,64,256]{2,1,0:T(8,128)S(1)} %get-tuple-element.82.toks), custom_call_target="tpu_custom_call" | custom-call | tf_op jit(solution)/shard_map/attend_grads/pallas_call | solution.py:626
  80.3 1.7 %collective-permute-done.18 = bf16[448,256]{1,0:T(8,128)(2,1)S(1)} collective-permute-done((bf16[448,256]{1,0:T(8,128)(2,1)S(1)}, bf16[448,256]{1,0:T(8,128)(2,1)S(1)}, u32[]{:S(2)}, u32[]{:S(2)}) %collective-permute-start.18) | collective-permute-done | bytes 229408 | tf_op jit(solution)/shard_map/ppermute | solution.py:387
  82.0 2.0 %collective-permute-done.17 = bf16[448,256]{1,0:T(8,128)(2,1)S(1)} collective-permute-done((bf16[448,256]{1,0:T(8,128)(2,1)S(1)}, bf16[448,256]{1,0:T(8,128)(2,1)S(1)}, u32[]{:S(2)}, u32[]{:S(2)}) %collective-permute-start.17) | collective-permute-done | bytes 229408 | tf_op jit(solution)/shard_map/ppermute | solution.py:387
  84.6 1.8 %collective-permute-start.21 = (bf16[448,256]{1,0:T(8,128)(2,1)S(1)}, bf16[448,256]{1,0:T(8,128)(2,1)S(1)}, u32[]{:S(2)}, u32[]{:S(2)}) collective-permute-start(bf16[448,256]{1,0:T(8,128)(2,1)S(1)} %add_add_fusion), channel_id=1, source_target_pairs={{0,64},{1,5},{2,66},{3,7},{4,68},{5,1},{6,70},{7,3},{8,72},{9,13},... | collective-permute-start | bytes 688136 | tf_op jit(solution)/shard_map/ppermute | solution.py:387
  87.9 3.2 %collective-permute-done.21 = bf16[448,256]{1,0:T(8,128)(2,1)S(1)} collective-permute-done((bf16[448,256]{1,0:T(8,128)(2,1)S(1)}, bf16[448,256]{1,0:T(8,128)(2,1)S(1)}, u32[]{:S(2)}, u32[]{:S(2)}) %collective-permute-start.21) | collective-permute-done | bytes 229408 | tf_op jit(solution)/shard_map/ppermute | solution.py:387
  93.9 3.6 %collective-permute-start.23 = (bf16[448,256]{1,0:T(8,128)(2,1)S(1)}, bf16[448,256]{1,0:T(8,128)(2,1)S(1)}, u32[]{:S(2)}, u32[]{:S(2)}) collective-permute-start(bf16[448,256]{1,0:T(8,128)(2,1)S(1)} %add_convert_fusion.mine), channel_id=1, source_target_pairs={{0,1},{1,0},{2,3},{3,2},{4,5},{5,4},{6,7},{7,6},{8,9},{9,8},{10,11... | collective-permute-start | bytes 688136 | tf_op jit(solution)/shard_map/ppermute | solution.py:387
  (62 shorter events, 23.6 us)
Async XLA Ops:
  3.8 8.5 %collective-permute-start.1 = (bf16[1024,256]{1,0:T(8,128)(2,1)}, bf16[1024,256]{1,0:T(8,128)(2,1)S(1)}, u32[]{:S(2)}, u32[]{:S(2)}) collective-permute-start(bf16[1024,256]{1,0:T(8,128)(2,1)} %get-tuple-element.55), channel_id=1, source_target_pairs={{0,1},{1,0},{2,3},{3,2},{4,5},{5,4},{6,7},{7,6},{8,9},{9,8},{10,11... | collective-permute-start | bytes 1572872 | tf_op jit(solution)/shard_map/ppermute | solution.py:387
  5.2 11.8 %collective-permute-start = (bf16[1024,256]{1,0:T(8,128)(2,1)}, bf16[1024,256]{1,0:T(8,128)(2,1)S(1)}, u32[]{:S(2)}, u32[]{:S(2)}) collective-permute-start(bf16[1024,256]{1,0:T(8,128)(2,1)} %get-tuple-element.51), channel_id=1, source_target_pairs={{1,2},{3,4},{5,6},{7,8},{9,10},{11,12},{13,14},{15,16},{17,18},{19... | collective-permute-start | bytes 1572872 | tf_op jit(solution)/shard_map/ppermute | solution.py:414
  21.7 1.4 %collective-permute-start.2 = (f32[32,640]{1,0:T(8,128)S(1)}, f32[32,640]{1,0:T(8,128)S(1)}, u32[]{:S(2)}, u32[]{:S(2)}) collective-permute-start(f32[32,640]{1,0:T(8,128)S(1)} %get-tuple-element.64), channel_id=1, source_target_pairs={{0,1},{1,0},{2,3},{3,2},{4,5},{5,4},{6,7},{7,6},{8,9},{9,8},{10,11... | collective-permute-start | bytes 245768 | tf_op jit(solution)/shard_map/ppermute | solution.py:387
  23.1 7.4 %collective-permute-start.5 = (f32[32,640]{1,0:T(8,128)S(1)}, f32[32,640]{1,0:T(8,128)S(1)}, u32[]{:S(2)}, u32[]{:S(2)}) collective-permute-start(f32[32,640]{1,0:T(8,128)S(1)} %add.60), channel_id=1, source_target_pairs={{0,6},{1,25},{2,4},{3,27},{4,2},{5,29},{6,0},{7,31},{8,14},{9,17},... | collective-permute-start | bytes 245768 | tf_op jit(solution)/shard_map/ppermute | solution.py:387
  28.2 4.8 %collective-permute-start.4 = (f32[32,640]{1,0:T(8,128)S(1)}, f32[32,640]{1,0:T(8,128)S(1)}, u32[]{:S(2)}, u32[]{:S(2)}) collective-permute-start(f32[32,640]{1,0:T(8,128)S(1)} %add.60), channel_id=1, source_target_pairs={{0,4},{1,17},{2,6},{3,19},{4,0},{5,21},{6,2},{7,23},{8,12},{9,25},... | collective-permute-start | bytes 245768 | tf_op jit(solution)/shard_map/ppermute | solution.py:387
  28.2 4.8 %collective-permute-start.3 = (f32[32,640]{1,0:T(8,128)S(1)}, f32[32,640]{1,0:T(8,128)S(1)}, u32[]{:S(2)}, u32[]{:S(2)}) collective-permute-start(f32[32,640]{1,0:T(8,128)S(1)} %add.60), channel_id=1, source_target_pairs={{0,2},{1,9},{2,0},{3,11},{4,6},{5,13},{6,4},{7,15},{8,10},{9,1},{1... | collective-permute-start | bytes 245768 | tf_op jit(solution)/shard_map/ppermute | solution.py:387
  33.0 6.6 %collective-permute-start.8 = (f32[32,640]{1,0:T(8,128)S(1)}, f32[32,640]{1,0:T(8,128)S(1)}, u32[]{:S(2)}, u32[]{:S(2)}) collective-permute-start(f32[32,640]{1,0:T(8,128)S(1)} %add_add_fusion.4), channel_id=1, source_target_pairs={{0,24},{1,97},{2,26},{3,99},{4,28},{5,101},{6,30},{7,103},{8,16},{... | collective-permute-start | bytes 245768 | tf_op jit(solution)/shard_map/ppermute | solution.py:387
  37.3 4.8 %collective-permute-start.7 = (f32[32,640]{1,0:T(8,128)S(1)}, f32[32,640]{1,0:T(8,128)S(1)}, u32[]{:S(2)}, u32[]{:S(2)}) collective-permute-start(f32[32,640]{1,0:T(8,128)S(1)} %add_add_fusion.4), channel_id=1, source_target_pairs={{0,16},{1,65},{2,18},{3,67},{4,20},{5,69},{6,22},{7,71},{8,24},{9,... | collective-permute-start | bytes 245768 | tf_op jit(solution)/shard_map/ppermute | solution.py:387
  37.4 4.7 %collective-permute-start.6 = (f32[32,640]{1,0:T(8,128)S(1)}, f32[32,640]{1,0:T(8,128)S(1)}, u32[]{:S(2)}, u32[]{:S(2)}) collective-permute-start(f32[32,640]{1,0:T(8,128)S(1)} %add_add_fusion.4), channel_id=1, source_target_pairs={{0,8},{1,33},{2,10},{3,35},{4,12},{5,37},{6,14},{7,39},{8,0},{9,41... | collective-permute-start | bytes 245768 | tf_op jit(solution)/shard_map/ppermute | solution.py:387
  42.1 4.6 %collective-permute-start.11 = (f32[32,640]{1,0:T(8,128)S(1)}, f32[32,640]{1,0:T(8,128)S(1)}, u32[]{:S(2)}, u32[]{:S(2)}) collective-permute-start(f32[32,640]{1,0:T(8,128)S(1)} %add_add_fusion.3), channel_id=1, source_target_pairs={{0,96},{1,7},{2,98},{3,5},{4,100},{5,3},{6,102},{7,1},{8,104},{9,1... | collective-permute-start | bytes 245768 | tf_op jit(solution)/shard_map/ppermute | solution.py:387
  44.3 4.8 %collective-permute-start.10 = (f32[32,640]{1,0:T(8,128)S(1)}, f32[32,640]{1,0:T(8,128)S(1)}, u32[]{:S(2)}, u32[]{:S(2)}) collective-permute-start(f32[32,640]{1,0:T(8,128)S(1)} %add_add_fusion.3), channel_id=1, source_target_pairs={{0,64},{1,5},{2,66},{3,7},{4,68},{5,1},{6,70},{7,3},{8,72},{9,13},... | collective-permute-start | bytes 245768 | tf_op jit(solution)/shard_map/ppermute | solution.py:387
  44.3 4.8 %collective-permute-start.9 = (f32[32,640]{1,0:T(8,128)S(1)}, f32[32,640]{1,0:T(8,128)S(1)}, u32[]{:S(2)}, u32[]{:S(2)}) collective-permute-start(f32[32,640]{1,0:T(8,128)S(1)} %add_add_fusion.3), channel_id=1, source_target_pairs={{0,32},{1,3},{2,34},{3,1},{4,36},{5,7},{6,38},{7,5},{8,40},{9,11},... | collective-permute-start | bytes 245768 | tf_op jit(solution)/shard_map/ppermute | solution.py:387
  49.1 5.6 %collective-permute-start.12 = (f32[32,640]{1,0:T(8,128)S(1)}, f32[32,640]{1,0:T(8,128)S(1)}, u32[]{:S(2)}, u32[]{:S(2)}) collective-permute-start(f32[32,640]{1,0:T(8,128)S(1)} %add_add_fusion.2.mine), channel_id=1, source_target_pairs={{0,1},{1,0},{2,3},{3,2},{4,5},{5,4},{6,7},{7,6},{8,9},{9,8},{10,11... | collective-permute-start | bytes 245768 | tf_op jit(solution)/shard_map/ppermute | solution.py:387
  63.9 1.6 %collective-permute-start.13 = (bf16[448,256]{1,0:T(8,128)(2,1)S(1)}, bf16[448,256]{1,0:T(8,128)(2,1)S(1)}, u32[]{:S(2)}, u32[]{:S(2)}) collective-permute-start(bf16[448,256]{1,0:T(8,128)(2,1)S(1)} %get-tuple-element.74), channel_id=1, source_target_pairs={{0,1},{1,0},{2,3},{3,2},{4,5},{5,4},{6,7},{7,6},{8,9},{9,8},{10,11... | collective-permute-start | bytes 688136 | tf_op jit(solution)/shard_map/ppermute | solution.py:387
  65.6 8.9 %collective-permute-start.16 = (bf16[448,256]{1,0:T(8,128)(2,1)S(1)}, bf16[448,256]{1,0:T(8,128)(2,1)S(1)}, u32[]{:S(2)}, u32[]{:S(2)}) collective-permute-start(bf16[448,256]{1,0:T(8,128)(2,1)S(1)} %add_convert_fusion.1), channel_id=1, source_target_pairs={{0,6},{1,25},{2,4},{3,27},{4,2},{5,29},{6,0},{7,31},{8,14},{9,17},... | collective-permute-start | bytes 688136 | tf_op jit(solution)/shard_map/ppermute | solution.py:387
  66.8 7.7 %collective-permute-start.15 = (bf16[448,256]{1,0:T(8,128)(2,1)S(1)}, bf16[448,256]{1,0:T(8,128)(2,1)S(1)}, u32[]{:S(2)}, u32[]{:S(2)}) collective-permute-start(bf16[448,256]{1,0:T(8,128)(2,1)S(1)} %add_convert_fusion.1), channel_id=1, source_target_pairs={{0,4},{1,17},{2,6},{3,19},{4,0},{5,21},{6,2},{7,23},{8,12},{9,25},... | collective-permute-start | bytes 688136 | tf_op jit(solution)/shard_map/ppermute | solution.py:387
  67.5 7.6 %collective-permute-start.14 = (bf16[448,256]{1,0:T(8,128)(2,1)S(1)}, bf16[448,256]{1,0:T(8,128)(2,1)S(1)}, u32[]{:S(2)}, u32[]{:S(2)}) collective-permute-start(bf16[448,256]{1,0:T(8,128)(2,1)S(1)} %add_convert_fusion.1), channel_id=1, source_target_pairs={{0,2},{1,9},{2,0},{3,11},{4,6},{5,13},{6,4},{7,15},{8,10},{9,1},{1... | collective-permute-start | bytes 688136 | tf_op jit(solution)/shard_map/ppermute | solution.py:387
  75.2 6.8 %collective-permute-start.18 = (bf16[448,256]{1,0:T(8,128)(2,1)S(1)}, bf16[448,256]{1,0:T(8,128)(2,1)S(1)}, u32[]{:S(2)}, u32[]{:S(2)}) collective-permute-start(bf16[448,256]{1,0:T(8,128)(2,1)S(1)} %add_add_fusion.1), channel_id=1, source_target_pairs={{0,16},{1,65},{2,18},{3,67},{4,20},{5,69},{6,22},{7,71},{8,24},{9,... | collective-permute-start | bytes 688136 | tf_op jit(solution)/shard_map/ppermute | solution.py:387
  77.5 6.4 %collective-permute-start.17 = (bf16[448,256]{1,0:T(8,128)(2,1)S(1)}, bf16[448,256]{1,0:T(8,128)(2,1)S(1)}, u32[]{:S(2)}, u32[]{:S(2)}) collective-permute-start(bf16[448,256]{1,0:T(8,128)(2,1)S(1)} %add_add_fusion.1), channel_id=1, source_target_pairs={{0,8},{1,33},{2,10},{3,35},{4,12},{5,37},{6,14},{7,39},{8,0},{9,41... | collective-permute-start | bytes 688136 | tf_op jit(solution)/shard_map/ppermute | solution.py:387
  77.8 6.6 %collective-permute-start.19 = (bf16[448,256]{1,0:T(8,128)(2,1)S(1)}, bf16[448,256]{1,0:T(8,128)(2,1)S(1)}, u32[]{:S(2)}, u32[]{:S(2)}) collective-permute-start(bf16[448,256]{1,0:T(8,128)(2,1)S(1)} %add_add_fusion.1), channel_id=1, source_target_pairs={{0,24},{1,97},{2,26},{3,99},{4,28},{5,101},{6,30},{7,103},{8,16},{... | collective-permute-start | bytes 688136 | tf_op jit(solution)/shard_map/ppermute | solution.py:387
  84.6 6.6 %collective-permute-start.21 = (bf16[448,256]{1,0:T(8,128)(2,1)S(1)}, bf16[448,256]{1,0:T(8,128)(2,1)S(1)}, u32[]{:S(2)}, u32[]{:S(2)}) collective-permute-start(bf16[448,256]{1,0:T(8,128)(2,1)S(1)} %add_add_fusion), channel_id=1, source_target_pairs={{0,64},{1,5},{2,66},{3,7},{4,68},{5,1},{6,70},{7,3},{8,72},{9,13},... | collective-permute-start | bytes 688136 | tf_op jit(solution)/shard_map/ppermute | solution.py:387
  86.4 6.1 %collective-permute-start.20 = (bf16[448,256]{1,0:T(8,128)(2,1)S(1)}, bf16[448,256]{1,0:T(8,128)(2,1)S(1)}, u32[]{:S(2)}, u32[]{:S(2)}) collective-permute-start(bf16[448,256]{1,0:T(8,128)(2,1)S(1)} %add_add_fusion), channel_id=1, source_target_pairs={{0,32},{1,3},{2,34},{3,1},{4,36},{5,7},{6,38},{7,5},{8,40},{9,11},... | collective-permute-start | bytes 688136 | tf_op jit(solution)/shard_map/ppermute | solution.py:387
  86.4 7.4 %collective-permute-start.22 = (bf16[448,256]{1,0:T(8,128)(2,1)S(1)}, bf16[448,256]{1,0:T(8,128)(2,1)S(1)}, u32[]{:S(2)}, u32[]{:S(2)}) collective-permute-start(bf16[448,256]{1,0:T(8,128)(2,1)S(1)} %add_add_fusion), channel_id=1, source_target_pairs={{0,96},{1,7},{2,98},{3,5},{4,100},{5,3},{6,102},{7,1},{8,104},{9,1... | collective-permute-start | bytes 688136 | tf_op jit(solution)/shard_map/ppermute | solution.py:387
  93.9 4.7 %collective-permute-start.23 = (bf16[448,256]{1,0:T(8,128)(2,1)S(1)}, bf16[448,256]{1,0:T(8,128)(2,1)S(1)}, u32[]{:S(2)}, u32[]{:S(2)}) collective-permute-start(bf16[448,256]{1,0:T(8,128)(2,1)S(1)} %add_convert_fusion.mine), channel_id=1, source_target_pairs={{0,1},{1,0},{2,3},{3,2},{4,5},{5,4},{6,7},{7,6},{8,9},{9,8},{10,11... | collective-permute-start | bytes 688136 | tf_op jit(solution)/shard_map/ppermute | solution.py:387
  (11 other events, 71.4 us)

commit v5 on v4

--- a/solution.py
+++ b/solution.py
@@ -18,7 +18,10 @@
 HS = HEADS * SLICES
 ROWS = B_DEV * BLOCK
 PAY1 = 640
-PAY2 = 896
+PAY2 = 800
+ORDER = (1, 2, 3)
+FT = 512
+SUB = BLOCK // FT
 BF = jnp.bfloat16
 F32 = jnp.float32
 HIGH = lax.Precision.HIGH
@@ -35,6 +38,10 @@
 
 def dot_high(a, b, dims=NN):
     return lax.dot_general(a, b, dims, precision=HIGH, preferred_element_type=F32)
+
+
+def dot_full(a, b):
+    return lax.dot_general(a, b, NN, precision=lax.Precision.HIGHEST, preferred_element_type=F32)
 
 
 def head_mask(rows):
@@ -70,7 +77,8 @@
     top = jnp.max(powers, axis=1, keepdims=True)
     e = jnp.exp2(powers - top)
     prob = e * (1.0 / jnp.sum(e, axis=1, keepdims=True))
-    return temper, inv, prob
+    raw_top = top[:, 0] * (scale * math.log(2.0))
+    return temper, inv, raw_top, prob
 
 
 def split_halves(core, full, send, keep):
@@ -101,15 +109,16 @@
         full[half:] = mine[...].astype(full.dtype)
 
 
-def pick_kernel(rank, counts, inner, outer, inner_out, outer_out):
+def pick_kernel(rank, counts, table, inner, outer, sel, inner_out, outer_out):
     inner_out[...] = inner[...]
     outer_out[...] = outer[...]
 
-
-def prep_kernel(
-    rank, counts, table, cot, wout, wf, wm, ws, wt, attw,
-    sel, dmix, wfmt, bd, bdt, wcol, watt,
-):
+    @pl.when(pl.program_id(0) == 0)
+    def _():
+        place_blocks(rank, counts, table, sel)
+
+
+def place_blocks(rank, counts, table, sel):
     here = rank[0]
     found, own = [], []
     for t in range(B_DEV):
@@ -131,16 +140,15 @@
         sel[1, t] = jnp.clip(place, 0, HALF - 1)
         sel[2, t] = found[t]
 
+
+def prep_kernel(cot, wout, wf, wm, ws, wt, dmix, wfmt, bd):
     dmix[...] = dot(cot[...], wout[...], NT).astype(BF)
     wfmt[:C] = wf[...].T
     wfmt[C:] = wm[...].T
-    lane_in = lax.broadcasted_iota(jnp.int32, (HEAD, C), 1) % HEAD
-    spread = (lax.broadcasted_iota(jnp.int32, (HEAD, C), 0) == lane_in).astype(F32)
+    spread = spread_matrix()
     slice_rows = dot(ws[...], spread.astype(BF), TN)
-    slice_bd = spread_heads(slice_rows)
-    bd[:HS] = slice_bd.astype(BF)
-    bdt[...] = slice_bd.T.astype(BF)
-    temper = dot_high(wt[...], spread)
+    bd[:HS] = spread_heads(slice_rows).astype(BF)
+    temper = dot_full(wt[...], spread)
     hi = temper.astype(BF).astype(F32)
     middle = (temper - hi).astype(BF).astype(F32)
     low = temper - hi - middle
@@ -148,29 +156,42 @@
     own_head = row == lax.broadcasted_iota(jnp.int32, (8, C), 1) // HEAD
     parts = [jnp.where(own_head, part, 0.0) for part in (hi, middle, low)]
     bd[HS:] = jnp.concatenate(parts + [jnp.zeros((8, C), F32)], axis=0).astype(BF)
+
+
+def spread_matrix():
+    lane_in = lax.broadcasted_iota(jnp.int32, (HEAD, C), 1) % HEAD
+    return (lax.broadcasted_iota(jnp.int32, (HEAD, C), 0) == lane_in).astype(F32)
+
+
+def prep_back_kernel(bd, wt, attw, bdt, wcol, watt):
+    spread = spread_matrix()
+    bdt[:C] = bd[...].astype(F32).T.astype(BF)
+    row = lax.broadcasted_iota(jnp.int32, (16, HS), 0)
+    bdt[C:] = (row == lax.broadcasted_iota(jnp.int32, (16, HS), 1) // SLICES).astype(BF)
+    temper = dot_full(wt[...], spread)
     rows = lax.broadcasted_iota(jnp.int32, (C, C), 0)
     cols = lax.broadcasted_iota(jnp.int32, (C, C), 1)
     wcol[...] = jnp.sum(jnp.where(rows == cols, temper, 0.0), axis=1, keepdims=True)
     same_head = rows // HEAD == cols // HEAD
     for i in range(3):
-        wide = dot_high(attw[i], spread)
+        wide = dot_full(attw[i], spread)
         watt[i] = jnp.where(same_head, jnp.concatenate([wide] * HEADS, axis=0), 0.0)
 
 
 def first_tile(t, core):
-    return t + HALF * (1 - core[0])
+    return t + HALF * SUB * (1 - core[0])
 
 
 def second_tile(t, core):
-    return t + HALF * core[0]
+    return t + HALF * SUB * core[0]
 
 
 def front_first(sel, core, own, other, dmix, gain, wf, wmt, bd, *outs):
     *arrays, pay, acc, den = outs
     tile = first_tile(pl.program_id(0), core)
-    front_tile(sel[2, tile], own, other, dmix, gain, wf, wmt, bd, *arrays, acc, den)
-
-    @pl.when(pl.program_id(0) == HALF - 1)
+    front_tile(sel[2, tile // SUB], own, other, dmix, gain, wf, wmt, bd, *arrays, acc, den)
+
+    @pl.when(pl.program_id(0) == HALF * SUB - 1)
     def _():
         fold_sums(acc, den, pay)
 
@@ -178,9 +199,9 @@
 def front_second(sel, core, own, other, dmix, gain, wf, wmt, bd, pay_first, *rest):
     *arrays, send, keep, acc, den, pay = rest[6:]
     tile = second_tile(pl.program_id(0), core)
-    front_tile(sel[2, tile], own, other, dmix, gain, wf, wmt, bd, *arrays, acc, den)
-
-    @pl.when(pl.program_id(0) == HALF - 1)
+    front_tile(sel[2, tile // SUB], own, other, dmix, gain, wf, wmt, bd, *arrays, acc, den)
+
+    @pl.when(pl.program_id(0) == HALF * SUB - 1)
     def _():
         fold_sums(acc, den, pay)
         pay[...] += pay_first[...]
@@ -208,11 +229,12 @@
     mid_t = dot(wmt[...], normed, NT).astype(BF)
     feat_out[...] = feat
     mid_out[...] = mid_t
-    temper, inv, prob = slice_softmax(mid_t, bd[...])
-    prob_out[...] = prob.reshape(HS, BLOCK)
+    temper, inv, raw_top, prob = slice_softmax(mid_t, bd[...])
+    prob_out[...] = prob.reshape(HS, FT)
     aux[:HEADS] = inv
-    aux[HEADS:] = inv * jax.nn.sigmoid(temper)
-    weights = prob.reshape(HS, BLOCK).astype(BF)
+    aux[HEADS : 2 * HEADS] = inv * jax.nn.sigmoid(temper)
+    aux[2 * HEADS :] = raw_top
+    weights = prob.reshape(HS, FT).astype(BF)
 
     @pl.when(t == 0)
     def _():
@@ -223,7 +245,7 @@
     for i in range(2):
         both = jnp.concatenate([feat[:, i * G : (i + 1) * G], grad[:, i * G : (i + 1) * G]], axis=1)
         acc[i * GS : (i + 1) * GS] += dot(weights[i * GS : (i + 1) * GS], both)
-    den[...] += dot(weights, jnp.ones((BLOCK, 128), BF))
+    den[...] += dot(weights, jnp.ones((FT, 128), BF))
 
 
 def fold_sums(acc, den, pay):
@@ -238,6 +260,11 @@
     lane = lax.broadcasted_iota(jnp.int32, (HS, 128), 1)
     placed = jnp.where(row_head == lane, den[...], 0.0)
     pay[:, 2 * C :] = jnp.sum(placed.reshape(HEADS, SLICES, 128), axis=0)
+
+
+def packed_mask():
+    row = lax.broadcasted_iota(jnp.int32, (SLICES, C), 0)
+    return lax.broadcasted_iota(jnp.int32, (SLICES, C), 1) // HEAD == row % 8
 
 
 def attention_step(pay, watt, an, ant, dd, toks):
@@ -322,13 +349,14 @@
     dl = prob * (dw - jnp.sum(prob * dw, axis=1, keepdims=True))
     d_raw = (dl * inv[:, None, :]).reshape(HS, BLOCK).astype(BF)
     direct = dot(bdt[...], d_raw)
-    inner = (mid_t.astype(F32) * direct).reshape(HEADS, HEAD, BLOCK)
-    d_temper = -jnp.sum(inner, axis=1) * aux[HEADS:]
+    inner = (mid_t.astype(F32) * direct[:C]).reshape(HEADS, HEAD, BLOCK)
+    against_top = jnp.sum(inner, axis=1) - aux[2 * HEADS :] * direct[C : C + HEADS]
+    d_temper = -against_top * aux[HEADS : 2 * HEADS]
     low = dot(ant[0], weights[:GS]).astype(BF)
     high = dot(ant[1], weights[GS:]).astype(BF)
     mixed_df = jnp.concatenate([low[:G], high[:G], low[G:], high[G:]], axis=0)
     spread = jnp.broadcast_to(d_temper[:, None, :], (HEADS, HEAD, BLOCK)).reshape(C, BLOCK)
-    dm = (direct + spread * wcol[...]).astype(BF)
+    dm = (direct[:C] + spread * wcol[...]).astype(BF)
     res[: 2 * C] = mixed_df
     res[2 * C :] = dm
     normed_here = normed[...]
@@ -345,15 +373,19 @@
         grad_fm = gfm[...]
         gpay[: 2 * C] = grad_fm
         gpay[2 * C : 3 * C] = gout[...]
-        gpay[3 * C : 3 * C + SLICES] = fold_heads(gsl[:HS])
+        rows = lax.broadcasted_iota(jnp.int32, (C, C), 0)
+        cols = lax.broadcasted_iota(jnp.int32, (C, C), 1)
+        over_heads = (rows % HEAD == cols % HEAD).astype(F32)
+        packed = jnp.where(packed_mask(), dot_high(fold_heads(gsl[:HS]), over_heads), 0.0)
+        gpay[3 * C : 3 * C + 8] = jnp.sum(packed.reshape(8, 8, C), axis=1)
         grad_gain = jnp.sum(grad_fm * wfmt[...].astype(F32), axis=0, keepdims=True) / gain[...]
         both = gsl[HS : HS + 8] + gsl[HS + 8 :]
         row = lax.broadcasted_iota(jnp.int32, (8, C), 0)
         lane_head = lax.broadcasted_iota(jnp.int32, (8, C), 1) // HEAD
         temper_row = jnp.sum(jnp.where(row == lane_head, both, 0.0), axis=0, keepdims=True)
-        row = lax.broadcasted_iota(jnp.int32, (SLICES, C), 0)
+        row = lax.broadcasted_iota(jnp.int32, (PAY2 - 3 * C - 8, C), 0)
         tail = jnp.where(row == 0, grad_gain, jnp.where(row == 1, temper_row, 0.0))
-        gpay[3 * C + SLICES :] = tail
+        gpay[3 * C + 8 :] = tail
         split_halves(core[0], gpay, send, keep)
 
 
@@ -376,8 +408,10 @@
     gout[...] = full[2 * C : 3 * C]
     lane_in = lax.broadcasted_iota(jnp.int32, (C, HEAD), 0) % HEAD
     fold = (lane_in == lax.broadcasted_iota(jnp.int32, (C, HEAD), 1)).astype(F32)
-    gslice[...] = dot_high(fold, full[3 * C : 3 * C + SLICES], (((0,), (1,)), ((), ())))
-    tail = full[3 * C + SLICES : 3 * C + SLICES + 8]
+    rows = jnp.broadcast_to(full[3 * C : 3 * C + 8].reshape(8, 1, C), (8, 8, C))
+    spread = jnp.where(packed_mask(), rows.reshape(SLICES, C), 0.0)
+    gslice[...] = dot_high(fold, spread, (((0,), (1,)), ((), ())))
+    tail = full[3 * C + 8 : 3 * C + 16]
     gtemper[...] = dot_high(tail, fold)[1:2]
     ggain[...] = tail[0:1]
 
@@ -389,10 +423,8 @@
 
 def quad_sum(x, even, odd, wire):
     w = x.astype(wire)
-    a = swap(w, even, odd).astype(F32)
-    b = swap(w, 2 * even, 2 * odd).astype(F32)
-    c = swap(w, 3 * even, 3 * odd).astype(F32)
-    return (w.astype(F32) + a) + (b + c)
+    got = {k: swap(w, k * even, k * odd).astype(F32) for k in ORDER}
+    return (w.astype(F32) + got[1]) + (got[2] + got[3])
 
 
 def sum_over_chips(send, keep, wire, beside=()):
@@ -439,65 +471,58 @@
     def tail_slot(t, rank, counts):
         return jnp.maximum(counts[rank[0]] - HALF, 0) + t
 
-    def inner_slot(t, rank, counts):
+    def inner_slot(t, rank, counts, table):
         return (jnp.where(rank[0] % 2 == 0, tail_slot(t, rank, counts), t), 0)
 
-    def outer_slot(t, rank, counts):
+    def outer_slot(t, rank, counts, table):
         return (jnp.where(rank[0] % 2 == 0, t, tail_slot(t, rank, counts)), 0)
 
-    inner, outer = pl.pallas_call(
+    sel, inner, outer = pl.pallas_call(
         pick_kernel,
         grid_spec=pltpu.PrefetchScalarGridSpec(
-            num_scalar_prefetch=2,
+            num_scalar_prefetch=3,
             grid=(HALF,),
             in_specs=[pl.BlockSpec((BLOCK, C), inner_slot), pl.BlockSpec((BLOCK, C), outer_slot)],
-            out_specs=[rows_spec(C)] * 2,
+            out_specs=[SCALARS] + [rows_spec(C)] * 2,
         ),
-        out_shape=[edge, edge],
+        out_shape=[jax.ShapeDtypeStruct((3, B_DEV), jnp.int32), edge, edge],
         name="pick",
-    )(rank, block_counts, loader_points, loader_points)
+    )(rank, block_counts, dest_table, loader_points, loader_points)
     got_inner, got_outer = neighbour_blocks(inner, outer)
     gain = norm_gain.reshape(1, C)
-    sel, d_mixed, wfmt, bd, bdt, wcol, watt = pl.pallas_call(
+    d_mixed, wfmt, bd = pl.pallas_call(
         prep_kernel,
         grid=(1,),
-        in_specs=[SCALARS] * 3
-        + [
-            whole((ROWS, C)),
-            whole((C, C)),
-            whole((C, C)),
-            whole((C, C)),
-            whole((HEAD, SLICES)),
-            whole((1, HEAD)),
-            whole((3, HEAD, HEAD)),
-        ],
-        out_specs=[
-            SCALARS,
-            whole((ROWS, C)),
-            whole((2 * C, C)),
-            whole((HS + 32, C)),
-            whole((C, HS)),
-            whole((C, 1)),
-            whole((3, C, C)),
-        ],
+        in_specs=[whole((ROWS, C))] + [whole((C, C))] * 3 + [whole((HEAD, SLICES)), whole((1, HEAD))],
+        out_specs=[whole((ROWS, C)), whole((2 * C, C)), whole((HS + 32, C))],
         out_shape=[
-            jax.ShapeDtypeStruct((3, B_DEV), jnp.int32),
             jax.ShapeDtypeStruct((ROWS, C), BF),
             jax.ShapeDtypeStruct((2 * C, C), BF),
             jax.ShapeDtypeStruct((HS + 32, C), BF),
-            jax.ShapeDtypeStruct((C, HS), BF),
-            jax.ShapeDtypeStruct((C, 1), F32),
-            jax.ShapeDtypeStruct((3, C, C), F32),
         ],
         compiler_params=PARAMS,
         cost_estimate=pl.CostEstimate(
             flops=2 * ROWS * C * C, bytes_accessed=4 * 1024 * 1024, transcendentals=0
         ),
         name="prep",
-    )(
-        rank, block_counts, dest_table, cotangent, w_output, w_feature, w_middle, w_slice,
-        w_temper.reshape(1, HEAD), attend_weight,
-    )
+    )(cotangent, w_output, w_feature, w_middle, w_slice, w_temper.reshape(1, HEAD))
+
+    back_weights = pl.pallas_call(
+        prep_back_kernel,
+        grid=(1,),
+        in_specs=[whole((HS, C)), whole((1, HEAD)), whole((3, HEAD, HEAD))],
+        out_specs=[whole((C + 16, HS)), whole((C, 1)), whole((3, C, C))],
+        out_shape=[
+            jax.ShapeDtypeStruct((C + 16, HS), BF),
+            jax.ShapeDtypeStruct((C, 1), F32),
+            jax.ShapeDtypeStruct((3, C, C), F32),
+        ],
+        compiler_params=PARAMS,
+        cost_estimate=pl.CostEstimate(
+            flops=C * C * C, bytes_accessed=2 * 1024 * 1024, transcendentals=0
+        ),
+        name="prep_back",
+    )(bd, w_temper.reshape(1, HEAD), attend_weight)
 
     wide = jax.ShapeDtypeStruct((ROWS, C), BF)
     half1 = jax.ShapeDtypeStruct((SLICES // 2, PAY1), F32)
@@ -505,22 +530,22 @@
     arrays = [wide] * 3 + [
         jax.ShapeDtypeStruct((C, ROWS), BF),
         jax.ShapeDtypeStruct((HS, ROWS), F32),
-        jax.ShapeDtypeStruct((2 * HEADS, ROWS), F32),
+        jax.ShapeDtypeStruct((3 * HEADS, ROWS), F32),
     ]
 
     def front_specs(tile):
-        rows = pl.BlockSpec((BLOCK, C), lambda t, s, c: (tile(t, c), 0))
-        cols = lambda n: pl.BlockSpec((n, BLOCK), lambda t, s, c: (0, tile(t, c)))
+        rows = pl.BlockSpec((FT, C), lambda t, s, c: (tile(t, c), 0))
+        cols = lambda n: pl.BlockSpec((n, FT), lambda t, s, c: (0, tile(t, c)))
         ins = [
-            pl.BlockSpec((BLOCK, C), lambda t, s, c: (s[0, tile(t, c)], 0)),
-            pl.BlockSpec((BLOCK, C), lambda t, s, c: (s[1, tile(t, c)], 0)),
+            pl.BlockSpec((FT, C), lambda t, s, c: (s[0, tile(t, c) // SUB] * SUB + t % SUB, 0)),
+            pl.BlockSpec((FT, C), lambda t, s, c: (s[1, tile(t, c) // SUB] * SUB + t % SUB, 0)),
             rows,
             whole((1, C)),
             whole((C, C)),
             pl.BlockSpec((C, C), lambda t, s, c: (1, 0)),
             whole((HS + 32, C)),
         ]
-        return ins, [rows] * 3 + [cols(C), cols(HS), cols(2 * HEADS)]
+        return ins, [rows] * 3 + [cols(C), cols(HS), cols(3 * HEADS)]
 
     sums = [pltpu.VMEM((HS, C), F32), pltpu.VMEM((HS, 128), F32)]
     ins, outs = front_specs(first_tile)
@@ -528,7 +553,7 @@
         front_first,
         grid_spec=pltpu.PrefetchScalarGridSpec(
             num_scalar_prefetch=2,
-            grid=(HALF,),
+            grid=(HALF * SUB,),
             in_specs=ins,
             out_specs=outs + [whole((SLICES, PAY1))],
             scratch_shapes=sums,
@@ -540,12 +565,13 @@
         ),
         name="front_first",
     )(sel, core, loader_points, got_inner, d_mixed, gain, w_feature, wfmt, bd)
+    pay, (bdt, wcol, watt) = lax.optimization_barrier((pay, back_weights))
     ins, outs = front_specs(second_tile)
     *first, send, keep = pl.pallas_call(
         front_second,
         grid_spec=pltpu.PrefetchScalarGridSpec(
             num_scalar_prefetch=2,
-            grid=(HALF,),
+            grid=(HALF * SUB,),
             in_specs=ins + [whole((SLICES, PAY1))] + [HBM] * 6,
             out_specs=outs + [whole((SLICES // 2, PAY1))] * 2,
             scratch_shapes=sums + [pltpu.VMEM((SLICES, PAY1), F32)],
@@ -566,12 +592,12 @@
         + [whole((SLICES // 2, PAY1))] * 2
         + [whole((3, C, C))]
         + [rows_spec(C)] * 2
-        + [cols_of(C), cols_of(HS), cols_of(2 * HEADS)]
+        + [cols_of(C), cols_of(HS), cols_of(3 * HEADS)]
         + [rows_spec(C)] * 2
         + [
             whole((1, C)),
             whole((2 * C, C)),
-            whole((C, HS)),
+            whole((C + 16, HS)),
             whole((C, 1)),
         ],
         out_specs=[

time: 99.9 us -> 98.7 us (0.988)
    pallas_call x1 -> x2, Pallas kernels: 1.82 us -> 0.79 us  [the longest x1 0.51 us: per_device(): pl.pallas_call(prep_kernel, grid=(1,), in_specs=[whole((ROWS, C))] + [who...]
    unnamed x22 -> x20, local copies, waits for them, and re-layouts: 2.14 us -> 1.5 us
  transfers between devices with their start and end apart: 24 -> 24, of which waited for: 18 -> 19; matrix products, arithmetic and copies ran while one was open for 0% -> 0% of each run, Pallas kernels for 12% -> 11%
where the time goes in v5:
time: 98.7 us; the launch traced here: 98.5 us
  starting transfers between devices  37.9 us (38%)
  Pallas kernels  29.2 us (30%)
  waiting for transfers between devices  28.6 us (29%)
  local copies, waits for them, and re-layouts  1.5 us (2%)
    ppermute x23, starting transfers between devices, swap(): lax.ppermute(array, 'pts', [(i, i ^ (odd if i % 2 else even)) for i in ra...  34.8 us
    ppermute x23, waiting for transfers between devices, swap(): lax.ppermute(array, 'pts', [(i, i ^ (odd if i % 2 else even)) for i in ra...  28 us
    pallas_call x1, Pallas kernels, per_device(): pl.pallas_call(back_kernel, grid=(B_DEV,), in_specs=[SCALARS] + [whole((S...  9.45 us
    pallas_call x1, Pallas kernels, per_device(): pl.pallas_call(front_second, grid_spec=pltpu.PrefetchScalarGridSpec(num_s...  4.66 us
    pallas_call x1, Pallas kernels, per_device(): pl.pallas_call(front_first, grid_spec=pltpu.PrefetchScalarGridSpec(num_sc...  4.62 us
    pallas_call x1, Pallas kernels, per_device(): pl.pallas_call(out_kernel, grid=(B_DEV,), in_specs=[rows_spec(C), rows_sp...  3.69 us
    pallas_call x1, Pallas kernels, per_device(): pl.pallas_call(pick_kernel, grid_spec=pltpu.PrefetchScalarGridSpec(num_sc...  3.11 us
    ppermute x1, starting transfers between devices, neighbour_blocks(): got_outer = lax.ppermute(outer, 'pts', edges + [(j, i) for i, j in edges])  3.08 us
  transfers between devices with their start and end apart: 24, of which 19 were waited for; matrix products, arithmetic and copies ran while one was open for 0% of the time, Pallas kernels for 11%

profile of v5, /device:TPU:1, one launch (start us, length us, event | category | flops | bytes accessed | tf_op | source)
XLA Modules:
  0.0 98.5 jit_solution(13833703945422990938)
XLA Ops:
  0.7 3.1 %pick.1 = (s32[3,4]{1,0:T(4,128)}, bf16[1024,256]{1,0:T(8,128)(2,1)}, bf16[1024,256]{1,0:T(8,128)(2,1)}) custom-call(s32[1]{0:T(128)} %bitcast.rank, s32[128]{0:T(128)} %counts.1, s32[8]{0:T(128)} %table.1, bf16[4096,256]{1,0:T(8,128)(2,1)} %own.3, bf16[4096,256]{1,0:T(8,128)(2,1)} %own.3), custom_call_target="tpu_custom_call" | custom-call | tf_op jit(solution)/shard_map/pick/pallas_call | solution.py:480
  3.8 1.4 %collective-permute-start.1 = (bf16[1024,256]{1,0:T(8,128)(2,1)}, bf16[1024,256]{1,0:T(8,128)(2,1)S(1)}, u32[]{:S(2)}, u32[]{:S(2)}) collective-permute-start(bf16[1024,256]{1,0:T(8,128)(2,1)} %get-tuple-element.59), channel_id=1, source_target_pairs={{0,1},{1,0},{2,3},{3,2},{4,5},{5,4},{6,7},{7,6},{8,9},{9,8},{10,11... | collective-permute-start | bytes 1572872 | tf_op jit(solution)/shard_map/ppermute | solution.py:421
  5.3 3.1 %collective-permute-start = (bf16[1024,256]{1,0:T(8,128)(2,1)}, bf16[1024,256]{1,0:T(8,128)(2,1)S(1)}, u32[]{:S(2)}, u32[]{:S(2)}) collective-permute-start(bf16[1024,256]{1,0:T(8,128)(2,1)} %get-tuple-element.55), channel_id=1, source_target_pairs={{1,2},{3,4},{5,6},{7,8},{9,10},{11,12},{13,14},{15,16},{17,18},{19... | collective-permute-start | bytes 1572872 | tf_op jit(solution)/shard_map/ppermute | solution.py:446
  10.7 4.6 %front_first.1 = (bf16[2048,256]{1,0:T(8,128)(2,1)S(1)}, bf16[2048,256]{1,0:T(8,128)(2,1)S(1)}, bf16[2048,256]{1,0:T(8,128)(2,1)S(1)}, bf16[256,2048]{1,0:T(8,12...) custom-call(s32[3,4]{1,0:T(4,128)S(1)} %copy-done.8, s32[1]{0:T(128)S(6)} %rem.18.core, ...), custom_call_target="tpu_custom_call" | custom-call | flops 805306368 | bytes 6291456 | tf_op jit(solution)/shard_map/front_first/pallas_call | solution.py:552
  16.0 4.7 %front_second.1 = (bf16[2048,256]{1,0:T(8,128)(2,1)S(1)}, bf16[2048,256]{1,0:T(8,128)(2,1)S(1)}, bf16[2048,256]{1,0:T(8,128)(2,1)S(1)}, bf16[256,2048]{1,0:T(8,1...) custom-call(s32[3,4]{1,0:T(4,128)S(1)} %copy-done.8, ...), custom_call_target="tpu_custom_call", output_to_operand_aliasing={{0}: (10, {}), {1}: (11, {}), {2}: (12, {}), {3}: (13, {}),... | custom-call | tf_op jit(solution)/shard_map/front_second/pallas_call | solution.py:570
  22.0 5.7 %collective-permute-start.5 = (f32[32,640]{1,0:T(8,128)S(1)}, f32[32,640]{1,0:T(8,128)S(1)}, u32[]{:S(2)}, u32[]{:S(2)}) collective-permute-start(f32[32,640]{1,0:T(8,128)S(1)} %add.60), channel_id=1, source_target_pairs={{0,6},{1,25},{2,4},{3,27},{4,2},{5,29},{6,0},{7,31},{8,14},{9,17},... | collective-permute-start | bytes 245768 | tf_op jit(solution)/shard_map/ppermute | solution.py:421
  28.4 1.6 %collective-permute-done.5 = f32[32,640]{1,0:T(8,128)S(1)} collective-permute-done((f32[32,640]{1,0:T(8,128)S(1)}, f32[32,640]{1,0:T(8,128)S(1)}, u32[]{:S(2)}, u32[]{:S(2)}) %collective-permute-start.5) | collective-permute-done | bytes 81952 | tf_op jit(solution)/shard_map/ppermute | solution.py:421
  30.0 2.8 %collective-permute-done.4 = f32[32,640]{1,0:T(8,128)S(1)} collective-permute-done((f32[32,640]{1,0:T(8,128)S(1)}, f32[32,640]{1,0:T(8,128)S(1)}, u32[]{:S(2)}, u32[]{:S(2)}) %collective-permute-start.4) | collective-permute-done | bytes 81952 | tf_op jit(solution)/shard_map/ppermute | solution.py:421
  32.8 2.9 %collective-permute-start.8 = (f32[32,640]{1,0:T(8,128)S(1)}, f32[32,640]{1,0:T(8,128)S(1)}, u32[]{:S(2)}, u32[]{:S(2)}) collective-permute-start(f32[32,640]{1,0:T(8,128)S(1)} %add_add_fusion.4), channel_id=1, source_target_pairs={{0,24},{1,97},{2,26},{3,99},{4,28},{5,101},{6,30},{7,103},{8,16},{... | collective-permute-start | bytes 245768 | tf_op jit(solution)/shard_map/ppermute | solution.py:421
  36.4 1.6 %collective-permute-done.8 = f32[32,640]{1,0:T(8,128)S(1)} collective-permute-done((f32[32,640]{1,0:T(8,128)S(1)}, f32[32,640]{1,0:T(8,128)S(1)}, u32[]{:S(2)}, u32[]{:S(2)}) %collective-permute-start.8) | collective-permute-done | bytes 81952 | tf_op jit(solution)/shard_map/ppermute | solution.py:421
  38.0 2.5 %collective-permute-done.7 = f32[32,640]{1,0:T(8,128)S(1)} collective-permute-done((f32[32,640]{1,0:T(8,128)S(1)}, f32[32,640]{1,0:T(8,128)S(1)}, u32[]{:S(2)}, u32[]{:S(2)}) %collective-permute-start.7) | collective-permute-done | bytes 81952 | tf_op jit(solution)/shard_map/ppermute | solution.py:421
  40.5 3.8 %collective-permute-start.11 = (f32[32,640]{1,0:T(8,128)S(1)}, f32[32,640]{1,0:T(8,128)S(1)}, u32[]{:S(2)}, u32[]{:S(2)}) collective-permute-start(f32[32,640]{1,0:T(8,128)S(1)} %add_add_fusion.3), channel_id=1, source_target_pairs={{0,96},{1,7},{2,98},{3,5},{4,100},{5,3},{6,102},{7,1},{8,104},{9,1... | collective-permute-start | bytes 245768 | tf_op jit(solution)/shard_map/ppermute | solution.py:421
  45.0 1.6 %collective-permute-done.11 = f32[32,640]{1,0:T(8,128)S(1)} collective-permute-done((f32[32,640]{1,0:T(8,128)S(1)}, f32[32,640]{1,0:T(8,128)S(1)}, u32[]{:S(2)}, u32[]{:S(2)}) %collective-permute-start.11) | collective-permute-done | bytes 81952 | tf_op jit(solution)/shard_map/ppermute | solution.py:421
  46.6 2.5 %collective-permute-done.10 = f32[32,640]{1,0:T(8,128)S(1)} collective-permute-done((f32[32,640]{1,0:T(8,128)S(1)}, f32[32,640]{1,0:T(8,128)S(1)}, u32[]{:S(2)}, u32[]{:S(2)}) %collective-permute-start.10) | collective-permute-done | bytes 81952 | tf_op jit(solution)/shard_map/ppermute | solution.py:421
  49.1 4.7 %collective-permute-start.12 = (f32[32,640]{1,0:T(8,128)S(1)}, f32[32,640]{1,0:T(8,128)S(1)}, u32[]{:S(2)}, u32[]{:S(2)}) collective-permute-start(f32[32,640]{1,0:T(8,128)S(1)} %add_add_fusion.2.mine), channel_id=1, source_target_pairs={{0,1},{1,0},{2,3},{3,2},{4,5},{5,4},{6,7},{7,6},{8,9},{9,8},{10,11... | collective-permute-start | bytes 245768 | tf_op jit(solution)/shard_map/ppermute | solution.py:421
  54.7 9.4 %back.1 = (bf16[768,2048]{1,0:T(8,128)(2,1)S(1)}, bf16[400,256]{1,0:T(8,128)(2,1)S(1)}, f32[400,256]{1,0:T(8,128)S(1)}, f32[4,64,256]{2,1,0:T(8,128)S(1)}) custom-call(s32[1]{0:T(128)S(6)} %rem.18.core, f32[32,640]{1,0:T(8,128)S(1)} %add_add_fusion.2.mine, f32[32,640]{1,0:T(8,128)S(1)} %collective-permute-done.12.other, ...), custom_call_target="tpu_custom_call" | custom-call | tf_op jit(solution)/shard_map/back/pallas_call | solution.py:588
  69.1 3.7 %outputs.1 = (bf16[2048,256]{1,0:T(8,128)(2,1)}, bf16[2048,256]{1,0:T(8,128)(2,1)}) custom-call(bf16[2048,256]{1,0:T(8,128)(2,1)S(1)} %get-tuple-element.83.ptsb, bf16[2048,256]{1,0:T(8,128)(2,1)S(1)} %copy-done.1, bf16[768,2048]{1,0:T(8,128)(2,1)S(1)} %get-tuple-element.84.res, f32[1,256]{1,0:T(1,128)S(1)} %bitcast.8, ...), custom_call_target="tpu_custom_call" | custom-call | flops 805306368 | bytes 7340032 | tf_op jit(solution)/shard_map/outputs/pallas_call | solution.py:632
  74.9 2.3 %collective-permute-start.18 = (bf16[400,256]{1,0:T(8,128)(2,1)S(1)}, bf16[400,256]{1,0:T(8,128)(2,1)S(1)}, u32[]{:S(2)}, u32[]{:S(2)}) collective-permute-start(bf16[400,256]{1,0:T(8,128)(2,1)S(1)} %add_add_fusion.1), channel_id=1, source_target_pairs={{0,16},{1,65},{2,18},{3,67},{4,20},{5,69},{6,22},{7,71},{8,24},{9,... | collective-permute-start | bytes 614408 | tf_op jit(solution)/shard_map/ppermute | solution.py:421
  78.2 1.7 %attend_grads.1 = f32[3,32,32]{2,1,0:T(8,128)} custom-call(f32[4,64,256]{2,1,0:T(8,128)S(1)} %get-tuple-element.90.toks), custom_call_target="tpu_custom_call" | custom-call | tf_op jit(solution)/shard_map/attend_grads/pallas_call | solution.py:652
  81.4 1.7 %collective-permute-done.17 = bf16[400,256]{1,0:T(8,128)(2,1)S(1)} collective-permute-done((bf16[400,256]{1,0:T(8,128)(2,1)S(1)}, bf16[400,256]{1,0:T(8,128)(2,1)S(1)}, u32[]{:S(2)}, u32[]{:S(2)}) %collective-permute-start.17) | collective-permute-done | bytes 204832 | tf_op jit(solution)/shard_map/ppermute | solution.py:421
  83.7 1.8 %collective-permute-start.21 = (bf16[400,256]{1,0:T(8,128)(2,1)S(1)}, bf16[400,256]{1,0:T(8,128)(2,1)S(1)}, u32[]{:S(2)}, u32[]{:S(2)}) collective-permute-start(bf16[400,256]{1,0:T(8,128)(2,1)S(1)} %add_add_fusion), channel_id=1, source_target_pairs={{0,64},{1,5},{2,66},{3,7},{4,68},{5,1},{6,70},{7,3},{8,72},{9,13},... | collective-permute-start | bytes 614408 | tf_op jit(solution)/shard_map/ppermute | solution.py:421
  85.5 1.5 %collective-permute-start.22 = (bf16[400,256]{1,0:T(8,128)(2,1)S(1)}, bf16[400,256]{1,0:T(8,128)(2,1)S(1)}, u32[]{:S(2)}, u32[]{:S(2)}) collective-permute-start(bf16[400,256]{1,0:T(8,128)(2,1)S(1)} %add_add_fusion), channel_id=1, source_target_pairs={{0,96},{1,7},{2,98},{3,5},{4,100},{5,3},{6,102},{7,1},{8,104},{9,1... | collective-permute-start | bytes 614408 | tf_op jit(solution)/shard_map/ppermute | solution.py:421
  87.0 2.9 %collective-permute-done.21 = bf16[400,256]{1,0:T(8,128)(2,1)S(1)} collective-permute-done((bf16[400,256]{1,0:T(8,128)(2,1)S(1)}, bf16[400,256]{1,0:T(8,128)(2,1)S(1)}, u32[]{:S(2)}, u32[]{:S(2)}) %collective-permute-start.21) | collective-permute-done | bytes 204832 | tf_op jit(solution)/shard_map/ppermute | solution.py:421
  92.5 3.8 %collective-permute-start.23 = (bf16[400,256]{1,0:T(8,128)(2,1)S(1)}, bf16[400,256]{1,0:T(8,128)(2,1)S(1)}, u32[]{:S(2)}, u32[]{:S(2)}) collective-permute-start(bf16[400,256]{1,0:T(8,128)(2,1)S(1)} %add_convert_fusion.mine), channel_id=1, source_target_pairs={{0,1},{1,0},{2,3},{3,2},{4,5},{5,4},{6,7},{7,6},{8,9},{9,8},{10,11... | collective-permute-start | bytes 614408 | tf_op jit(solution)/shard_map/ppermute | solution.py:421
  (61 shorter events, 22.0 us)
Async XLA Ops:
  3.8 6.2 %collective-permute-start.1 = (bf16[1024,256]{1,0:T(8,128)(2,1)}, bf16[1024,256]{1,0:T(8,128)(2,1)S(1)}, u32[]{:S(2)}, u32[]{:S(2)}) collective-permute-start(bf16[1024,256]{1,0:T(8,128)(2,1)} %get-tuple-element.59), channel_id=1, source_target_pairs={{0,1},{1,0},{2,3},{3,2},{4,5},{5,4},{6,7},{7,6},{8,9},{9,8},{10,11... | collective-permute-start | bytes 1572872 | tf_op jit(solution)/shard_map/ppermute | solution.py:421
  5.3 10.7 %collective-permute-start = (bf16[1024,256]{1,0:T(8,128)(2,1)}, bf16[1024,256]{1,0:T(8,128)(2,1)S(1)}, u32[]{:S(2)}, u32[]{:S(2)}) collective-permute-start(bf16[1024,256]{1,0:T(8,128)(2,1)} %get-tuple-element.55), channel_id=1, source_target_pairs={{1,2},{3,4},{5,6},{7,8},{9,10},{11,12},{13,14},{15,16},{17,18},{19... | collective-permute-start | bytes 1572872 | tf_op jit(solution)/shard_map/ppermute | solution.py:446
  20.6 1.4 %collective-permute-start.2 = (f32[32,640]{1,0:T(8,128)S(1)}, f32[32,640]{1,0:T(8,128)S(1)}, u32[]{:S(2)}, u32[]{:S(2)}) collective-permute-start(f32[32,640]{1,0:T(8,128)S(1)} %get-tuple-element.72), channel_id=1, source_target_pairs={{0,1},{1,0},{2,3},{3,2},{4,5},{5,4},{6,7},{7,6},{8,9},{9,8},{10,11... | collective-permute-start | bytes 245768 | tf_op jit(solution)/shard_map/ppermute | solution.py:421
  22.0 7.9 %collective-permute-start.5 = (f32[32,640]{1,0:T(8,128)S(1)}, f32[32,640]{1,0:T(8,128)S(1)}, u32[]{:S(2)}, u32[]{:S(2)}) collective-permute-start(f32[32,640]{1,0:T(8,128)S(1)} %add.60), channel_id=1, source_target_pairs={{0,6},{1,25},{2,4},{3,27},{4,2},{5,29},{6,0},{7,31},{8,14},{9,17},... | collective-permute-start | bytes 245768 | tf_op jit(solution)/shard_map/ppermute | solution.py:421
  27.7 5.1 %collective-permute-start.4 = (f32[32,640]{1,0:T(8,128)S(1)}, f32[32,640]{1,0:T(8,128)S(1)}, u32[]{:S(2)}, u32[]{:S(2)}) collective-permute-start(f32[32,640]{1,0:T(8,128)S(1)} %add.60), channel_id=1, source_target_pairs={{0,4},{1,17},{2,6},{3,19},{4,0},{5,21},{6,2},{7,23},{8,12},{9,25},... | collective-permute-start | bytes 245768 | tf_op jit(solution)/shard_map/ppermute | solution.py:421
  27.7 5.1 %collective-permute-start.3 = (f32[32,640]{1,0:T(8,128)S(1)}, f32[32,640]{1,0:T(8,128)S(1)}, u32[]{:S(2)}, u32[]{:S(2)}) collective-permute-start(f32[32,640]{1,0:T(8,128)S(1)} %add.60), channel_id=1, source_target_pairs={{0,2},{1,9},{2,0},{3,11},{4,6},{5,13},{6,4},{7,15},{8,10},{9,1},{1... | collective-permute-start | bytes 245768 | tf_op jit(solution)/shard_map/ppermute | solution.py:421
  32.8 5.2 %collective-permute-start.8 = (f32[32,640]{1,0:T(8,128)S(1)}, f32[32,640]{1,0:T(8,128)S(1)}, u32[]{:S(2)}, u32[]{:S(2)}) collective-permute-start(f32[32,640]{1,0:T(8,128)S(1)} %add_add_fusion.4), channel_id=1, source_target_pairs={{0,24},{1,97},{2,26},{3,99},{4,28},{5,101},{6,30},{7,103},{8,16},{... | collective-permute-start | bytes 245768 | tf_op jit(solution)/shard_map/ppermute | solution.py:421
  35.7 4.8 %collective-permute-start.7 = (f32[32,640]{1,0:T(8,128)S(1)}, f32[32,640]{1,0:T(8,128)S(1)}, u32[]{:S(2)}, u32[]{:S(2)}) collective-permute-start(f32[32,640]{1,0:T(8,128)S(1)} %add_add_fusion.4), channel_id=1, source_target_pairs={{0,16},{1,65},{2,18},{3,67},{4,20},{5,69},{6,22},{7,71},{8,24},{9,... | collective-permute-start | bytes 245768 | tf_op jit(solution)/shard_map/ppermute | solution.py:421
  35.9 4.6 %collective-permute-start.6 = (f32[32,640]{1,0:T(8,128)S(1)}, f32[32,640]{1,0:T(8,128)S(1)}, u32[]{:S(2)}, u32[]{:S(2)}) collective-permute-start(f32[32,640]{1,0:T(8,128)S(1)} %add_add_fusion.4), channel_id=1, source_target_pairs={{0,8},{1,33},{2,10},{3,35},{4,12},{5,37},{6,14},{7,39},{8,0},{9,41... | collective-permute-start | bytes 245768 | tf_op jit(solution)/shard_map/ppermute | solution.py:421
  40.5 6.0 %collective-permute-start.11 = (f32[32,640]{1,0:T(8,128)S(1)}, f32[32,640]{1,0:T(8,128)S(1)}, u32[]{:S(2)}, u32[]{:S(2)}) collective-permute-start(f32[32,640]{1,0:T(8,128)S(1)} %add_add_fusion.3), channel_id=1, source_target_pairs={{0,96},{1,7},{2,98},{3,5},{4,100},{5,3},{6,102},{7,1},{8,104},{9,1... | collective-permute-start | bytes 245768 | tf_op jit(solution)/shard_map/ppermute | solution.py:421
  44.3 4.8 %collective-permute-start.10 = (f32[32,640]{1,0:T(8,128)S(1)}, f32[32,640]{1,0:T(8,128)S(1)}, u32[]{:S(2)}, u32[]{:S(2)}) collective-permute-start(f32[32,640]{1,0:T(8,128)S(1)} %add_add_fusion.3), channel_id=1, source_target_pairs={{0,64},{1,5},{2,66},{3,7},{4,68},{5,1},{6,70},{7,3},{8,72},{9,13},... | collective-permute-start | bytes 245768 | tf_op jit(solution)/shard_map/ppermute | solution.py:421
  44.3 4.8 %collective-permute-start.9 = (f32[32,640]{1,0:T(8,128)S(1)}, f32[32,640]{1,0:T(8,128)S(1)}, u32[]{:S(2)}, u32[]{:S(2)}) collective-permute-start(f32[32,640]{1,0:T(8,128)S(1)} %add_add_fusion.3), channel_id=1, source_target_pairs={{0,32},{1,3},{2,34},{3,1},{4,36},{5,7},{6,38},{7,5},{8,40},{9,11},... | collective-permute-start | bytes 245768 | tf_op jit(solution)/shard_map/ppermute | solution.py:421
  49.1 5.6 %collective-permute-start.12 = (f32[32,640]{1,0:T(8,128)S(1)}, f32[32,640]{1,0:T(8,128)S(1)}, u32[]{:S(2)}, u32[]{:S(2)}) collective-permute-start(f32[32,640]{1,0:T(8,128)S(1)} %add_add_fusion.2.mine), channel_id=1, source_target_pairs={{0,1},{1,0},{2,3},{3,2},{4,5},{5,4},{6,7},{7,6},{8,9},{9,8},{10,11... | collective-permute-start | bytes 245768 | tf_op jit(solution)/shard_map/ppermute | solution.py:421
  64.2 1.5 %collective-permute-start.13 = (bf16[400,256]{1,0:T(8,128)(2,1)S(1)}, bf16[400,256]{1,0:T(8,128)(2,1)S(1)}, u32[]{:S(2)}, u32[]{:S(2)}) collective-permute-start(bf16[400,256]{1,0:T(8,128)(2,1)S(1)} %get-tuple-element.82), channel_id=1, source_target_pairs={{0,1},{1,0},{2,3},{3,2},{4,5},{5,4},{6,7},{7,6},{8,9},{9,8},{10,11... | collective-permute-start | bytes 614408 | tf_op jit(solution)/shard_map/ppermute | solution.py:421
  65.8 8.4 %collective-permute-start.16 = (bf16[400,256]{1,0:T(8,128)(2,1)S(1)}, bf16[400,256]{1,0:T(8,128)(2,1)S(1)}, u32[]{:S(2)}, u32[]{:S(2)}) collective-permute-start(bf16[400,256]{1,0:T(8,128)(2,1)S(1)} %add_convert_fusion.1), channel_id=1, source_target_pairs={{0,6},{1,25},{2,4},{3,27},{4,2},{5,29},{6,0},{7,31},{8,14},{9,17},... | collective-permute-start | bytes 614408 | tf_op jit(solution)/shard_map/ppermute | solution.py:421
  67.0 7.1 %collective-permute-start.15 = (bf16[400,256]{1,0:T(8,128)(2,1)S(1)}, bf16[400,256]{1,0:T(8,128)(2,1)S(1)}, u32[]{:S(2)}, u32[]{:S(2)}) collective-permute-start(bf16[400,256]{1,0:T(8,128)(2,1)S(1)} %add_convert_fusion.1), channel_id=1, source_target_pairs={{0,4},{1,17},{2,6},{3,19},{4,0},{5,21},{6,2},{7,23},{8,12},{9,25},... | collective-permute-start | bytes 614408 | tf_op jit(solution)/shard_map/ppermute | solution.py:421
  67.7 7.1 %collective-permute-start.14 = (bf16[400,256]{1,0:T(8,128)(2,1)S(1)}, bf16[400,256]{1,0:T(8,128)(2,1)S(1)}, u32[]{:S(2)}, u32[]{:S(2)}) collective-permute-start(bf16[400,256]{1,0:T(8,128)(2,1)S(1)} %add_convert_fusion.1), channel_id=1, source_target_pairs={{0,2},{1,9},{2,0},{3,11},{4,6},{5,13},{6,4},{7,15},{8,10},{9,1},{1... | collective-permute-start | bytes 614408 | tf_op jit(solution)/shard_map/ppermute | solution.py:421
  74.9 6.5 %collective-permute-start.18 = (bf16[400,256]{1,0:T(8,128)(2,1)S(1)}, bf16[400,256]{1,0:T(8,128)(2,1)S(1)}, u32[]{:S(2)}, u32[]{:S(2)}) collective-permute-start(bf16[400,256]{1,0:T(8,128)(2,1)S(1)} %add_add_fusion.1), channel_id=1, source_target_pairs={{0,16},{1,65},{2,18},{3,67},{4,20},{5,69},{6,22},{7,71},{8,24},{9,... | collective-permute-start | bytes 614408 | tf_op jit(solution)/shard_map/ppermute | solution.py:421
  77.2 5.9 %collective-permute-start.17 = (bf16[400,256]{1,0:T(8,128)(2,1)S(1)}, bf16[400,256]{1,0:T(8,128)(2,1)S(1)}, u32[]{:S(2)}, u32[]{:S(2)}) collective-permute-start(bf16[400,256]{1,0:T(8,128)(2,1)S(1)} %add_add_fusion.1), channel_id=1, source_target_pairs={{0,8},{1,33},{2,10},{3,35},{4,12},{5,37},{6,14},{7,39},{8,0},{9,41... | collective-permute-start | bytes 614408 | tf_op jit(solution)/shard_map/ppermute | solution.py:421
  77.5 6.1 %collective-permute-start.19 = (bf16[400,256]{1,0:T(8,128)(2,1)S(1)}, bf16[400,256]{1,0:T(8,128)(2,1)S(1)}, u32[]{:S(2)}, u32[]{:S(2)}) collective-permute-start(bf16[400,256]{1,0:T(8,128)(2,1)S(1)} %add_add_fusion.1), channel_id=1, source_target_pairs={{0,24},{1,97},{2,26},{3,99},{4,28},{5,101},{6,30},{7,103},{8,16},{... | collective-permute-start | bytes 614408 | tf_op jit(solution)/shard_map/ppermute | solution.py:421
  83.7 6.3 %collective-permute-start.21 = (bf16[400,256]{1,0:T(8,128)(2,1)S(1)}, bf16[400,256]{1,0:T(8,128)(2,1)S(1)}, u32[]{:S(2)}, u32[]{:S(2)}) collective-permute-start(bf16[400,256]{1,0:T(8,128)(2,1)S(1)} %add_add_fusion), channel_id=1, source_target_pairs={{0,64},{1,5},{2,66},{3,7},{4,68},{5,1},{6,70},{7,3},{8,72},{9,13},... | collective-permute-start | bytes 614408 | tf_op jit(solution)/shard_map/ppermute | solution.py:421
  85.5 5.6 %collective-permute-start.20 = (bf16[400,256]{1,0:T(8,128)(2,1)S(1)}, bf16[400,256]{1,0:T(8,128)(2,1)S(1)}, u32[]{:S(2)}, u32[]{:S(2)}) collective-permute-start(bf16[400,256]{1,0:T(8,128)(2,1)S(1)} %add_add_fusion), channel_id=1, source_target_pairs={{0,32},{1,3},{2,34},{3,1},{4,36},{5,7},{6,38},{7,5},{8,40},{9,11},... | collective-permute-start | bytes 614408 | tf_op jit(solution)/shard_map/ppermute | solution.py:421
  85.5 6.9 %collective-permute-start.22 = (bf16[400,256]{1,0:T(8,128)(2,1)S(1)}, bf16[400,256]{1,0:T(8,128)(2,1)S(1)}, u32[]{:S(2)}, u32[]{:S(2)}) collective-permute-start(bf16[400,256]{1,0:T(8,128)(2,1)S(1)} %add_add_fusion), channel_id=1, source_target_pairs={{0,96},{1,7},{2,98},{3,5},{4,100},{5,3},{6,102},{7,1},{8,104},{9,1... | collective-permute-start | bytes 614408 | tf_op jit(solution)/shard_map/ppermute | solution.py:421
  92.5 4.9 %collective-permute-start.23 = (bf16[400,256]{1,0:T(8,128)(2,1)S(1)}, bf16[400,256]{1,0:T(8,128)(2,1)S(1)}, u32[]{:S(2)}, u32[]{:S(2)}) collective-permute-start(bf16[400,256]{1,0:T(8,128)(2,1)S(1)} %add_convert_fusion.mine), channel_id=1, source_target_pairs={{0,1},{1,0},{2,3},{3,2},{4,5},{5,4},{6,7},{7,6},{8,9},{9,8},{10,11... | collective-permute-start | bytes 614408 | tf_op jit(solution)/shard_map/ppermute | solution.py:421
  (10 other events, 66.4 us)

commit v6 on v5

--- a/solution.py
+++ b/solution.py
@@ -20,8 +20,8 @@
 PAY1 = 640
 PAY2 = 800
 ORDER = (1, 2, 3)
-FT = 512
-SUB = BLOCK // FT
+FT = HALF * BLOCK
+BT = 1024
 BF = jnp.bfloat16
 F32 = jnp.float32
 HIGH = lax.Precision.HIGH
@@ -178,49 +178,44 @@
         watt[i] = jnp.where(same_head, jnp.concatenate([wide] * HEADS, axis=0), 0.0)
 
 
-def first_tile(t, core):
-    return t + HALF * SUB * (1 - core[0])
-
-
-def second_tile(t, core):
-    return t + HALF * SUB * core[0]
-
-
-def front_first(sel, core, own, other, dmix, gain, wf, wmt, bd, *outs):
-    *arrays, pay, acc, den = outs
-    tile = first_tile(pl.program_id(0), core)
-    front_tile(sel[2, tile // SUB], own, other, dmix, gain, wf, wmt, bd, *arrays, acc, den)
-
-    @pl.when(pl.program_id(0) == HALF * SUB - 1)
-    def _():
-        fold_sums(acc, den, pay)
-
-
-def front_second(sel, core, own, other, dmix, gain, wf, wmt, bd, pay_first, *rest):
-    *arrays, send, keep, acc, den, pay = rest[6:]
-    tile = second_tile(pl.program_id(0), core)
-    front_tile(sel[2, tile // SUB], own, other, dmix, gain, wf, wmt, bd, *arrays, acc, den)
-
-    @pl.when(pl.program_id(0) == HALF * SUB - 1)
-    def _():
-        fold_sums(acc, den, pay)
-        pay[...] += pay_first[...]
-        split_halves(core[0], pay, send, keep)
-
-
-def front_tile(
-    found, own, other, dmix, gain, wf, wmt, bd,
+def first_half(core):
+    return 1 - core[0]
+
+
+def second_half(core):
+    return core[0]
+
+
+def front_first(sel, core, *refs):
+    *arrays, pay, acc, den = refs
+    front_rows(sel, first_half(core), *arrays, acc, den)
+    fold_sums(acc, den, pay)
+
+
+def front_second(sel, core, *refs):
+    ins, pay_first, rest = refs[:9], refs[9], refs[16:]
+    *arrays, send, keep, acc, den, pay = rest
+    front_rows(sel, second_half(core), *ins, *arrays, acc, den)
+    fold_sums(acc, den, pay)
+    pay[...] += pay_first[...]
+    split_halves(core[0], pay, send, keep)
+
+
+def front_rows(
+    sel, half, own_a, own_b, other_a, other_b, dmix, gain, wf, wmt, bd,
     ptsb, normed_out, feat_out, mid_out, prob_out, aux, acc, den,
 ):
-    t = pl.program_id(0)
-
-    @pl.when(found == 1)
-    def _():
-        ptsb[...] = own[...]
-
-    @pl.when(found != 1)
-    def _():
-        ptsb[...] = other[...]
+    for i, (own, other) in enumerate(((own_a, other_a), (own_b, other_b))):
+        found = sel[2, HALF * half + i]
+        place = slice(i * BLOCK, (i + 1) * BLOCK)
+
+        @pl.when(found == 1)
+        def _(own=own, place=place):
+            ptsb[place] = own[...]
+
+        @pl.when(found != 1)
+        def _(other=other, place=place):
+            ptsb[place] = other[...]
 
     x_hat, _ = normalize(ptsb[...])
     normed = (x_hat * gain[...]).astype(BF)
@@ -236,16 +231,11 @@
     aux[2 * HEADS :] = raw_top
     weights = prob.reshape(HS, FT).astype(BF)
 
-    @pl.when(t == 0)
-    def _():
-        acc[...] = jnp.zeros_like(acc)
-        den[...] = jnp.zeros_like(den)
-
     grad = dmix[...]
     for i in range(2):
         both = jnp.concatenate([feat[:, i * G : (i + 1) * G], grad[:, i * G : (i + 1) * G]], axis=1)
-        acc[i * GS : (i + 1) * GS] += dot(weights[i * GS : (i + 1) * GS], both)
-    den[...] += dot(weights, jnp.ones((FT, 128), BF))
+        acc[i * GS : (i + 1) * GS] = dot(weights[i * GS : (i + 1) * GS], both)
+    den[...] = dot(weights, jnp.ones((FT, 128), BF))
 
 
 def fold_sums(acc, den, pay):
@@ -338,24 +328,24 @@
 
     mid_t = mid[...]
     weights = prob_in[...].astype(BF)
-    prob = prob_in[...].reshape(HEADS, SLICES, BLOCK)
+    prob = prob_in[...].reshape(HEADS, SLICES, BT)
     inv = aux[:HEADS]
     groups = []
     for i in range(2):
         lanes = slice(i * G, (i + 1) * G)
         groups.append(dot(an[i], jnp.concatenate([dmix[:, lanes], feat[:, lanes]], axis=1), NT))
     dw = jnp.concatenate(groups, axis=0) + dd[...]
-    dw = dw.reshape(HEADS, SLICES, BLOCK)
+    dw = dw.reshape(HEADS, SLICES, BT)
     dl = prob * (dw - jnp.sum(prob * dw, axis=1, keepdims=True))
-    d_raw = (dl * inv[:, None, :]).reshape(HS, BLOCK).astype(BF)
+    d_raw = (dl * inv[:, None, :]).reshape(HS, BT).astype(BF)
     direct = dot(bdt[...], d_raw)
-    inner = (mid_t.astype(F32) * direct[:C]).reshape(HEADS, HEAD, BLOCK)
+    inner = (mid_t.astype(F32) * direct[:C]).reshape(HEADS, HEAD, BT)
     against_top = jnp.sum(inner, axis=1) - aux[2 * HEADS :] * direct[C : C + HEADS]
     d_temper = -against_top * aux[HEADS : 2 * HEADS]
     low = dot(ant[0], weights[:GS]).astype(BF)
     high = dot(ant[1], weights[GS:]).astype(BF)
     mixed_df = jnp.concatenate([low[:G], high[:G], low[G:], high[G:]], axis=0)
-    spread = jnp.broadcast_to(d_temper[:, None, :], (HEADS, HEAD, BLOCK)).reshape(C, BLOCK)
+    spread = jnp.broadcast_to(d_temper[:, None, :], (HEADS, HEAD, BT)).reshape(C, BT)
     dm = (direct[:C] + spread * wcol[...]).astype(BF)
     res[: 2 * C] = mixed_df
     res[2 * C :] = dm
@@ -368,7 +358,7 @@
     gsl[:HS] += dot(d_raw, mid_t, NT)
     gsl[HS:] += dot(jnp.concatenate([dt_hi, dt_lo], axis=0), mid_t, NT)
 
-    @pl.when(t == B_DEV - 1)
+    @pl.when(t == ROWS // BT - 1)
     def _():
         grad_fm = gfm[...]
         gpay[: 2 * C] = grad_fm
@@ -456,6 +446,7 @@
 
 
 PARAMS = pltpu.CompilerParams(vmem_limit_bytes=24 * 1024 * 1024)
+BACK_PARAMS = pltpu.CompilerParams(vmem_limit_bytes=32 * 1024 * 1024)
 SCALARS = pl.BlockSpec(memory_space=pltpu.SMEM)
 HBM = pl.BlockSpec(memory_space=pl.ANY)
 
@@ -526,19 +517,23 @@
 
     wide = jax.ShapeDtypeStruct((ROWS, C), BF)
     half1 = jax.ShapeDtypeStruct((SLICES // 2, PAY1), F32)
-    cols_of = lambda rows: pl.BlockSpec((rows, BLOCK), lambda t, *_: (0, t))
     arrays = [wide] * 3 + [
         jax.ShapeDtypeStruct((C, ROWS), BF),
         jax.ShapeDtypeStruct((HS, ROWS), F32),
         jax.ShapeDtypeStruct((3 * HEADS, ROWS), F32),
     ]
 
-    def front_specs(tile):
-        rows = pl.BlockSpec((FT, C), lambda t, s, c: (tile(t, c), 0))
-        cols = lambda n: pl.BlockSpec((n, FT), lambda t, s, c: (0, tile(t, c)))
+    def front_specs(half):
+        rows = pl.BlockSpec((FT, C), lambda t, s, c: (half(c), 0))
+        cols = lambda n: pl.BlockSpec((n, FT), lambda t, s, c: (0, half(c)))
+        block = lambda row, i: pl.BlockSpec(
+            (BLOCK, C), lambda t, s, c: (s[row, HALF * half(c) + i], 0)
+        )
         ins = [
-            pl.BlockSpec((FT, C), lambda t, s, c: (s[0, tile(t, c) // SUB] * SUB + t % SUB, 0)),
-            pl.BlockSpec((FT, C), lambda t, s, c: (s[1, tile(t, c) // SUB] * SUB + t % SUB, 0)),
+            block(0, 0),
+            block(0, 1),
+            block(1, 0),
+            block(1, 1),
             rows,
             whole((1, C)),
             whole((C, C)),
@@ -548,12 +543,12 @@
         return ins, [rows] * 3 + [cols(C), cols(HS), cols(3 * HEADS)]
 
     sums = [pltpu.VMEM((HS, C), F32), pltpu.VMEM((HS, 128), F32)]
-    ins, outs = front_specs(first_tile)
+    ins, outs = front_specs(first_half)
     *first, pay = pl.pallas_call(
         front_first,
         grid_spec=pltpu.PrefetchScalarGridSpec(
             num_scalar_prefetch=2,
-            grid=(HALF * SUB,),
+            grid=(1,),
             in_specs=ins,
             out_specs=outs + [whole((SLICES, PAY1))],
             scratch_shapes=sums,
@@ -564,36 +559,41 @@
             flops=2 * ROWS * C * 3 * C, bytes_accessed=6 * 1024 * 1024, transcendentals=0
         ),
         name="front_first",
-    )(sel, core, loader_points, got_inner, d_mixed, gain, w_feature, wfmt, bd)
+    )(sel, core, loader_points, loader_points, got_inner, got_inner, d_mixed, gain, w_feature, wfmt, bd)
     pay, (bdt, wcol, watt) = lax.optimization_barrier((pay, back_weights))
-    ins, outs = front_specs(second_tile)
+    ins, outs = front_specs(second_half)
     *first, send, keep = pl.pallas_call(
         front_second,
         grid_spec=pltpu.PrefetchScalarGridSpec(
             num_scalar_prefetch=2,
-            grid=(HALF * SUB,),
+            grid=(1,),
             in_specs=ins + [whole((SLICES, PAY1))] + [HBM] * 6,
             out_specs=outs + [whole((SLICES // 2, PAY1))] * 2,
             scratch_shapes=sums + [pltpu.VMEM((SLICES, PAY1), F32)],
         ),
         out_shape=arrays + [half1] * 2,
-        input_output_aliases={10 + i: i for i in range(6)},
+        input_output_aliases={12 + i: i for i in range(6)},
         compiler_params=PARAMS,
         name="front_second",
-    )(sel, core, loader_points, got_outer, d_mixed, gain, w_feature, wfmt, bd, pay, *first)
+    )(
+        sel, core, loader_points, loader_points, got_outer, got_outer, d_mixed, gain, w_feature,
+        wfmt, bd, pay, *first,
+    )
     ptsb, normed, feat, mid, prob, aux = first
 
     mine, other, _ = sum_over_chips(send, keep, F32)
 
+    back_rows = pl.BlockSpec((BT, C), lambda t: (t, 0))
+    back_cols = lambda rows: pl.BlockSpec((rows, BT), lambda t: (0, t))
     res, send, keep, toks = pl.pallas_call(
         back_kernel,
-        grid=(B_DEV,),
+        grid=(ROWS // BT,),
         in_specs=[SCALARS]
         + [whole((SLICES // 2, PAY1))] * 2
         + [whole((3, C, C))]
-        + [rows_spec(C)] * 2
-        + [cols_of(C), cols_of(HS), cols_of(3 * HEADS)]
-        + [rows_spec(C)] * 2
+        + [back_rows] * 2
+        + [back_cols(C), back_cols(HS), back_cols(3 * HEADS)]
+        + [back_rows] * 2
         + [
             whole((1, C)),
             whole((2 * C, C)),
@@ -601,7 +601,7 @@
             whole((C, 1)),
         ],
         out_specs=[
-            pl.BlockSpec((3 * C, BLOCK), lambda t: (0, t)),
+            back_cols(3 * C),
             whole((PAY2 // 2, C)),
             whole((PAY2 // 2, C)),
             whole((4, SLICES, C)),
@@ -622,7 +622,7 @@
             pltpu.VMEM((SLICES, PAY1), F32),
             pltpu.VMEM((PAY2, C), F32),
         ],
-        compiler_params=PARAMS,
+        compiler_params=BACK_PARAMS,
         name="back",
     )(
         core, mine, other, watt, normed, feat, mid, prob, aux, d_mixed, cotangent, gain, wfmt,

time: 98.7 us -> 97 us (0.983)
  Pallas kernels: 29.2 us -> 26.2 us
  waiting for transfers between devices: 28.6 us -> 29.7 us
    ppermute x1, waiting for transfers between devices: 0.6 us -> 1.78 us  [neighbour_blocks(): got_outer = lax.ppermute(outer, 'pts', edges + [(j, i) for i, j in edges])]
    pallas_call x1, Pallas kernels: 4.62 us -> 3.44 us  [per_device(): pl.pallas_call(front_first, grid_spec=pltpu.PrefetchScalarGridSpec(num_sc...]
    pallas_call x1, Pallas kernels: 4.66 us -> 3.64 us  [per_device(): pl.pallas_call(front_second, grid_spec=pltpu.PrefetchScalarGridSpec(num_s...]
  transfers between devices with their start and end apart: 24 -> 24, of which waited for: 19 -> 19; matrix products, arithmetic and copies ran while one was open for 0% -> 0% of each run, Pallas kernels for 11% -> 10%
where the time goes in v6:
time: 97 us; the launch traced here: 96.8 us
  starting transfers between devices  37.9 us (39%)
  waiting for transfers between devices  29.7 us (31%)
  Pallas kernels  26.2 us (27%)
  local copies, waits for them, and re-layouts  1.5 us (2%)
    ppermute x23, starting transfers between devices, swap(): lax.ppermute(array, 'pts', [(i, i ^ (odd if i % 2 else even)) for i in ra...  34.8 us
    ppermute x23, waiting for transfers between devices, swap(): lax.ppermute(array, 'pts', [(i, i ^ (odd if i % 2 else even)) for i in ra...  28 us
    pallas_call x1, Pallas kernels, per_device(): pl.pallas_call(back_kernel, grid=(ROWS // BT,), in_specs=[SCALARS] + [who...  8.71 us
    pallas_call x1, Pallas kernels, per_device(): pl.pallas_call(out_kernel, grid=(B_DEV,), in_specs=[rows_spec(C), rows_sp...  3.69 us
    pallas_call x1, Pallas kernels, per_device(): pl.pallas_call(front_second, grid_spec=pltpu.PrefetchScalarGridSpec(num_s...  3.64 us
    pallas_call x1, Pallas kernels, per_device(): pl.pallas_call(front_first, grid_spec=pltpu.PrefetchScalarGridSpec(num_sc...  3.44 us
    pallas_call x1, Pallas kernels, per_device(): pl.pallas_call(pick_kernel, grid_spec=pltpu.PrefetchScalarGridSpec(num_sc...  3.11 us
    ppermute x1, starting transfers between devices, neighbour_blocks(): got_outer = lax.ppermute(outer, 'pts', edges + [(j, i) for i, j in edges])  3.08 us
  transfers between devices with their start and end apart: 24, of which 19 were waited for; matrix products, arithmetic and copies ran while one was open for 0% of the time, Pallas kernels for 10%

profile of v6, /device:TPU:1, one launch (start us, length us, event | category | flops | bytes accessed | tf_op | source)
XLA Modules:
  0.0 96.8 jit_solution(15930448647689033699)
XLA Ops:
  0.7 3.1 %pick.1 = (s32[3,4]{1,0:T(4,128)}, bf16[1024,256]{1,0:T(8,128)(2,1)}, bf16[1024,256]{1,0:T(8,128)(2,1)}) custom-call(s32[1]{0:T(128)} %bitcast.rank, s32[128]{0:T(128)} %counts.1, s32[8]{0:T(128)} %table.1, bf16[4096,256]{1,0:T(8,128)(2,1)} %refs_1_.3, bf16[4096,256]{1,0:T(8,128)(2,1)} %refs_1_.3), custom_call_target="tpu_custom_call" | custom-call | tf_op jit(solution)/shard_map/pick/pallas_call | solution.py:471
  5.3 3.1 %collective-permute-start = (bf16[1024,256]{1,0:T(8,128)(2,1)}, bf16[1024,256]{1,0:T(8,128)(2,1)S(1)}, u32[]{:S(2)}, u32[]{:S(2)}) collective-permute-start(bf16[1024,256]{1,0:T(8,128)(2,1)} %get-tuple-element.55), channel_id=1, source_target_pairs={{1,2},{3,4},{5,6},{7,8},{9,10},{11,12},{13,14},{15,16},{17,18},{19... | collective-permute-start | bytes 1572872 | tf_op jit(solution)/shard_map/ppermute | solution.py:436
  10.7 3.4 %front_first.1 = (bf16[2048,256]{1,0:T(8,128)(2,1)S(1)}, bf16[2048,256]{1,0:T(8,128)(2,1)S(1)}, bf16[2048,256]{1,0:T(8,128)(2,1)S(1)}, bf16[256,2048]{1,0:T(8,12...) custom-call(s32[3,4]{1,0:T(4,128)S(1)} %copy-done.8, s32[1]{0:T(128)S(6)} %rem.18.core, ...), custom_call_target="tpu_custom_call" | custom-call | flops 805306368 | bytes 6291456 | tf_op jit(solution)/shard_map/front_first/pallas_call | solution.py:547
  14.2 1.8 %collective-permute-done.refs_2_.refs_3_ = bf16[1024,256]{1,0:T(8,128)(2,1)S(1)} collective-permute-done((bf16[1024,256]{1,0:T(8,128)(2,1)}, bf16[1024,256]{1,0:T(8,128)(2,1)S(1)}, u32[]{:S(2)}, u32[]{:S(2)}) %collective-permute-start) | collective-permute-done | bytes 524320 | tf_op jit(solution)/shard_map/ppermute | solution.py:436
  16.0 3.6 %front_second.1 = (bf16[2048,256]{1,0:T(8,128)(2,1)S(1)}, bf16[2048,256]{1,0:T(8,128)(2,1)S(1)}, bf16[2048,256]{1,0:T(8,128)(2,1)S(1)}, bf16[256,2048]{1,0:T(8,1...) custom-call(s32[3,4]{1,0:T(4,128)S(1)} %copy-done.8, ...), custom_call_target="tpu_custom_call", output_to_operand_aliasing={{0}: (12, {}), {1}: (13, {}), {2}: (14, {}), {3}: (15, {}),... | custom-call | tf_op jit(solution)/shard_map/front_second/pallas_call | solution.py:565
  21.0 5.7 %collective-permute-start.5 = (f32[32,640]{1,0:T(8,128)S(1)}, f32[32,640]{1,0:T(8,128)S(1)}, u32[]{:S(2)}, u32[]{:S(2)}) collective-permute-start(f32[32,640]{1,0:T(8,128)S(1)} %add.60), channel_id=1, source_target_pairs={{0,6},{1,25},{2,4},{3,27},{4,2},{5,29},{6,0},{7,31},{8,14},{9,17},... | collective-permute-start | bytes 245768 | tf_op jit(solution)/shard_map/ppermute | solution.py:411
  27.3 1.6 %collective-permute-done.5 = f32[32,640]{1,0:T(8,128)S(1)} collective-permute-done((f32[32,640]{1,0:T(8,128)S(1)}, f32[32,640]{1,0:T(8,128)S(1)}, u32[]{:S(2)}, u32[]{:S(2)}) %collective-permute-start.5) | collective-permute-done | bytes 81952 | tf_op jit(solution)/shard_map/ppermute | solution.py:411
  28.9 2.8 %collective-permute-done.4 = f32[32,640]{1,0:T(8,128)S(1)} collective-permute-done((f32[32,640]{1,0:T(8,128)S(1)}, f32[32,640]{1,0:T(8,128)S(1)}, u32[]{:S(2)}, u32[]{:S(2)}) %collective-permute-start.4) | collective-permute-done | bytes 81952 | tf_op jit(solution)/shard_map/ppermute | solution.py:411
  31.8 2.9 %collective-permute-start.8 = (f32[32,640]{1,0:T(8,128)S(1)}, f32[32,640]{1,0:T(8,128)S(1)}, u32[]{:S(2)}, u32[]{:S(2)}) collective-permute-start(f32[32,640]{1,0:T(8,128)S(1)} %add_add_fusion.4), channel_id=1, source_target_pairs={{0,24},{1,97},{2,26},{3,99},{4,28},{5,101},{6,30},{7,103},{8,16},{... | collective-permute-start | bytes 245768 | tf_op jit(solution)/shard_map/ppermute | solution.py:411
  35.3 1.6 %collective-permute-done.8 = f32[32,640]{1,0:T(8,128)S(1)} collective-permute-done((f32[32,640]{1,0:T(8,128)S(1)}, f32[32,640]{1,0:T(8,128)S(1)}, u32[]{:S(2)}, u32[]{:S(2)}) %collective-permute-start.8) | collective-permute-done | bytes 81952 | tf_op jit(solution)/shard_map/ppermute | solution.py:411
  36.9 2.5 %collective-permute-done.7 = f32[32,640]{1,0:T(8,128)S(1)} collective-permute-done((f32[32,640]{1,0:T(8,128)S(1)}, f32[32,640]{1,0:T(8,128)S(1)}, u32[]{:S(2)}, u32[]{:S(2)}) %collective-permute-start.7) | collective-permute-done | bytes 81952 | tf_op jit(solution)/shard_map/ppermute | solution.py:411
  39.5 3.8 %collective-permute-start.11 = (f32[32,640]{1,0:T(8,128)S(1)}, f32[32,640]{1,0:T(8,128)S(1)}, u32[]{:S(2)}, u32[]{:S(2)}) collective-permute-start(f32[32,640]{1,0:T(8,128)S(1)} %add_add_fusion.3), channel_id=1, source_target_pairs={{0,96},{1,7},{2,98},{3,5},{4,100},{5,3},{6,102},{7,1},{8,104},{9,1... | collective-permute-start | bytes 245768 | tf_op jit(solution)/shard_map/ppermute | solution.py:411
  44.0 1.6 %collective-permute-done.11 = f32[32,640]{1,0:T(8,128)S(1)} collective-permute-done((f32[32,640]{1,0:T(8,128)S(1)}, f32[32,640]{1,0:T(8,128)S(1)}, u32[]{:S(2)}, u32[]{:S(2)}) %collective-permute-start.11) | collective-permute-done | bytes 81952 | tf_op jit(solution)/shard_map/ppermute | solution.py:411
  45.5 2.5 %collective-permute-done.10 = f32[32,640]{1,0:T(8,128)S(1)} collective-permute-done((f32[32,640]{1,0:T(8,128)S(1)}, f32[32,640]{1,0:T(8,128)S(1)}, u32[]{:S(2)}, u32[]{:S(2)}) %collective-permute-start.10) | collective-permute-done | bytes 81952 | tf_op jit(solution)/shard_map/ppermute | solution.py:411
  48.1 4.7 %collective-permute-start.12 = (f32[32,640]{1,0:T(8,128)S(1)}, f32[32,640]{1,0:T(8,128)S(1)}, u32[]{:S(2)}, u32[]{:S(2)}) collective-permute-start(f32[32,640]{1,0:T(8,128)S(1)} %add_add_fusion.2.mine), channel_id=1, source_target_pairs={{0,1},{1,0},{2,3},{3,2},{4,5},{5,4},{6,7},{7,6},{8,9},{9,8},{10,11... | collective-permute-start | bytes 245768 | tf_op jit(solution)/shard_map/ppermute | solution.py:411
  53.7 8.7 %back.1 = (bf16[768,2048]{1,0:T(8,128)(2,1)S(1)}, bf16[400,256]{1,0:T(8,128)(2,1)S(1)}, f32[400,256]{1,0:T(8,128)S(1)}, f32[4,64,256]{2,1,0:T(8,128)S(1)}) custom-call(s32[1]{0:T(128)S(6)} %rem.18.core, f32[32,640]{1,0:T(8,128)S(1)} %add_add_fusion.2.mine, f32[32,640]{1,0:T(8,128)S(1)} %collective-permute-done.12.other, ...), custom_call_target="tpu_custom_call" | custom-call | tf_op jit(solution)/shard_map/back/pallas_call | solution.py:588
  67.4 3.7 %outputs.1 = (bf16[2048,256]{1,0:T(8,128)(2,1)}, bf16[2048,256]{1,0:T(8,128)(2,1)}) custom-call(bf16[2048,256]{1,0:T(8,128)(2,1)S(1)} %get-tuple-element.83.ptsb, bf16[2048,256]{1,0:T(8,128)(2,1)S(1)} %copy-done.1, bf16[768,2048]{1,0:T(8,128)(2,1)S(1)} %get-tuple-element.84.res, f32[1,256]{1,0:T(1,128)S(1)} %bitcast.8, ...), custom_call_target="tpu_custom_call" | custom-call | flops 805306368 | bytes 7340032 | tf_op jit(solution)/shard_map/outputs/pallas_call | solution.py:632
  73.2 2.3 %collective-permute-start.18 = (bf16[400,256]{1,0:T(8,128)(2,1)S(1)}, bf16[400,256]{1,0:T(8,128)(2,1)S(1)}, u32[]{:S(2)}, u32[]{:S(2)}) collective-permute-start(bf16[400,256]{1,0:T(8,128)(2,1)S(1)} %add_add_fusion.1), channel_id=1, source_target_pairs={{0,16},{1,65},{2,18},{3,67},{4,20},{5,69},{6,22},{7,71},{8,24},{9,... | collective-permute-start | bytes 614408 | tf_op jit(solution)/shard_map/ppermute | solution.py:411
  76.5 1.7 %attend_grads.1 = f32[3,32,32]{2,1,0:T(8,128)} custom-call(f32[4,64,256]{2,1,0:T(8,128)S(1)} %get-tuple-element.90.toks), custom_call_target="tpu_custom_call" | custom-call | tf_op jit(solution)/shard_map/attend_grads/pallas_call | solution.py:652
  79.6 1.7 %collective-permute-done.17 = bf16[400,256]{1,0:T(8,128)(2,1)S(1)} collective-permute-done((bf16[400,256]{1,0:T(8,128)(2,1)S(1)}, bf16[400,256]{1,0:T(8,128)(2,1)S(1)}, u32[]{:S(2)}, u32[]{:S(2)}) %collective-permute-start.17) | collective-permute-done | bytes 204832 | tf_op jit(solution)/shard_map/ppermute | solution.py:411
  82.0 1.8 %collective-permute-start.21 = (bf16[400,256]{1,0:T(8,128)(2,1)S(1)}, bf16[400,256]{1,0:T(8,128)(2,1)S(1)}, u32[]{:S(2)}, u32[]{:S(2)}) collective-permute-start(bf16[400,256]{1,0:T(8,128)(2,1)S(1)} %add_add_fusion), channel_id=1, source_target_pairs={{0,64},{1,5},{2,66},{3,7},{4,68},{5,1},{6,70},{7,3},{8,72},{9,13},... | collective-permute-start | bytes 614408 | tf_op jit(solution)/shard_map/ppermute | solution.py:411
  83.8 1.5 %collective-permute-start.22 = (bf16[400,256]{1,0:T(8,128)(2,1)S(1)}, bf16[400,256]{1,0:T(8,128)(2,1)S(1)}, u32[]{:S(2)}, u32[]{:S(2)}) collective-permute-start(bf16[400,256]{1,0:T(8,128)(2,1)S(1)} %add_add_fusion), channel_id=1, source_target_pairs={{0,96},{1,7},{2,98},{3,5},{4,100},{5,3},{6,102},{7,1},{8,104},{9,1... | collective-permute-start | bytes 614408 | tf_op jit(solution)/shard_map/ppermute | solution.py:411
  85.3 2.9 %collective-permute-done.21 = bf16[400,256]{1,0:T(8,128)(2,1)S(1)} collective-permute-done((bf16[400,256]{1,0:T(8,128)(2,1)S(1)}, bf16[400,256]{1,0:T(8,128)(2,1)S(1)}, u32[]{:S(2)}, u32[]{:S(2)}) %collective-permute-start.21) | collective-permute-done | bytes 204832 | tf_op jit(solution)/shard_map/ppermute | solution.py:411
  90.8 3.8 %collective-permute-start.23 = (bf16[400,256]{1,0:T(8,128)(2,1)S(1)}, bf16[400,256]{1,0:T(8,128)(2,1)S(1)}, u32[]{:S(2)}, u32[]{:S(2)}) collective-permute-start(bf16[400,256]{1,0:T(8,128)(2,1)S(1)} %add_convert_fusion.mine), channel_id=1, source_target_pairs={{0,1},{1,0},{2,3},{3,2},{4,5},{5,4},{6,7},{7,6},{8,9},{9,8},{10,11... | collective-permute-start | bytes 614408 | tf_op jit(solution)/shard_map/ppermute | solution.py:411
  (61 shorter events, 22.9 us)
Async XLA Ops:
  3.8 6.2 %collective-permute-start.1 = (bf16[1024,256]{1,0:T(8,128)(2,1)}, bf16[1024,256]{1,0:T(8,128)(2,1)S(1)}, u32[]{:S(2)}, u32[]{:S(2)}) collective-permute-start(bf16[1024,256]{1,0:T(8,128)(2,1)} %get-tuple-element.59), channel_id=1, source_target_pairs={{0,1},{1,0},{2,3},{3,2},{4,5},{5,4},{6,7},{7,6},{8,9},{9,8},{10,11... | collective-permute-start | bytes 1572872 | tf_op jit(solution)/shard_map/ppermute | solution.py:411
  5.3 10.7 %collective-permute-start = (bf16[1024,256]{1,0:T(8,128)(2,1)}, bf16[1024,256]{1,0:T(8,128)(2,1)S(1)}, u32[]{:S(2)}, u32[]{:S(2)}) collective-permute-start(bf16[1024,256]{1,0:T(8,128)(2,1)} %get-tuple-element.55), channel_id=1, source_target_pairs={{1,2},{3,4},{5,6},{7,8},{9,10},{11,12},{13,14},{15,16},{17,18},{19... | collective-permute-start | bytes 1572872 | tf_op jit(solution)/shard_map/ppermute | solution.py:436
  19.6 1.4 %collective-permute-start.2 = (f32[32,640]{1,0:T(8,128)S(1)}, f32[32,640]{1,0:T(8,128)S(1)}, u32[]{:S(2)}, u32[]{:S(2)}) collective-permute-start(f32[32,640]{1,0:T(8,128)S(1)} %get-tuple-element.72), channel_id=1, source_target_pairs={{0,1},{1,0},{2,3},{3,2},{4,5},{5,4},{6,7},{7,6},{8,9},{9,8},{10,11... | collective-permute-start | bytes 245768 | tf_op jit(solution)/shard_map/ppermute | solution.py:411
  21.0 7.9 %collective-permute-start.5 = (f32[32,640]{1,0:T(8,128)S(1)}, f32[32,640]{1,0:T(8,128)S(1)}, u32[]{:S(2)}, u32[]{:S(2)}) collective-permute-start(f32[32,640]{1,0:T(8,128)S(1)} %add.60), channel_id=1, source_target_pairs={{0,6},{1,25},{2,4},{3,27},{4,2},{5,29},{6,0},{7,31},{8,14},{9,17},... | collective-permute-start | bytes 245768 | tf_op jit(solution)/shard_map/ppermute | solution.py:411
  26.7 5.1 %collective-permute-start.4 = (f32[32,640]{1,0:T(8,128)S(1)}, f32[32,640]{1,0:T(8,128)S(1)}, u32[]{:S(2)}, u32[]{:S(2)}) collective-permute-start(f32[32,640]{1,0:T(8,128)S(1)} %add.60), channel_id=1, source_target_pairs={{0,4},{1,17},{2,6},{3,19},{4,0},{5,21},{6,2},{7,23},{8,12},{9,25},... | collective-permute-start | bytes 245768 | tf_op jit(solution)/shard_map/ppermute | solution.py:411
  26.7 5.1 %collective-permute-start.3 = (f32[32,640]{1,0:T(8,128)S(1)}, f32[32,640]{1,0:T(8,128)S(1)}, u32[]{:S(2)}, u32[]{:S(2)}) collective-permute-start(f32[32,640]{1,0:T(8,128)S(1)} %add.60), channel_id=1, source_target_pairs={{0,2},{1,9},{2,0},{3,11},{4,6},{5,13},{6,4},{7,15},{8,10},{9,1},{1... | collective-permute-start | bytes 245768 | tf_op jit(solution)/shard_map/ppermute | solution.py:411
  31.8 5.2 %collective-permute-start.8 = (f32[32,640]{1,0:T(8,128)S(1)}, f32[32,640]{1,0:T(8,128)S(1)}, u32[]{:S(2)}, u32[]{:S(2)}) collective-permute-start(f32[32,640]{1,0:T(8,128)S(1)} %add_add_fusion.4), channel_id=1, source_target_pairs={{0,24},{1,97},{2,26},{3,99},{4,28},{5,101},{6,30},{7,103},{8,16},{... | collective-permute-start | bytes 245768 | tf_op jit(solution)/shard_map/ppermute | solution.py:411
  34.7 4.8 %collective-permute-start.7 = (f32[32,640]{1,0:T(8,128)S(1)}, f32[32,640]{1,0:T(8,128)S(1)}, u32[]{:S(2)}, u32[]{:S(2)}) collective-permute-start(f32[32,640]{1,0:T(8,128)S(1)} %add_add_fusion.4), channel_id=1, source_target_pairs={{0,16},{1,65},{2,18},{3,67},{4,20},{5,69},{6,22},{7,71},{8,24},{9,... | collective-permute-start | bytes 245768 | tf_op jit(solution)/shard_map/ppermute | solution.py:411
  34.9 4.6 %collective-permute-start.6 = (f32[32,640]{1,0:T(8,128)S(1)}, f32[32,640]{1,0:T(8,128)S(1)}, u32[]{:S(2)}, u32[]{:S(2)}) collective-permute-start(f32[32,640]{1,0:T(8,128)S(1)} %add_add_fusion.4), channel_id=1, source_target_pairs={{0,8},{1,33},{2,10},{3,35},{4,12},{5,37},{6,14},{7,39},{8,0},{9,41... | collective-permute-start | bytes 245768 | tf_op jit(solution)/shard_map/ppermute | solution.py:411
  39.5 6.0 %collective-permute-start.11 = (f32[32,640]{1,0:T(8,128)S(1)}, f32[32,640]{1,0:T(8,128)S(1)}, u32[]{:S(2)}, u32[]{:S(2)}) collective-permute-start(f32[32,640]{1,0:T(8,128)S(1)} %add_add_fusion.3), channel_id=1, source_target_pairs={{0,96},{1,7},{2,98},{3,5},{4,100},{5,3},{6,102},{7,1},{8,104},{9,1... | collective-permute-start | bytes 245768 | tf_op jit(solution)/shard_map/ppermute | solution.py:411
  43.3 4.8 %collective-permute-start.10 = (f32[32,640]{1,0:T(8,128)S(1)}, f32[32,640]{1,0:T(8,128)S(1)}, u32[]{:S(2)}, u32[]{:S(2)}) collective-permute-start(f32[32,640]{1,0:T(8,128)S(1)} %add_add_fusion.3), channel_id=1, source_target_pairs={{0,64},{1,5},{2,66},{3,7},{4,68},{5,1},{6,70},{7,3},{8,72},{9,13},... | collective-permute-start | bytes 245768 | tf_op jit(solution)/shard_map/ppermute | solution.py:411
  43.3 4.8 %collective-permute-start.9 = (f32[32,640]{1,0:T(8,128)S(1)}, f32[32,640]{1,0:T(8,128)S(1)}, u32[]{:S(2)}, u32[]{:S(2)}) collective-permute-start(f32[32,640]{1,0:T(8,128)S(1)} %add_add_fusion.3), channel_id=1, source_target_pairs={{0,32},{1,3},{2,34},{3,1},{4,36},{5,7},{6,38},{7,5},{8,40},{9,11},... | collective-permute-start | bytes 245768 | tf_op jit(solution)/shard_map/ppermute | solution.py:411
  48.1 5.6 %collective-permute-start.12 = (f32[32,640]{1,0:T(8,128)S(1)}, f32[32,640]{1,0:T(8,128)S(1)}, u32[]{:S(2)}, u32[]{:S(2)}) collective-permute-start(f32[32,640]{1,0:T(8,128)S(1)} %add_add_fusion.2.mine), channel_id=1, source_target_pairs={{0,1},{1,0},{2,3},{3,2},{4,5},{5,4},{6,7},{7,6},{8,9},{9,8},{10,11... | collective-permute-start | bytes 245768 | tf_op jit(solution)/shard_map/ppermute | solution.py:411
  62.4 1.5 %collective-permute-start.13 = (bf16[400,256]{1,0:T(8,128)(2,1)S(1)}, bf16[400,256]{1,0:T(8,128)(2,1)S(1)}, u32[]{:S(2)}, u32[]{:S(2)}) collective-permute-start(bf16[400,256]{1,0:T(8,128)(2,1)S(1)} %get-tuple-element.82), channel_id=1, source_target_pairs={{0,1},{1,0},{2,3},{3,2},{4,5},{5,4},{6,7},{7,6},{8,9},{9,8},{10,11... | collective-permute-start | bytes 614408 | tf_op jit(solution)/shard_map/ppermute | solution.py:411
  64.0 8.4 %collective-permute-start.16 = (bf16[400,256]{1,0:T(8,128)(2,1)S(1)}, bf16[400,256]{1,0:T(8,128)(2,1)S(1)}, u32[]{:S(2)}, u32[]{:S(2)}) collective-permute-start(bf16[400,256]{1,0:T(8,128)(2,1)S(1)} %add_convert_fusion.1), channel_id=1, source_target_pairs={{0,6},{1,25},{2,4},{3,27},{4,2},{5,29},{6,0},{7,31},{8,14},{9,17},... | collective-permute-start | bytes 614408 | tf_op jit(solution)/shard_map/ppermute | solution.py:411
  65.3 7.2 %collective-permute-start.15 = (bf16[400,256]{1,0:T(8,128)(2,1)S(1)}, bf16[400,256]{1,0:T(8,128)(2,1)S(1)}, u32[]{:S(2)}, u32[]{:S(2)}) collective-permute-start(bf16[400,256]{1,0:T(8,128)(2,1)S(1)} %add_convert_fusion.1), channel_id=1, source_target_pairs={{0,4},{1,17},{2,6},{3,19},{4,0},{5,21},{6,2},{7,23},{8,12},{9,25},... | collective-permute-start | bytes 614408 | tf_op jit(solution)/shard_map/ppermute | solution.py:411
  65.9 7.1 %collective-permute-start.14 = (bf16[400,256]{1,0:T(8,128)(2,1)S(1)}, bf16[400,256]{1,0:T(8,128)(2,1)S(1)}, u32[]{:S(2)}, u32[]{:S(2)}) collective-permute-start(bf16[400,256]{1,0:T(8,128)(2,1)S(1)} %add_convert_fusion.1), channel_id=1, source_target_pairs={{0,2},{1,9},{2,0},{3,11},{4,6},{5,13},{6,4},{7,15},{8,10},{9,1},{1... | collective-permute-start | bytes 614408 | tf_op jit(solution)/shard_map/ppermute | solution.py:411
  73.2 6.5 %collective-permute-start.18 = (bf16[400,256]{1,0:T(8,128)(2,1)S(1)}, bf16[400,256]{1,0:T(8,128)(2,1)S(1)}, u32[]{:S(2)}, u32[]{:S(2)}) collective-permute-start(bf16[400,256]{1,0:T(8,128)(2,1)S(1)} %add_add_fusion.1), channel_id=1, source_target_pairs={{0,16},{1,65},{2,18},{3,67},{4,20},{5,69},{6,22},{7,71},{8,24},{9,... | collective-permute-start | bytes 614408 | tf_op jit(solution)/shard_map/ppermute | solution.py:411
  75.4 5.9 %collective-permute-start.17 = (bf16[400,256]{1,0:T(8,128)(2,1)S(1)}, bf16[400,256]{1,0:T(8,128)(2,1)S(1)}, u32[]{:S(2)}, u32[]{:S(2)}) collective-permute-start(bf16[400,256]{1,0:T(8,128)(2,1)S(1)} %add_add_fusion.1), channel_id=1, source_target_pairs={{0,8},{1,33},{2,10},{3,35},{4,12},{5,37},{6,14},{7,39},{8,0},{9,41... | collective-permute-start | bytes 614408 | tf_op jit(solution)/shard_map/ppermute | solution.py:411
  75.7 6.1 %collective-permute-start.19 = (bf16[400,256]{1,0:T(8,128)(2,1)S(1)}, bf16[400,256]{1,0:T(8,128)(2,1)S(1)}, u32[]{:S(2)}, u32[]{:S(2)}) collective-permute-start(bf16[400,256]{1,0:T(8,128)(2,1)S(1)} %add_add_fusion.1), channel_id=1, source_target_pairs={{0,24},{1,97},{2,26},{3,99},{4,28},{5,101},{6,30},{7,103},{8,16},{... | collective-permute-start | bytes 614408 | tf_op jit(solution)/shard_map/ppermute | solution.py:411
  82.0 6.3 %collective-permute-start.21 = (bf16[400,256]{1,0:T(8,128)(2,1)S(1)}, bf16[400,256]{1,0:T(8,128)(2,1)S(1)}, u32[]{:S(2)}, u32[]{:S(2)}) collective-permute-start(bf16[400,256]{1,0:T(8,128)(2,1)S(1)} %add_add_fusion), channel_id=1, source_target_pairs={{0,64},{1,5},{2,66},{3,7},{4,68},{5,1},{6,70},{7,3},{8,72},{9,13},... | collective-permute-start | bytes 614408 | tf_op jit(solution)/shard_map/ppermute | solution.py:411
  83.8 5.6 %collective-permute-start.20 = (bf16[400,256]{1,0:T(8,128)(2,1)S(1)}, bf16[400,256]{1,0:T(8,128)(2,1)S(1)}, u32[]{:S(2)}, u32[]{:S(2)}) collective-permute-start(bf16[400,256]{1,0:T(8,128)(2,1)S(1)} %add_add_fusion), channel_id=1, source_target_pairs={{0,32},{1,3},{2,34},{3,1},{4,36},{5,7},{6,38},{7,5},{8,40},{9,11},... | collective-permute-start | bytes 614408 | tf_op jit(solution)/shard_map/ppermute | solution.py:411
  83.8 6.9 %collective-permute-start.22 = (bf16[400,256]{1,0:T(8,128)(2,1)S(1)}, bf16[400,256]{1,0:T(8,128)(2,1)S(1)}, u32[]{:S(2)}, u32[]{:S(2)}) collective-permute-start(bf16[400,256]{1,0:T(8,128)(2,1)S(1)} %add_add_fusion), channel_id=1, source_target_pairs={{0,96},{1,7},{2,98},{3,5},{4,100},{5,3},{6,102},{7,1},{8,104},{9,1... | collective-permute-start | bytes 614408 | tf_op jit(solution)/shard_map/ppermute | solution.py:411
  90.8 4.9 %collective-permute-start.23 = (bf16[400,256]{1,0:T(8,128)(2,1)S(1)}, bf16[400,256]{1,0:T(8,128)(2,1)S(1)}, u32[]{:S(2)}, u32[]{:S(2)}) collective-permute-start(bf16[400,256]{1,0:T(8,128)(2,1)S(1)} %add_convert_fusion.mine), channel_id=1, source_target_pairs={{0,1},{1,0},{2,3},{3,2},{4,5},{5,4},{6,7},{7,6},{8,9},{9,8},{10,11... | collective-permute-start | bytes 614408 | tf_op jit(solution)/shard_map/ppermute | solution.py:411
  (10 other events, 66.4 us)

commit v7 on v6

--- a/solution.py
+++ b/solution.py
@@ -21,7 +21,7 @@
 PAY2 = 800
 ORDER = (1, 2, 3)
 FT = HALF * BLOCK
-BT = 1024
+BT = ROWS
 BF = jnp.bfloat16
 F32 = jnp.float32
 HIGH = lax.Precision.HIGH
@@ -316,16 +316,8 @@
     core, mine, other, watt, normed, feat, mid, prob_in, aux, dmix, cot, gain, wfmt, bdt, wcol,
     res, send, keep, toks, an, ant, dd, gfm, gout, gsl, pay, gpay,
 ):
-    t = pl.program_id(0)
-
-    @pl.when(t == 0)
-    def _():
-        join_halves(core[0], mine, other, pay)
-        attention_step(pay, watt, an, ant, dd, toks)
-        gfm[...] = jnp.zeros_like(gfm)
-        gout[...] = jnp.zeros_like(gout)
-        gsl[...] = jnp.zeros_like(gsl)
-
+    join_halves(core[0], mine, other, pay)
+    attention_step(pay, watt, an, ant, dd, toks)
     mid_t = mid[...]
     weights = prob_in[...].astype(BF)
     prob = prob_in[...].reshape(HEADS, SLICES, BT)
@@ -350,33 +342,31 @@
     res[: 2 * C] = mixed_df
     res[2 * C :] = dm
     normed_here = normed[...]
-    gfm[:C] += dot(mixed_df[C:], normed_here)
-    gfm[C:] += dot(dm, normed_here)
-    gout[...] += dot(mixed_df[:C], cot[...])
+    gfm[:C] = dot(mixed_df[C:], normed_here)
+    gfm[C:] = dot(dm, normed_here)
+    gout[...] = dot(mixed_df[:C], cot[...])
     dt_hi = d_temper.astype(BF)
     dt_lo = (d_temper - dt_hi.astype(F32)).astype(BF)
-    gsl[:HS] += dot(d_raw, mid_t, NT)
-    gsl[HS:] += dot(jnp.concatenate([dt_hi, dt_lo], axis=0), mid_t, NT)
-
-    @pl.when(t == ROWS // BT - 1)
-    def _():
-        grad_fm = gfm[...]
-        gpay[: 2 * C] = grad_fm
-        gpay[2 * C : 3 * C] = gout[...]
-        rows = lax.broadcasted_iota(jnp.int32, (C, C), 0)
-        cols = lax.broadcasted_iota(jnp.int32, (C, C), 1)
-        over_heads = (rows % HEAD == cols % HEAD).astype(F32)
-        packed = jnp.where(packed_mask(), dot_high(fold_heads(gsl[:HS]), over_heads), 0.0)
-        gpay[3 * C : 3 * C + 8] = jnp.sum(packed.reshape(8, 8, C), axis=1)
-        grad_gain = jnp.sum(grad_fm * wfmt[...].astype(F32), axis=0, keepdims=True) / gain[...]
-        both = gsl[HS : HS + 8] + gsl[HS + 8 :]
-        row = lax.broadcasted_iota(jnp.int32, (8, C), 0)
-        lane_head = lax.broadcasted_iota(jnp.int32, (8, C), 1) // HEAD
-        temper_row = jnp.sum(jnp.where(row == lane_head, both, 0.0), axis=0, keepdims=True)
-        row = lax.broadcasted_iota(jnp.int32, (PAY2 - 3 * C - 8, C), 0)
-        tail = jnp.where(row == 0, grad_gain, jnp.where(row == 1, temper_row, 0.0))
-        gpay[3 * C + 8 :] = tail
-        split_halves(core[0], gpay, send, keep)
+    gsl[:HS] = dot(d_raw, mid_t, NT)
+    gsl[HS:] = dot(jnp.concatenate([dt_hi, dt_lo], axis=0), mid_t, NT)
+
+    grad_fm = gfm[...]
+    gpay[: 2 * C] = grad_fm
+    gpay[2 * C : 3 * C] = gout[...]
+    rows = lax.broadcasted_iota(jnp.int32, (C, C), 0)
+    cols = lax.broadcasted_iota(jnp.int32, (C, C), 1)
+    over_heads = (rows % HEAD == cols % HEAD).astype(F32)
+    packed = jnp.where(packed_mask(), dot_high(fold_heads(gsl[:HS]), over_heads), 0.0)
+    gpay[3 * C : 3 * C + 8] = jnp.sum(packed.reshape(8, 8, C), axis=1)
+    grad_gain = jnp.sum(grad_fm * wfmt[...].astype(F32), axis=0, keepdims=True) / gain[...]
+    both = gsl[HS : HS + 8] + gsl[HS + 8 :]
+    row = lax.broadcasted_iota(jnp.int32, (8, C), 0)
+    lane_head = lax.broadcasted_iota(jnp.int32, (8, C), 1) // HEAD
+    temper_row = jnp.sum(jnp.where(row == lane_head, both, 0.0), axis=0, keepdims=True)
+    row = lax.broadcasted_iota(jnp.int32, (PAY2 - 3 * C - 8, C), 0)
+    tail = jnp.where(row == 0, grad_gain, jnp.where(row == 1, temper_row, 0.0))
+    gpay[3 * C + 8 :] = tail
+    split_halves(core[0], gpay, send, keep)
 
 
 def out_kernel(ptsb, cot, res, gain, wfmt, wout, layer, grad):
@@ -446,7 +436,7 @@
 
 
 PARAMS = pltpu.CompilerParams(vmem_limit_bytes=24 * 1024 * 1024)
-BACK_PARAMS = pltpu.CompilerParams(vmem_limit_bytes=32 * 1024 * 1024)
+BACK_PARAMS = pltpu.CompilerParams(vmem_limit_bytes=36 * 1024 * 1024)
 SCALARS = pl.BlockSpec(memory_space=pltpu.SMEM)
 HBM = pl.BlockSpec(memory_space=pl.ANY)
 

time: 97 us -> 96.3 us (level)
  no operation moved by 1% of the time
where the time goes in v7:
time: 96.3 us; the launch traced here: 96.1 us
  starting transfers between devices  37.8 us (39%)
  waiting for transfers between devices  29.7 us (31%)
  Pallas kernels  25.8 us (27%)
  local copies, waits for them, and re-layouts  1.5 us (2%)
    ppermute x23, starting transfers between devices, swap(): lax.ppermute(array, 'pts', [(i, i ^ (odd if i % 2 else even)) for i in ra...  34.7 us
    ppermute x23, waiting for transfers between devices, swap(): lax.ppermute(array, 'pts', [(i, i ^ (odd if i % 2 else even)) for i in ra...  27.9 us
    pallas_call x1, Pallas kernels, per_device(): pl.pallas_call(back_kernel, grid=(ROWS // BT,), in_specs=[SCALARS] + [who...  8.25 us
    pallas_call x1, Pallas kernels, per_device(): pl.pallas_call(out_kernel, grid=(B_DEV,), in_specs=[rows_spec(C), rows_sp...  3.69 us
    pallas_call x1, Pallas kernels, per_device(): pl.pallas_call(front_second, grid_spec=pltpu.PrefetchScalarGridSpec(num_s...  3.64 us
    pallas_call x1, Pallas kernels, per_device(): pl.pallas_call(front_first, grid_spec=pltpu.PrefetchScalarGridSpec(num_sc...  3.44 us
    pallas_call x1, Pallas kernels, per_device(): pl.pallas_call(pick_kernel, grid_spec=pltpu.PrefetchScalarGridSpec(num_sc...  3.11 us
    ppermute x1, starting transfers between devices, neighbour_blocks(): got_outer = lax.ppermute(outer, 'pts', edges + [(j, i) for i, j in edges])  3.08 us
  transfers between devices with their start and end apart: 24, of which 19 were waited for; matrix products, arithmetic and copies ran while one was open for 0% of the time, Pallas kernels for 10%

profile of v7, /device:TPU:1, one launch (start us, length us, event | category | flops | bytes accessed | tf_op | source)
XLA Modules:
  0.0 96.1 jit_solution(16131197746217975635)
XLA Ops:
  0.7 3.1 %pick.1 = (s32[3,4]{1,0:T(4,128)}, bf16[1024,256]{1,0:T(8,128)(2,1)}, bf16[1024,256]{1,0:T(8,128)(2,1)}) custom-call(s32[1]{0:T(128)} %bitcast.rank, s32[128]{0:T(128)} %counts.1, s32[8]{0:T(128)} %table.1, bf16[4096,256]{1,0:T(8,128)(2,1)} %refs_1_.3, bf16[4096,256]{1,0:T(8,128)(2,1)} %refs_1_.3), custom_call_target="tpu_custom_call" | custom-call | tf_op jit(solution)/shard_map/pick/pallas_call | solution.py:461
  5.3 3.1 %collective-permute-start = (bf16[1024,256]{1,0:T(8,128)(2,1)}, bf16[1024,256]{1,0:T(8,128)(2,1)S(1)}, u32[]{:S(2)}, u32[]{:S(2)}) collective-permute-start(bf16[1024,256]{1,0:T(8,128)(2,1)} %get-tuple-element.55), channel_id=1, source_target_pairs={{1,2},{3,4},{5,6},{7,8},{9,10},{11,12},{13,14},{15,16},{17,18},{19... | collective-permute-start | bytes 1572872 | tf_op jit(solution)/shard_map/ppermute | solution.py:426
  10.7 3.4 %front_first.1 = (bf16[2048,256]{1,0:T(8,128)(2,1)S(1)}, bf16[2048,256]{1,0:T(8,128)(2,1)S(1)}, bf16[2048,256]{1,0:T(8,128)(2,1)S(1)}, bf16[256,2048]{1,0:T(8,12...) custom-call(s32[3,4]{1,0:T(4,128)S(1)} %copy-done.8, s32[1]{0:T(128)S(6)} %rem.18.core, ...), custom_call_target="tpu_custom_call" | custom-call | flops 805306368 | bytes 6291456 | tf_op jit(solution)/shard_map/front_first/pallas_call | solution.py:537
  14.2 1.8 %collective-permute-done.refs_2_.refs_3_ = bf16[1024,256]{1,0:T(8,128)(2,1)S(1)} collective-permute-done((bf16[1024,256]{1,0:T(8,128)(2,1)}, bf16[1024,256]{1,0:T(8,128)(2,1)S(1)}, u32[]{:S(2)}, u32[]{:S(2)}) %collective-permute-start) | collective-permute-done | bytes 524320 | tf_op jit(solution)/shard_map/ppermute | solution.py:426
  16.0 3.6 %front_second.1 = (bf16[2048,256]{1,0:T(8,128)(2,1)S(1)}, bf16[2048,256]{1,0:T(8,128)(2,1)S(1)}, bf16[2048,256]{1,0:T(8,128)(2,1)S(1)}, bf16[256,2048]{1,0:T(8,1...) custom-call(s32[3,4]{1,0:T(4,128)S(1)} %copy-done.8, ...), custom_call_target="tpu_custom_call", output_to_operand_aliasing={{0}: (12, {}), {1}: (13, {}), {2}: (14, {}), {3}: (15, {}),... | custom-call | tf_op jit(solution)/shard_map/front_second/pallas_call | solution.py:555
  21.0 5.7 %collective-permute-start.5 = (f32[32,640]{1,0:T(8,128)S(1)}, f32[32,640]{1,0:T(8,128)S(1)}, u32[]{:S(2)}, u32[]{:S(2)}) collective-permute-start(f32[32,640]{1,0:T(8,128)S(1)} %add.60), channel_id=1, source_target_pairs={{0,6},{1,25},{2,4},{3,27},{4,2},{5,29},{6,0},{7,31},{8,14},{9,17},... | collective-permute-start | bytes 245768 | tf_op jit(solution)/shard_map/ppermute | solution.py:401
  27.3 1.6 %collective-permute-done.5 = f32[32,640]{1,0:T(8,128)S(1)} collective-permute-done((f32[32,640]{1,0:T(8,128)S(1)}, f32[32,640]{1,0:T(8,128)S(1)}, u32[]{:S(2)}, u32[]{:S(2)}) %collective-permute-start.5) | collective-permute-done | bytes 81952 | tf_op jit(solution)/shard_map/ppermute | solution.py:401
  28.9 2.8 %collective-permute-done.4 = f32[32,640]{1,0:T(8,128)S(1)} collective-permute-done((f32[32,640]{1,0:T(8,128)S(1)}, f32[32,640]{1,0:T(8,128)S(1)}, u32[]{:S(2)}, u32[]{:S(2)}) %collective-permute-start.4) | collective-permute-done | bytes 81952 | tf_op jit(solution)/shard_map/ppermute | solution.py:401
  31.7 2.9 %collective-permute-start.8 = (f32[32,640]{1,0:T(8,128)S(1)}, f32[32,640]{1,0:T(8,128)S(1)}, u32[]{:S(2)}, u32[]{:S(2)}) collective-permute-start(f32[32,640]{1,0:T(8,128)S(1)} %add_add_fusion.4), channel_id=1, source_target_pairs={{0,24},{1,97},{2,26},{3,99},{4,28},{5,101},{6,30},{7,103},{8,16},{... | collective-permute-start | bytes 245768 | tf_op jit(solution)/shard_map/ppermute | solution.py:401
  35.3 1.6 %collective-permute-done.8 = f32[32,640]{1,0:T(8,128)S(1)} collective-permute-done((f32[32,640]{1,0:T(8,128)S(1)}, f32[32,640]{1,0:T(8,128)S(1)}, u32[]{:S(2)}, u32[]{:S(2)}) %collective-permute-start.8) | collective-permute-done | bytes 81952 | tf_op jit(solution)/shard_map/ppermute | solution.py:401
  36.9 2.5 %collective-permute-done.7 = f32[32,640]{1,0:T(8,128)S(1)} collective-permute-done((f32[32,640]{1,0:T(8,128)S(1)}, f32[32,640]{1,0:T(8,128)S(1)}, u32[]{:S(2)}, u32[]{:S(2)}) %collective-permute-start.7) | collective-permute-done | bytes 81952 | tf_op jit(solution)/shard_map/ppermute | solution.py:401
  39.5 3.8 %collective-permute-start.11 = (f32[32,640]{1,0:T(8,128)S(1)}, f32[32,640]{1,0:T(8,128)S(1)}, u32[]{:S(2)}, u32[]{:S(2)}) collective-permute-start(f32[32,640]{1,0:T(8,128)S(1)} %add_add_fusion.3), channel_id=1, source_target_pairs={{0,96},{1,7},{2,98},{3,5},{4,100},{5,3},{6,102},{7,1},{8,104},{9,1... | collective-permute-start | bytes 245768 | tf_op jit(solution)/shard_map/ppermute | solution.py:401
  44.0 1.6 %collective-permute-done.11 = f32[32,640]{1,0:T(8,128)S(1)} collective-permute-done((f32[32,640]{1,0:T(8,128)S(1)}, f32[32,640]{1,0:T(8,128)S(1)}, u32[]{:S(2)}, u32[]{:S(2)}) %collective-permute-start.11) | collective-permute-done | bytes 81952 | tf_op jit(solution)/shard_map/ppermute | solution.py:401
  45.5 2.5 %collective-permute-done.10 = f32[32,640]{1,0:T(8,128)S(1)} collective-permute-done((f32[32,640]{1,0:T(8,128)S(1)}, f32[32,640]{1,0:T(8,128)S(1)}, u32[]{:S(2)}, u32[]{:S(2)}) %collective-permute-start.10) | collective-permute-done | bytes 81952 | tf_op jit(solution)/shard_map/ppermute | solution.py:401
  48.1 4.5 %collective-permute-start.12 = (f32[32,640]{1,0:T(8,128)S(1)}, f32[32,640]{1,0:T(8,128)S(1)}, u32[]{:S(2)}, u32[]{:S(2)}) collective-permute-start(f32[32,640]{1,0:T(8,128)S(1)} %add_add_fusion.2.mine), channel_id=1, source_target_pairs={{0,1},{1,0},{2,3},{3,2},{4,5},{5,4},{6,7},{7,6},{8,9},{9,8},{10,11... | collective-permute-start | bytes 245768 | tf_op jit(solution)/shard_map/ppermute | solution.py:401
  53.5 8.2 %back.1 = (bf16[768,2048]{1,0:T(8,128)(2,1)S(1)}, bf16[400,256]{1,0:T(8,128)(2,1)S(1)}, f32[400,256]{1,0:T(8,128)S(1)}, f32[4,64,256]{2,1,0:T(8,128)S(1)}) custom-call(s32[1]{0:T(128)S(6)} %rem.18.core, f32[32,640]{1,0:T(8,128)S(1)} %add_add_fusion.2.mine, f32[32,640]{1,0:T(8,128)S(1)} %collective-permute-done.12.other, ...), custom_call_target="tpu_custom_call" | custom-call | tf_op jit(solution)/shard_map/back/pallas_call | solution.py:578
  66.7 3.7 %outputs.1 = (bf16[2048,256]{1,0:T(8,128)(2,1)}, bf16[2048,256]{1,0:T(8,128)(2,1)}) custom-call(bf16[2048,256]{1,0:T(8,128)(2,1)S(1)} %get-tuple-element.83.ptsb, bf16[2048,256]{1,0:T(8,128)(2,1)S(1)} %copy-done.1, bf16[768,2048]{1,0:T(8,128)(2,1)S(1)} %get-tuple-element.84.res, f32[1,256]{1,0:T(1,128)S(1)} %bitcast.8, ...), custom_call_target="tpu_custom_call" | custom-call | flops 805306368 | bytes 7340032 | tf_op jit(solution)/shard_map/outputs/pallas_call | solution.py:622
  72.5 2.3 %collective-permute-start.18 = (bf16[400,256]{1,0:T(8,128)(2,1)S(1)}, bf16[400,256]{1,0:T(8,128)(2,1)S(1)}, u32[]{:S(2)}, u32[]{:S(2)}) collective-permute-start(bf16[400,256]{1,0:T(8,128)(2,1)S(1)} %add_add_fusion.1), channel_id=1, source_target_pairs={{0,16},{1,65},{2,18},{3,67},{4,20},{5,69},{6,22},{7,71},{8,24},{9,... | collective-permute-start | bytes 614408 | tf_op jit(solution)/shard_map/ppermute | solution.py:401
  75.8 1.7 %attend_grads.1 = f32[3,32,32]{2,1,0:T(8,128)} custom-call(f32[4,64,256]{2,1,0:T(8,128)S(1)} %get-tuple-element.90.toks), custom_call_target="tpu_custom_call" | custom-call | tf_op jit(solution)/shard_map/attend_grads/pallas_call | solution.py:642
  79.0 1.7 %collective-permute-done.17 = bf16[400,256]{1,0:T(8,128)(2,1)S(1)} collective-permute-done((bf16[400,256]{1,0:T(8,128)(2,1)S(1)}, bf16[400,256]{1,0:T(8,128)(2,1)S(1)}, u32[]{:S(2)}, u32[]{:S(2)}) %collective-permute-start.17) | collective-permute-done | bytes 204832 | tf_op jit(solution)/shard_map/ppermute | solution.py:401
  81.3 1.8 %collective-permute-start.21 = (bf16[400,256]{1,0:T(8,128)(2,1)S(1)}, bf16[400,256]{1,0:T(8,128)(2,1)S(1)}, u32[]{:S(2)}, u32[]{:S(2)}) collective-permute-start(bf16[400,256]{1,0:T(8,128)(2,1)S(1)} %add_add_fusion), channel_id=1, source_target_pairs={{0,64},{1,5},{2,66},{3,7},{4,68},{5,1},{6,70},{7,3},{8,72},{9,13},... | collective-permute-start | bytes 614408 | tf_op jit(solution)/shard_map/ppermute | solution.py:401
  83.1 1.5 %collective-permute-start.22 = (bf16[400,256]{1,0:T(8,128)(2,1)S(1)}, bf16[400,256]{1,0:T(8,128)(2,1)S(1)}, u32[]{:S(2)}, u32[]{:S(2)}) collective-permute-start(bf16[400,256]{1,0:T(8,128)(2,1)S(1)} %add_add_fusion), channel_id=1, source_target_pairs={{0,96},{1,7},{2,98},{3,5},{4,100},{5,3},{6,102},{7,1},{8,104},{9,1... | collective-permute-start | bytes 614408 | tf_op jit(solution)/shard_map/ppermute | solution.py:401
  84.6 2.9 %collective-permute-done.21 = bf16[400,256]{1,0:T(8,128)(2,1)S(1)} collective-permute-done((bf16[400,256]{1,0:T(8,128)(2,1)S(1)}, bf16[400,256]{1,0:T(8,128)(2,1)S(1)}, u32[]{:S(2)}, u32[]{:S(2)}) %collective-permute-start.21) | collective-permute-done | bytes 204832 | tf_op jit(solution)/shard_map/ppermute | solution.py:401
  90.1 3.8 %collective-permute-start.23 = (bf16[400,256]{1,0:T(8,128)(2,1)S(1)}, bf16[400,256]{1,0:T(8,128)(2,1)S(1)}, u32[]{:S(2)}, u32[]{:S(2)}) collective-permute-start(bf16[400,256]{1,0:T(8,128)(2,1)S(1)} %add_convert_fusion.mine), channel_id=1, source_target_pairs={{0,1},{1,0},{2,3},{3,2},{4,5},{5,4},{6,7},{7,6},{8,9},{9,8},{10,11... | collective-permute-start | bytes 614408 | tf_op jit(solution)/shard_map/ppermute | solution.py:401
  (61 shorter events, 22.9 us)
Async XLA Ops:
  3.8 6.2 %collective-permute-start.1 = (bf16[1024,256]{1,0:T(8,128)(2,1)}, bf16[1024,256]{1,0:T(8,128)(2,1)S(1)}, u32[]{:S(2)}, u32[]{:S(2)}) collective-permute-start(bf16[1024,256]{1,0:T(8,128)(2,1)} %get-tuple-element.59), channel_id=1, source_target_pairs={{0,1},{1,0},{2,3},{3,2},{4,5},{5,4},{6,7},{7,6},{8,9},{9,8},{10,11... | collective-permute-start | bytes 1572872 | tf_op jit(solution)/shard_map/ppermute | solution.py:401
  5.3 10.7 %collective-permute-start = (bf16[1024,256]{1,0:T(8,128)(2,1)}, bf16[1024,256]{1,0:T(8,128)(2,1)S(1)}, u32[]{:S(2)}, u32[]{:S(2)}) collective-permute-start(bf16[1024,256]{1,0:T(8,128)(2,1)} %get-tuple-element.55), channel_id=1, source_target_pairs={{1,2},{3,4},{5,6},{7,8},{9,10},{11,12},{13,14},{15,16},{17,18},{19... | collective-permute-start | bytes 1572872 | tf_op jit(solution)/shard_map/ppermute | solution.py:426
  19.6 1.4 %collective-permute-start.2 = (f32[32,640]{1,0:T(8,128)S(1)}, f32[32,640]{1,0:T(8,128)S(1)}, u32[]{:S(2)}, u32[]{:S(2)}) collective-permute-start(f32[32,640]{1,0:T(8,128)S(1)} %get-tuple-element.72), channel_id=1, source_target_pairs={{0,1},{1,0},{2,3},{3,2},{4,5},{5,4},{6,7},{7,6},{8,9},{9,8},{10,11... | collective-permute-start | bytes 245768 | tf_op jit(solution)/shard_map/ppermute | solution.py:401
  21.0 7.9 %collective-permute-start.5 = (f32[32,640]{1,0:T(8,128)S(1)}, f32[32,640]{1,0:T(8,128)S(1)}, u32[]{:S(2)}, u32[]{:S(2)}) collective-permute-start(f32[32,640]{1,0:T(8,128)S(1)} %add.60), channel_id=1, source_target_pairs={{0,6},{1,25},{2,4},{3,27},{4,2},{5,29},{6,0},{7,31},{8,14},{9,17},... | collective-permute-start | bytes 245768 | tf_op jit(solution)/shard_map/ppermute | solution.py:401
  26.7 5.1 %collective-permute-start.4 = (f32[32,640]{1,0:T(8,128)S(1)}, f32[32,640]{1,0:T(8,128)S(1)}, u32[]{:S(2)}, u32[]{:S(2)}) collective-permute-start(f32[32,640]{1,0:T(8,128)S(1)} %add.60), channel_id=1, source_target_pairs={{0,4},{1,17},{2,6},{3,19},{4,0},{5,21},{6,2},{7,23},{8,12},{9,25},... | collective-permute-start | bytes 245768 | tf_op jit(solution)/shard_map/ppermute | solution.py:401
  26.7 5.1 %collective-permute-start.3 = (f32[32,640]{1,0:T(8,128)S(1)}, f32[32,640]{1,0:T(8,128)S(1)}, u32[]{:S(2)}, u32[]{:S(2)}) collective-permute-start(f32[32,640]{1,0:T(8,128)S(1)} %add.60), channel_id=1, source_target_pairs={{0,2},{1,9},{2,0},{3,11},{4,6},{5,13},{6,4},{7,15},{8,10},{9,1},{1... | collective-permute-start | bytes 245768 | tf_op jit(solution)/shard_map/ppermute | solution.py:401
  31.7 5.2 %collective-permute-start.8 = (f32[32,640]{1,0:T(8,128)S(1)}, f32[32,640]{1,0:T(8,128)S(1)}, u32[]{:S(2)}, u32[]{:S(2)}) collective-permute-start(f32[32,640]{1,0:T(8,128)S(1)} %add_add_fusion.4), channel_id=1, source_target_pairs={{0,24},{1,97},{2,26},{3,99},{4,28},{5,101},{6,30},{7,103},{8,16},{... | collective-permute-start | bytes 245768 | tf_op jit(solution)/shard_map/ppermute | solution.py:401
  34.7 4.8 %collective-permute-start.7 = (f32[32,640]{1,0:T(8,128)S(1)}, f32[32,640]{1,0:T(8,128)S(1)}, u32[]{:S(2)}, u32[]{:S(2)}) collective-permute-start(f32[32,640]{1,0:T(8,128)S(1)} %add_add_fusion.4), channel_id=1, source_target_pairs={{0,16},{1,65},{2,18},{3,67},{4,20},{5,69},{6,22},{7,71},{8,24},{9,... | collective-permute-start | bytes 245768 | tf_op jit(solution)/shard_map/ppermute | solution.py:401
  34.9 4.6 %collective-permute-start.6 = (f32[32,640]{1,0:T(8,128)S(1)}, f32[32,640]{1,0:T(8,128)S(1)}, u32[]{:S(2)}, u32[]{:S(2)}) collective-permute-start(f32[32,640]{1,0:T(8,128)S(1)} %add_add_fusion.4), channel_id=1, source_target_pairs={{0,8},{1,33},{2,10},{3,35},{4,12},{5,37},{6,14},{7,39},{8,0},{9,41... | collective-permute-start | bytes 245768 | tf_op jit(solution)/shard_map/ppermute | solution.py:401
  39.5 6.0 %collective-permute-start.11 = (f32[32,640]{1,0:T(8,128)S(1)}, f32[32,640]{1,0:T(8,128)S(1)}, u32[]{:S(2)}, u32[]{:S(2)}) collective-permute-start(f32[32,640]{1,0:T(8,128)S(1)} %add_add_fusion.3), channel_id=1, source_target_pairs={{0,96},{1,7},{2,98},{3,5},{4,100},{5,3},{6,102},{7,1},{8,104},{9,1... | collective-permute-start | bytes 245768 | tf_op jit(solution)/shard_map/ppermute | solution.py:401
  43.3 4.8 %collective-permute-start.10 = (f32[32,640]{1,0:T(8,128)S(1)}, f32[32,640]{1,0:T(8,128)S(1)}, u32[]{:S(2)}, u32[]{:S(2)}) collective-permute-start(f32[32,640]{1,0:T(8,128)S(1)} %add_add_fusion.3), channel_id=1, source_target_pairs={{0,64},{1,5},{2,66},{3,7},{4,68},{5,1},{6,70},{7,3},{8,72},{9,13},... | collective-permute-start | bytes 245768 | tf_op jit(solution)/shard_map/ppermute | solution.py:401
  43.3 4.8 %collective-permute-start.9 = (f32[32,640]{1,0:T(8,128)S(1)}, f32[32,640]{1,0:T(8,128)S(1)}, u32[]{:S(2)}, u32[]{:S(2)}) collective-permute-start(f32[32,640]{1,0:T(8,128)S(1)} %add_add_fusion.3), channel_id=1, source_target_pairs={{0,32},{1,3},{2,34},{3,1},{4,36},{5,7},{6,38},{7,5},{8,40},{9,11},... | collective-permute-start | bytes 245768 | tf_op jit(solution)/shard_map/ppermute | solution.py:401
  48.1 5.4 %collective-permute-start.12 = (f32[32,640]{1,0:T(8,128)S(1)}, f32[32,640]{1,0:T(8,128)S(1)}, u32[]{:S(2)}, u32[]{:S(2)}) collective-permute-start(f32[32,640]{1,0:T(8,128)S(1)} %add_add_fusion.2.mine), channel_id=1, source_target_pairs={{0,1},{1,0},{2,3},{3,2},{4,5},{5,4},{6,7},{7,6},{8,9},{9,8},{10,11... | collective-permute-start | bytes 245768 | tf_op jit(solution)/shard_map/ppermute | solution.py:401
  61.8 1.5 %collective-permute-start.13 = (bf16[400,256]{1,0:T(8,128)(2,1)S(1)}, bf16[400,256]{1,0:T(8,128)(2,1)S(1)}, u32[]{:S(2)}, u32[]{:S(2)}) collective-permute-start(bf16[400,256]{1,0:T(8,128)(2,1)S(1)} %get-tuple-element.82), channel_id=1, source_target_pairs={{0,1},{1,0},{2,3},{3,2},{4,5},{5,4},{6,7},{7,6},{8,9},{9,8},{10,11... | collective-permute-start | bytes 614408 | tf_op jit(solution)/shard_map/ppermute | solution.py:401
  63.4 8.4 %collective-permute-start.16 = (bf16[400,256]{1,0:T(8,128)(2,1)S(1)}, bf16[400,256]{1,0:T(8,128)(2,1)S(1)}, u32[]{:S(2)}, u32[]{:S(2)}) collective-permute-start(bf16[400,256]{1,0:T(8,128)(2,1)S(1)} %add_convert_fusion.1), channel_id=1, source_target_pairs={{0,6},{1,25},{2,4},{3,27},{4,2},{5,29},{6,0},{7,31},{8,14},{9,17},... | collective-permute-start | bytes 614408 | tf_op jit(solution)/shard_map/ppermute | solution.py:401
  64.6 7.1 %collective-permute-start.15 = (bf16[400,256]{1,0:T(8,128)(2,1)S(1)}, bf16[400,256]{1,0:T(8,128)(2,1)S(1)}, u32[]{:S(2)}, u32[]{:S(2)}) collective-permute-start(bf16[400,256]{1,0:T(8,128)(2,1)S(1)} %add_convert_fusion.1), channel_id=1, source_target_pairs={{0,4},{1,17},{2,6},{3,19},{4,0},{5,21},{6,2},{7,23},{8,12},{9,25},... | collective-permute-start | bytes 614408 | tf_op jit(solution)/shard_map/ppermute | solution.py:401
  65.3 7.1 %collective-permute-start.14 = (bf16[400,256]{1,0:T(8,128)(2,1)S(1)}, bf16[400,256]{1,0:T(8,128)(2,1)S(1)}, u32[]{:S(2)}, u32[]{:S(2)}) collective-permute-start(bf16[400,256]{1,0:T(8,128)(2,1)S(1)} %add_convert_fusion.1), channel_id=1, source_target_pairs={{0,2},{1,9},{2,0},{3,11},{4,6},{5,13},{6,4},{7,15},{8,10},{9,1},{1... | collective-permute-start | bytes 614408 | tf_op jit(solution)/shard_map/ppermute | solution.py:401
  72.5 6.5 %collective-permute-start.18 = (bf16[400,256]{1,0:T(8,128)(2,1)S(1)}, bf16[400,256]{1,0:T(8,128)(2,1)S(1)}, u32[]{:S(2)}, u32[]{:S(2)}) collective-permute-start(bf16[400,256]{1,0:T(8,128)(2,1)S(1)} %add_add_fusion.1), channel_id=1, source_target_pairs={{0,16},{1,65},{2,18},{3,67},{4,20},{5,69},{6,22},{7,71},{8,24},{9,... | collective-permute-start | bytes 614408 | tf_op jit(solution)/shard_map/ppermute | solution.py:401
  74.8 5.9 %collective-permute-start.17 = (bf16[400,256]{1,0:T(8,128)(2,1)S(1)}, bf16[400,256]{1,0:T(8,128)(2,1)S(1)}, u32[]{:S(2)}, u32[]{:S(2)}) collective-permute-start(bf16[400,256]{1,0:T(8,128)(2,1)S(1)} %add_add_fusion.1), channel_id=1, source_target_pairs={{0,8},{1,33},{2,10},{3,35},{4,12},{5,37},{6,14},{7,39},{8,0},{9,41... | collective-permute-start | bytes 614408 | tf_op jit(solution)/shard_map/ppermute | solution.py:401
  75.1 6.1 %collective-permute-start.19 = (bf16[400,256]{1,0:T(8,128)(2,1)S(1)}, bf16[400,256]{1,0:T(8,128)(2,1)S(1)}, u32[]{:S(2)}, u32[]{:S(2)}) collective-permute-start(bf16[400,256]{1,0:T(8,128)(2,1)S(1)} %add_add_fusion.1), channel_id=1, source_target_pairs={{0,24},{1,97},{2,26},{3,99},{4,28},{5,101},{6,30},{7,103},{8,16},{... | collective-permute-start | bytes 614408 | tf_op jit(solution)/shard_map/ppermute | solution.py:401
  81.3 6.3 %collective-permute-start.21 = (bf16[400,256]{1,0:T(8,128)(2,1)S(1)}, bf16[400,256]{1,0:T(8,128)(2,1)S(1)}, u32[]{:S(2)}, u32[]{:S(2)}) collective-permute-start(bf16[400,256]{1,0:T(8,128)(2,1)S(1)} %add_add_fusion), channel_id=1, source_target_pairs={{0,64},{1,5},{2,66},{3,7},{4,68},{5,1},{6,70},{7,3},{8,72},{9,13},... | collective-permute-start | bytes 614408 | tf_op jit(solution)/shard_map/ppermute | solution.py:401
  83.1 5.6 %collective-permute-start.20 = (bf16[400,256]{1,0:T(8,128)(2,1)S(1)}, bf16[400,256]{1,0:T(8,128)(2,1)S(1)}, u32[]{:S(2)}, u32[]{:S(2)}) collective-permute-start(bf16[400,256]{1,0:T(8,128)(2,1)S(1)} %add_add_fusion), channel_id=1, source_target_pairs={{0,32},{1,3},{2,34},{3,1},{4,36},{5,7},{6,38},{7,5},{8,40},{9,11},... | collective-permute-start | bytes 614408 | tf_op jit(solution)/shard_map/ppermute | solution.py:401
  83.1 6.8 %collective-permute-start.22 = (bf16[400,256]{1,0:T(8,128)(2,1)S(1)}, bf16[400,256]{1,0:T(8,128)(2,1)S(1)}, u32[]{:S(2)}, u32[]{:S(2)}) collective-permute-start(bf16[400,256]{1,0:T(8,128)(2,1)S(1)} %add_add_fusion), channel_id=1, source_target_pairs={{0,96},{1,7},{2,98},{3,5},{4,100},{5,3},{6,102},{7,1},{8,104},{9,1... | collective-permute-start | bytes 614408 | tf_op jit(solution)/shard_map/ppermute | solution.py:401
  90.1 4.9 %collective-permute-start.23 = (bf16[400,256]{1,0:T(8,128)(2,1)S(1)}, bf16[400,256]{1,0:T(8,128)(2,1)S(1)}, u32[]{:S(2)}, u32[]{:S(2)}) collective-permute-start(bf16[400,256]{1,0:T(8,128)(2,1)S(1)} %add_convert_fusion.mine), channel_id=1, source_target_pairs={{0,1},{1,0},{2,3},{3,2},{4,5},{5,4},{6,7},{7,6},{8,9},{9,8},{10,11... | collective-permute-start | bytes 614408 | tf_op jit(solution)/shard_map/ppermute | solution.py:401
  (10 other events, 66.4 us)

commit v8 on v7

--- a/solution.py
+++ b/solution.py
@@ -619,18 +619,19 @@
         bdt, wcol,
     )
 
+    out_rows = pl.BlockSpec((FT, C), lambda t: (t, 0))
     layer_out, grad_points = pl.pallas_call(
         out_kernel,
-        grid=(B_DEV,),
+        grid=(ROWS // FT,),
         in_specs=[
-            rows_spec(C),
-            rows_spec(C),
-            pl.BlockSpec((3 * C, BLOCK), lambda t: (0, t)),
+            out_rows,
+            out_rows,
+            pl.BlockSpec((3 * C, FT), lambda t: (0, t)),
             whole((1, C)),
             whole((2 * C, C)),
             whole((C, C)),
         ],
-        out_specs=[rows_spec(C)] * 2,
+        out_specs=[out_rows] * 2,
         out_shape=[wide] * 2,
         compiler_params=PARAMS,
         cost_estimate=pl.CostEstimate(

time: 96.3 us -> 96.3 us (level)
  no operation moved by 1% of the time
where the time goes in v8:
time: 96.3 us; the launch traced here: 96.1 us
  starting transfers between devices  37.8 us (39%)
  waiting for transfers between devices  29.8 us (31%)
  Pallas kernels  25.7 us (27%)
  local copies, waits for them, and re-layouts  1.5 us (2%)
    ppermute x23, starting transfers between devices, swap(): lax.ppermute(array, 'pts', [(i, i ^ (odd if i % 2 else even)) for i in ra...  34.7 us
    ppermute x23, waiting for transfers between devices, swap(): lax.ppermute(array, 'pts', [(i, i ^ (odd if i % 2 else even)) for i in ra...  28 us
    pallas_call x1, Pallas kernels, per_device(): pl.pallas_call(back_kernel, grid=(ROWS // BT,), in_specs=[SCALARS] + [who...  8.25 us
    pallas_call x1, Pallas kernels, per_device(): pl.pallas_call(front_second, grid_spec=pltpu.PrefetchScalarGridSpec(num_s...  3.64 us
    pallas_call x1, Pallas kernels, per_device(): pl.pallas_call(out_kernel, grid=(ROWS // FT,), in_specs=[out_rows, out_ro...  3.62 us
    pallas_call x1, Pallas kernels, per_device(): pl.pallas_call(front_first, grid_spec=pltpu.PrefetchScalarGridSpec(num_sc...  3.44 us
    pallas_call x1, Pallas kernels, per_device(): pl.pallas_call(pick_kernel, grid_spec=pltpu.PrefetchScalarGridSpec(num_sc...  3.11 us
    ppermute x1, starting transfers between devices, neighbour_blocks(): got_outer = lax.ppermute(outer, 'pts', edges + [(j, i) for i, j in edges])  3.08 us
  transfers between devices with their start and end apart: 24, of which 19 were waited for; matrix products, arithmetic and copies ran while one was open for 0% of the time, Pallas kernels for 10%

profile of v8, /device:TPU:1, one launch (start us, length us, event | category | flops | bytes accessed | tf_op | source)
XLA Modules:
  0.0 96.1 jit_solution(6108764708275020402)
XLA Ops:
  0.7 3.1 %pick.1 = (s32[3,4]{1,0:T(4,128)}, bf16[1024,256]{1,0:T(8,128)(2,1)}, bf16[1024,256]{1,0:T(8,128)(2,1)}) custom-call(s32[1]{0:T(128)} %bitcast.rank, s32[128]{0:T(128)} %counts.1, s32[8]{0:T(128)} %table.1, bf16[4096,256]{1,0:T(8,128)(2,1)} %refs_1_.3, bf16[4096,256]{1,0:T(8,128)(2,1)} %refs_1_.3), custom_call_target="tpu_custom_call" | custom-call | tf_op jit(solution)/shard_map/pick/pallas_call | solution.py:461
  5.3 3.1 %collective-permute-start = (bf16[1024,256]{1,0:T(8,128)(2,1)}, bf16[1024,256]{1,0:T(8,128)(2,1)S(1)}, u32[]{:S(2)}, u32[]{:S(2)}) collective-permute-start(bf16[1024,256]{1,0:T(8,128)(2,1)} %get-tuple-element.55), channel_id=1, source_target_pairs={{1,2},{3,4},{5,6},{7,8},{9,10},{11,12},{13,14},{15,16},{17,18},{19... | collective-permute-start | bytes 1572872 | tf_op jit(solution)/shard_map/ppermute | solution.py:426
  10.7 3.4 %front_first.1 = (bf16[2048,256]{1,0:T(8,128)(2,1)S(1)}, bf16[2048,256]{1,0:T(8,128)(2,1)S(1)}, bf16[2048,256]{1,0:T(8,128)(2,1)S(1)}, bf16[256,2048]{1,0:T(8,12...) custom-call(s32[3,4]{1,0:T(4,128)S(1)} %copy-done.8, s32[1]{0:T(128)S(6)} %rem.18.core, ...), custom_call_target="tpu_custom_call" | custom-call | flops 805306368 | bytes 6291456 | tf_op jit(solution)/shard_map/front_first/pallas_call | solution.py:537
  14.2 1.8 %collective-permute-done.refs_2_.refs_3_ = bf16[1024,256]{1,0:T(8,128)(2,1)S(1)} collective-permute-done((bf16[1024,256]{1,0:T(8,128)(2,1)}, bf16[1024,256]{1,0:T(8,128)(2,1)S(1)}, u32[]{:S(2)}, u32[]{:S(2)}) %collective-permute-start) | collective-permute-done | bytes 524320 | tf_op jit(solution)/shard_map/ppermute | solution.py:426
  16.0 3.6 %front_second.1 = (bf16[2048,256]{1,0:T(8,128)(2,1)S(1)}, bf16[2048,256]{1,0:T(8,128)(2,1)S(1)}, bf16[2048,256]{1,0:T(8,128)(2,1)S(1)}, bf16[256,2048]{1,0:T(8,1...) custom-call(s32[3,4]{1,0:T(4,128)S(1)} %copy-done.8, ...), custom_call_target="tpu_custom_call", output_to_operand_aliasing={{0}: (12, {}), {1}: (13, {}), {2}: (14, {}), {3}: (15, {}),... | custom-call | tf_op jit(solution)/shard_map/front_second/pallas_call | solution.py:555
  21.0 5.7 %collective-permute-start.5 = (f32[32,640]{1,0:T(8,128)S(1)}, f32[32,640]{1,0:T(8,128)S(1)}, u32[]{:S(2)}, u32[]{:S(2)}) collective-permute-start(f32[32,640]{1,0:T(8,128)S(1)} %add.60), channel_id=1, source_target_pairs={{0,6},{1,25},{2,4},{3,27},{4,2},{5,29},{6,0},{7,31},{8,14},{9,17},... | collective-permute-start | bytes 245768 | tf_op jit(solution)/shard_map/ppermute | solution.py:401
  27.3 1.6 %collective-permute-done.5 = f32[32,640]{1,0:T(8,128)S(1)} collective-permute-done((f32[32,640]{1,0:T(8,128)S(1)}, f32[32,640]{1,0:T(8,128)S(1)}, u32[]{:S(2)}, u32[]{:S(2)}) %collective-permute-start.5) | collective-permute-done | bytes 81952 | tf_op jit(solution)/shard_map/ppermute | solution.py:401
  28.9 2.8 %collective-permute-done.4 = f32[32,640]{1,0:T(8,128)S(1)} collective-permute-done((f32[32,640]{1,0:T(8,128)S(1)}, f32[32,640]{1,0:T(8,128)S(1)}, u32[]{:S(2)}, u32[]{:S(2)}) %collective-permute-start.4) | collective-permute-done | bytes 81952 | tf_op jit(solution)/shard_map/ppermute | solution.py:401
  31.7 2.9 %collective-permute-start.8 = (f32[32,640]{1,0:T(8,128)S(1)}, f32[32,640]{1,0:T(8,128)S(1)}, u32[]{:S(2)}, u32[]{:S(2)}) collective-permute-start(f32[32,640]{1,0:T(8,128)S(1)} %add_add_fusion.4), channel_id=1, source_target_pairs={{0,24},{1,97},{2,26},{3,99},{4,28},{5,101},{6,30},{7,103},{8,16},{... | collective-permute-start | bytes 245768 | tf_op jit(solution)/shard_map/ppermute | solution.py:401
  35.3 1.6 %collective-permute-done.8 = f32[32,640]{1,0:T(8,128)S(1)} collective-permute-done((f32[32,640]{1,0:T(8,128)S(1)}, f32[32,640]{1,0:T(8,128)S(1)}, u32[]{:S(2)}, u32[]{:S(2)}) %collective-permute-start.8) | collective-permute-done | bytes 81952 | tf_op jit(solution)/shard_map/ppermute | solution.py:401
  36.9 2.5 %collective-permute-done.7 = f32[32,640]{1,0:T(8,128)S(1)} collective-permute-done((f32[32,640]{1,0:T(8,128)S(1)}, f32[32,640]{1,0:T(8,128)S(1)}, u32[]{:S(2)}, u32[]{:S(2)}) %collective-permute-start.7) | collective-permute-done | bytes 81952 | tf_op jit(solution)/shard_map/ppermute | solution.py:401
  39.5 3.8 %collective-permute-start.11 = (f32[32,640]{1,0:T(8,128)S(1)}, f32[32,640]{1,0:T(8,128)S(1)}, u32[]{:S(2)}, u32[]{:S(2)}) collective-permute-start(f32[32,640]{1,0:T(8,128)S(1)} %add_add_fusion.3), channel_id=1, source_target_pairs={{0,96},{1,7},{2,98},{3,5},{4,100},{5,3},{6,102},{7,1},{8,104},{9,1... | collective-permute-start | bytes 245768 | tf_op jit(solution)/shard_map/ppermute | solution.py:401
  44.0 1.6 %collective-permute-done.11 = f32[32,640]{1,0:T(8,128)S(1)} collective-permute-done((f32[32,640]{1,0:T(8,128)S(1)}, f32[32,640]{1,0:T(8,128)S(1)}, u32[]{:S(2)}, u32[]{:S(2)}) %collective-permute-start.11) | collective-permute-done | bytes 81952 | tf_op jit(solution)/shard_map/ppermute | solution.py:401
  45.5 2.5 %collective-permute-done.10 = f32[32,640]{1,0:T(8,128)S(1)} collective-permute-done((f32[32,640]{1,0:T(8,128)S(1)}, f32[32,640]{1,0:T(8,128)S(1)}, u32[]{:S(2)}, u32[]{:S(2)}) %collective-permute-start.10) | collective-permute-done | bytes 81952 | tf_op jit(solution)/shard_map/ppermute | solution.py:401
  48.1 4.5 %collective-permute-start.12 = (f32[32,640]{1,0:T(8,128)S(1)}, f32[32,640]{1,0:T(8,128)S(1)}, u32[]{:S(2)}, u32[]{:S(2)}) collective-permute-start(f32[32,640]{1,0:T(8,128)S(1)} %add_add_fusion.2.mine), channel_id=1, source_target_pairs={{0,1},{1,0},{2,3},{3,2},{4,5},{5,4},{6,7},{7,6},{8,9},{9,8},{10,11... | collective-permute-start | bytes 245768 | tf_op jit(solution)/shard_map/ppermute | solution.py:401
  53.5 8.2 %back.1 = (bf16[768,2048]{1,0:T(8,128)(2,1)S(1)}, bf16[400,256]{1,0:T(8,128)(2,1)S(1)}, f32[400,256]{1,0:T(8,128)S(1)}, f32[4,64,256]{2,1,0:T(8,128)S(1)}) custom-call(s32[1]{0:T(128)S(6)} %rem.18.core, f32[32,640]{1,0:T(8,128)S(1)} %add_add_fusion.2.mine, f32[32,640]{1,0:T(8,128)S(1)} %collective-permute-done.12.other, ...), custom_call_target="tpu_custom_call" | custom-call | tf_op jit(solution)/shard_map/back/pallas_call | solution.py:578
  66.7 3.6 %outputs.1 = (bf16[2048,256]{1,0:T(8,128)(2,1)}, bf16[2048,256]{1,0:T(8,128)(2,1)}) custom-call(bf16[2048,256]{1,0:T(8,128)(2,1)S(1)} %get-tuple-element.83.ptsb, bf16[2048,256]{1,0:T(8,128)(2,1)S(1)} %copy-done.1, bf16[768,2048]{1,0:T(8,128)(2,1)S(1)} %get-tuple-element.84.res, f32[1,256]{1,0:T(1,128)S(1)} %bitcast.8, ...), custom_call_target="tpu_custom_call" | custom-call | flops 805306368 | bytes 7340032 | tf_op jit(solution)/shard_map/outputs/pallas_call | solution.py:623
  72.5 2.3 %collective-permute-start.18 = (bf16[400,256]{1,0:T(8,128)(2,1)S(1)}, bf16[400,256]{1,0:T(8,128)(2,1)S(1)}, u32[]{:S(2)}, u32[]{:S(2)}) collective-permute-start(bf16[400,256]{1,0:T(8,128)(2,1)S(1)} %add_add_fusion.1), channel_id=1, source_target_pairs={{0,16},{1,65},{2,18},{3,67},{4,20},{5,69},{6,22},{7,71},{8,24},{9,... | collective-permute-start | bytes 614408 | tf_op jit(solution)/shard_map/ppermute | solution.py:401
  75.8 1.7 %attend_grads.1 = f32[3,32,32]{2,1,0:T(8,128)} custom-call(f32[4,64,256]{2,1,0:T(8,128)S(1)} %get-tuple-element.90.toks), custom_call_target="tpu_custom_call" | custom-call | tf_op jit(solution)/shard_map/attend_grads/pallas_call | solution.py:643
  79.0 1.7 %collective-permute-done.17 = bf16[400,256]{1,0:T(8,128)(2,1)S(1)} collective-permute-done((bf16[400,256]{1,0:T(8,128)(2,1)S(1)}, bf16[400,256]{1,0:T(8,128)(2,1)S(1)}, u32[]{:S(2)}, u32[]{:S(2)}) %collective-permute-start.17) | collective-permute-done | bytes 204832 | tf_op jit(solution)/shard_map/ppermute | solution.py:401
  81.3 1.8 %collective-permute-start.21 = (bf16[400,256]{1,0:T(8,128)(2,1)S(1)}, bf16[400,256]{1,0:T(8,128)(2,1)S(1)}, u32[]{:S(2)}, u32[]{:S(2)}) collective-permute-start(bf16[400,256]{1,0:T(8,128)(2,1)S(1)} %add_add_fusion), channel_id=1, source_target_pairs={{0,64},{1,5},{2,66},{3,7},{4,68},{5,1},{6,70},{7,3},{8,72},{9,13},... | collective-permute-start | bytes 614408 | tf_op jit(solution)/shard_map/ppermute | solution.py:401
  83.1 1.5 %collective-permute-start.22 = (bf16[400,256]{1,0:T(8,128)(2,1)S(1)}, bf16[400,256]{1,0:T(8,128)(2,1)S(1)}, u32[]{:S(2)}, u32[]{:S(2)}) collective-permute-start(bf16[400,256]{1,0:T(8,128)(2,1)S(1)} %add_add_fusion), channel_id=1, source_target_pairs={{0,96},{1,7},{2,98},{3,5},{4,100},{5,3},{6,102},{7,1},{8,104},{9,1... | collective-permute-start | bytes 614408 | tf_op jit(solution)/shard_map/ppermute | solution.py:401
  84.6 2.9 %collective-permute-done.21 = bf16[400,256]{1,0:T(8,128)(2,1)S(1)} collective-permute-done((bf16[400,256]{1,0:T(8,128)(2,1)S(1)}, bf16[400,256]{1,0:T(8,128)(2,1)S(1)}, u32[]{:S(2)}, u32[]{:S(2)}) %collective-permute-start.21) | collective-permute-done | bytes 204832 | tf_op jit(solution)/shard_map/ppermute | solution.py:401
  90.1 3.8 %collective-permute-start.23 = (bf16[400,256]{1,0:T(8,128)(2,1)S(1)}, bf16[400,256]{1,0:T(8,128)(2,1)S(1)}, u32[]{:S(2)}, u32[]{:S(2)}) collective-permute-start(bf16[400,256]{1,0:T(8,128)(2,1)S(1)} %add_convert_fusion.mine), channel_id=1, source_target_pairs={{0,1},{1,0},{2,3},{3,2},{4,5},{5,4},{6,7},{7,6},{8,9},{9,8},{10,11... | collective-permute-start | bytes 614408 | tf_op jit(solution)/shard_map/ppermute | solution.py:401
  (61 shorter events, 22.9 us)
Async XLA Ops:
  3.8 6.2 %collective-permute-start.1 = (bf16[1024,256]{1,0:T(8,128)(2,1)}, bf16[1024,256]{1,0:T(8,128)(2,1)S(1)}, u32[]{:S(2)}, u32[]{:S(2)}) collective-permute-start(bf16[1024,256]{1,0:T(8,128)(2,1)} %get-tuple-element.59), channel_id=1, source_target_pairs={{0,1},{1,0},{2,3},{3,2},{4,5},{5,4},{6,7},{7,6},{8,9},{9,8},{10,11... | collective-permute-start | bytes 1572872 | tf_op jit(solution)/shard_map/ppermute | solution.py:401
  5.3 10.7 %collective-permute-start = (bf16[1024,256]{1,0:T(8,128)(2,1)}, bf16[1024,256]{1,0:T(8,128)(2,1)S(1)}, u32[]{:S(2)}, u32[]{:S(2)}) collective-permute-start(bf16[1024,256]{1,0:T(8,128)(2,1)} %get-tuple-element.55), channel_id=1, source_target_pairs={{1,2},{3,4},{5,6},{7,8},{9,10},{11,12},{13,14},{15,16},{17,18},{19... | collective-permute-start | bytes 1572872 | tf_op jit(solution)/shard_map/ppermute | solution.py:426
  19.6 1.4 %collective-permute-start.2 = (f32[32,640]{1,0:T(8,128)S(1)}, f32[32,640]{1,0:T(8,128)S(1)}, u32[]{:S(2)}, u32[]{:S(2)}) collective-permute-start(f32[32,640]{1,0:T(8,128)S(1)} %get-tuple-element.72), channel_id=1, source_target_pairs={{0,1},{1,0},{2,3},{3,2},{4,5},{5,4},{6,7},{7,6},{8,9},{9,8},{10,11... | collective-permute-start | bytes 245768 | tf_op jit(solution)/shard_map/ppermute | solution.py:401
  21.0 7.9 %collective-permute-start.5 = (f32[32,640]{1,0:T(8,128)S(1)}, f32[32,640]{1,0:T(8,128)S(1)}, u32[]{:S(2)}, u32[]{:S(2)}) collective-permute-start(f32[32,640]{1,0:T(8,128)S(1)} %add.60), channel_id=1, source_target_pairs={{0,6},{1,25},{2,4},{3,27},{4,2},{5,29},{6,0},{7,31},{8,14},{9,17},... | collective-permute-start | bytes 245768 | tf_op jit(solution)/shard_map/ppermute | solution.py:401
  26.7 5.1 %collective-permute-start.4 = (f32[32,640]{1,0:T(8,128)S(1)}, f32[32,640]{1,0:T(8,128)S(1)}, u32[]{:S(2)}, u32[]{:S(2)}) collective-permute-start(f32[32,640]{1,0:T(8,128)S(1)} %add.60), channel_id=1, source_target_pairs={{0,4},{1,17},{2,6},{3,19},{4,0},{5,21},{6,2},{7,23},{8,12},{9,25},... | collective-permute-start | bytes 245768 | tf_op jit(solution)/shard_map/ppermute | solution.py:401
  26.7 5.1 %collective-permute-start.3 = (f32[32,640]{1,0:T(8,128)S(1)}, f32[32,640]{1,0:T(8,128)S(1)}, u32[]{:S(2)}, u32[]{:S(2)}) collective-permute-start(f32[32,640]{1,0:T(8,128)S(1)} %add.60), channel_id=1, source_target_pairs={{0,2},{1,9},{2,0},{3,11},{4,6},{5,13},{6,4},{7,15},{8,10},{9,1},{1... | collective-permute-start | bytes 245768 | tf_op jit(solution)/shard_map/ppermute | solution.py:401
  31.7 5.2 %collective-permute-start.8 = (f32[32,640]{1,0:T(8,128)S(1)}, f32[32,640]{1,0:T(8,128)S(1)}, u32[]{:S(2)}, u32[]{:S(2)}) collective-permute-start(f32[32,640]{1,0:T(8,128)S(1)} %add_add_fusion.4), channel_id=1, source_target_pairs={{0,24},{1,97},{2,26},{3,99},{4,28},{5,101},{6,30},{7,103},{8,16},{... | collective-permute-start | bytes 245768 | tf_op jit(solution)/shard_map/ppermute | solution.py:401
  34.7 4.8 %collective-permute-start.7 = (f32[32,640]{1,0:T(8,128)S(1)}, f32[32,640]{1,0:T(8,128)S(1)}, u32[]{:S(2)}, u32[]{:S(2)}) collective-permute-start(f32[32,640]{1,0:T(8,128)S(1)} %add_add_fusion.4), channel_id=1, source_target_pairs={{0,16},{1,65},{2,18},{3,67},{4,20},{5,69},{6,22},{7,71},{8,24},{9,... | collective-permute-start | bytes 245768 | tf_op jit(solution)/shard_map/ppermute | solution.py:401
  34.9 4.6 %collective-permute-start.6 = (f32[32,640]{1,0:T(8,128)S(1)}, f32[32,640]{1,0:T(8,128)S(1)}, u32[]{:S(2)}, u32[]{:S(2)}) collective-permute-start(f32[32,640]{1,0:T(8,128)S(1)} %add_add_fusion.4), channel_id=1, source_target_pairs={{0,8},{1,33},{2,10},{3,35},{4,12},{5,37},{6,14},{7,39},{8,0},{9,41... | collective-permute-start | bytes 245768 | tf_op jit(solution)/shard_map/ppermute | solution.py:401
  39.5 6.0 %collective-permute-start.11 = (f32[32,640]{1,0:T(8,128)S(1)}, f32[32,640]{1,0:T(8,128)S(1)}, u32[]{:S(2)}, u32[]{:S(2)}) collective-permute-start(f32[32,640]{1,0:T(8,128)S(1)} %add_add_fusion.3), channel_id=1, source_target_pairs={{0,96},{1,7},{2,98},{3,5},{4,100},{5,3},{6,102},{7,1},{8,104},{9,1... | collective-permute-start | bytes 245768 | tf_op jit(solution)/shard_map/ppermute | solution.py:401
  43.3 4.8 %collective-permute-start.10 = (f32[32,640]{1,0:T(8,128)S(1)}, f32[32,640]{1,0:T(8,128)S(1)}, u32[]{:S(2)}, u32[]{:S(2)}) collective-permute-start(f32[32,640]{1,0:T(8,128)S(1)} %add_add_fusion.3), channel_id=1, source_target_pairs={{0,64},{1,5},{2,66},{3,7},{4,68},{5,1},{6,70},{7,3},{8,72},{9,13},... | collective-permute-start | bytes 245768 | tf_op jit(solution)/shard_map/ppermute | solution.py:401
  43.3 4.8 %collective-permute-start.9 = (f32[32,640]{1,0:T(8,128)S(1)}, f32[32,640]{1,0:T(8,128)S(1)}, u32[]{:S(2)}, u32[]{:S(2)}) collective-permute-start(f32[32,640]{1,0:T(8,128)S(1)} %add_add_fusion.3), channel_id=1, source_target_pairs={{0,32},{1,3},{2,34},{3,1},{4,36},{5,7},{6,38},{7,5},{8,40},{9,11},... | collective-permute-start | bytes 245768 | tf_op jit(solution)/shard_map/ppermute | solution.py:401
  48.1 5.4 %collective-permute-start.12 = (f32[32,640]{1,0:T(8,128)S(1)}, f32[32,640]{1,0:T(8,128)S(1)}, u32[]{:S(2)}, u32[]{:S(2)}) collective-permute-start(f32[32,640]{1,0:T(8,128)S(1)} %add_add_fusion.2.mine), channel_id=1, source_target_pairs={{0,1},{1,0},{2,3},{3,2},{4,5},{5,4},{6,7},{7,6},{8,9},{9,8},{10,11... | collective-permute-start | bytes 245768 | tf_op jit(solution)/shard_map/ppermute | solution.py:401
  61.8 1.5 %collective-permute-start.13 = (bf16[400,256]{1,0:T(8,128)(2,1)S(1)}, bf16[400,256]{1,0:T(8,128)(2,1)S(1)}, u32[]{:S(2)}, u32[]{:S(2)}) collective-permute-start(bf16[400,256]{1,0:T(8,128)(2,1)S(1)} %get-tuple-element.82), channel_id=1, source_target_pairs={{0,1},{1,0},{2,3},{3,2},{4,5},{5,4},{6,7},{7,6},{8,9},{9,8},{10,11... | collective-permute-start | bytes 614408 | tf_op jit(solution)/shard_map/ppermute | solution.py:401
  63.4 8.4 %collective-permute-start.16 = (bf16[400,256]{1,0:T(8,128)(2,1)S(1)}, bf16[400,256]{1,0:T(8,128)(2,1)S(1)}, u32[]{:S(2)}, u32[]{:S(2)}) collective-permute-start(bf16[400,256]{1,0:T(8,128)(2,1)S(1)} %add_convert_fusion.1), channel_id=1, source_target_pairs={{0,6},{1,25},{2,4},{3,27},{4,2},{5,29},{6,0},{7,31},{8,14},{9,17},... | collective-permute-start | bytes 614408 | tf_op jit(solution)/shard_map/ppermute | solution.py:401
  64.6 7.1 %collective-permute-start.15 = (bf16[400,256]{1,0:T(8,128)(2,1)S(1)}, bf16[400,256]{1,0:T(8,128)(2,1)S(1)}, u32[]{:S(2)}, u32[]{:S(2)}) collective-permute-start(bf16[400,256]{1,0:T(8,128)(2,1)S(1)} %add_convert_fusion.1), channel_id=1, source_target_pairs={{0,4},{1,17},{2,6},{3,19},{4,0},{5,21},{6,2},{7,23},{8,12},{9,25},... | collective-permute-start | bytes 614408 | tf_op jit(solution)/shard_map/ppermute | solution.py:401
  65.3 7.1 %collective-permute-start.14 = (bf16[400,256]{1,0:T(8,128)(2,1)S(1)}, bf16[400,256]{1,0:T(8,128)(2,1)S(1)}, u32[]{:S(2)}, u32[]{:S(2)}) collective-permute-start(bf16[400,256]{1,0:T(8,128)(2,1)S(1)} %add_convert_fusion.1), channel_id=1, source_target_pairs={{0,2},{1,9},{2,0},{3,11},{4,6},{5,13},{6,4},{7,15},{8,10},{9,1},{1... | collective-permute-start | bytes 614408 | tf_op jit(solution)/shard_map/ppermute | solution.py:401
  72.5 6.5 %collective-permute-start.18 = (bf16[400,256]{1,0:T(8,128)(2,1)S(1)}, bf16[400,256]{1,0:T(8,128)(2,1)S(1)}, u32[]{:S(2)}, u32[]{:S(2)}) collective-permute-start(bf16[400,256]{1,0:T(8,128)(2,1)S(1)} %add_add_fusion.1), channel_id=1, source_target_pairs={{0,16},{1,65},{2,18},{3,67},{4,20},{5,69},{6,22},{7,71},{8,24},{9,... | collective-permute-start | bytes 614408 | tf_op jit(solution)/shard_map/ppermute | solution.py:401
  74.8 5.9 %collective-permute-start.17 = (bf16[400,256]{1,0:T(8,128)(2,1)S(1)}, bf16[400,256]{1,0:T(8,128)(2,1)S(1)}, u32[]{:S(2)}, u32[]{:S(2)}) collective-permute-start(bf16[400,256]{1,0:T(8,128)(2,1)S(1)} %add_add_fusion.1), channel_id=1, source_target_pairs={{0,8},{1,33},{2,10},{3,35},{4,12},{5,37},{6,14},{7,39},{8,0},{9,41... | collective-permute-start | bytes 614408 | tf_op jit(solution)/shard_map/ppermute | solution.py:401
  75.1 6.1 %collective-permute-start.19 = (bf16[400,256]{1,0:T(8,128)(2,1)S(1)}, bf16[400,256]{1,0:T(8,128)(2,1)S(1)}, u32[]{:S(2)}, u32[]{:S(2)}) collective-permute-start(bf16[400,256]{1,0:T(8,128)(2,1)S(1)} %add_add_fusion.1), channel_id=1, source_target_pairs={{0,24},{1,97},{2,26},{3,99},{4,28},{5,101},{6,30},{7,103},{8,16},{... | collective-permute-start | bytes 614408 | tf_op jit(solution)/shard_map/ppermute | solution.py:401
  81.3 6.3 %collective-permute-start.21 = (bf16[400,256]{1,0:T(8,128)(2,1)S(1)}, bf16[400,256]{1,0:T(8,128)(2,1)S(1)}, u32[]{:S(2)}, u32[]{:S(2)}) collective-permute-start(bf16[400,256]{1,0:T(8,128)(2,1)S(1)} %add_add_fusion), channel_id=1, source_target_pairs={{0,64},{1,5},{2,66},{3,7},{4,68},{5,1},{6,70},{7,3},{8,72},{9,13},... | collective-permute-start | bytes 614408 | tf_op jit(solution)/shard_map/ppermute | solution.py:401
  83.1 5.6 %collective-permute-start.20 = (bf16[400,256]{1,0:T(8,128)(2,1)S(1)}, bf16[400,256]{1,0:T(8,128)(2,1)S(1)}, u32[]{:S(2)}, u32[]{:S(2)}) collective-permute-start(bf16[400,256]{1,0:T(8,128)(2,1)S(1)} %add_add_fusion), channel_id=1, source_target_pairs={{0,32},{1,3},{2,34},{3,1},{4,36},{5,7},{6,38},{7,5},{8,40},{9,11},... | collective-permute-start | bytes 614408 | tf_op jit(solution)/shard_map/ppermute | solution.py:401
  83.1 6.8 %collective-permute-start.22 = (bf16[400,256]{1,0:T(8,128)(2,1)S(1)}, bf16[400,256]{1,0:T(8,128)(2,1)S(1)}, u32[]{:S(2)}, u32[]{:S(2)}) collective-permute-start(bf16[400,256]{1,0:T(8,128)(2,1)S(1)} %add_add_fusion), channel_id=1, source_target_pairs={{0,96},{1,7},{2,98},{3,5},{4,100},{5,3},{6,102},{7,1},{8,104},{9,1... | collective-permute-start | bytes 614408 | tf_op jit(solution)/shard_map/ppermute | solution.py:401
  90.1 4.9 %collective-permute-start.23 = (bf16[400,256]{1,0:T(8,128)(2,1)S(1)}, bf16[400,256]{1,0:T(8,128)(2,1)S(1)}, u32[]{:S(2)}, u32[]{:S(2)}) collective-permute-start(bf16[400,256]{1,0:T(8,128)(2,1)S(1)} %add_convert_fusion.mine), channel_id=1, source_target_pairs={{0,1},{1,0},{2,3},{3,2},{4,5},{5,4},{6,7},{7,6},{8,9},{9,8},{10,11... | collective-permute-start | bytes 614408 | tf_op jit(solution)/shard_map/ppermute | solution.py:401
  (10 other events, 66.4 us)
